TPU v7x, 512 devices: a whole 4x8x8 slice. The times are simulated.
512 devices in a mesh: tile: 128 (over y, z, core), rep: 4 (over x).
Axes of the slice: x: 4, y: 8, z: 8, core: 2. Of those that a mesh axis runs over, the one named last changes fastest.
Arguments:
- inputs: bfloat16 [4, 6, 1024, 16, 256], P('rep', None, 'tile'), may hold values from -6 to 6
- cotangent: bfloat16 [4, 2, 2048, 32, 128], P('rep', None, 'tile'), may hold values from -6 to 6
- first_weight: bfloat16 [3, 3, 3, 256, 128], replicated, may hold values from -0.078125 to 0.078125
- second_weight: bfloat16 [3, 3, 3, 128, 128], replicated, may hold values from -0.109375 to 0.109375
- tile_clip: int32 [4, 128], P('rep'), may hold values from 0 to 7, never falling along the last dimension, each value on 1 to 32 neighbouring positions
- clip_cols: int32 [4, 8], P('rep'), may hold values from 10 to 16, as said below
- clip_start: int32 [4, 8], P('rep'), may hold values from 0 to 2
Outputs:
- input_grad: bfloat16 [4, 6, 1024, 16, 256], P('rep', None, 'tile')
- grad_first: float32 [3, 3, 3, 256, 128], P(None, None, None, None, 'rep')
- grad_second: float32 [3, 3, 3, 128, 128], P(None, None, None, None, 'rep')
Inputs may be any that keep to these rules, and one draw needn't show every extreme that they name: `tile_clip`: clip numbers never fall along the tiles of a group; each clip 0 to 7 has 1 to 32 consecutive tiles, and one has exactly 32. `clip_cols`: each clip has 16 columns (1080p) or 2 * 16 // 3 (720p); both kinds occur in every group.
All inputs are finite; a program needn't handle non-finite values.
Results may differ from a plain program's by a relative error of at most 0.018.
Values may be sent and summed in bfloat16 or wider, within the bound.
No kernel may reach another device: no remote copies, remote signals or barrier semaphores. Data moves between devices by JAX's collectives and lax.ppermute only.
A program may use at most 64 MiB of HBM per device.

v0:
```python
import math

import jax
import jax.numpy as jnp
from jax import lax
from jax.sharding import PartitionSpec as P


def padded_2(cells, sides, width):
    for axis, dim in sides:
        count = lax.axis_size(axis)
        ends = count - 1
        head = lax.slice_in_dim(cells, 0, width, axis=dim)
        tail = lax.slice_in_dim(cells, cells.shape[dim] - width, cells.shape[dim], axis=dim)
        cells = jnp.concatenate(
            [
                lax.ppermute(tail, axis, [(i, (i + 1) % count) for i in range(ends)]),
                cells,
                lax.ppermute(head, axis, [((i + 1) % count, i) for i in range(ends)]),
            ],
            axis=dim,
        )
    return cells


def silu_slope(values):
    sigmoid_of = jax.nn.sigmoid(values)
    return sigmoid_of * (1.0 + values * (1.0 - sigmoid_of))


def row_flags(row_first, row_count, row_limit, up_same, down_same):
    offsets = row_first + jnp.arange(row_count)
    return jnp.where(offsets < 0, up_same, jnp.where(offsets >= row_limit, down_same, True)).astype(
        jnp.float32
    )


def conv_rows(values, kernel):
    return lax.conv_general_dilated(
        values[None],
        kernel,
        (1, 1, 1),
        ((0, 0), (0, 0), (1, 1)),
        dimension_numbers=("NDHWC", "DHWIO", "NDHWC"),
        preferred_element_type=jnp.float32,
    )[0]


def flipped(kernel):
    return jnp.transpose(kernel[::-1, ::-1, ::-1], (0, 1, 2, 4, 3))


def frame_pad(values, before, after, extra_rows):
    return jnp.pad(values, ((before, after), (extra_rows, extra_rows), (0, 0), (0, 0)))


def upsample(values):
    return jnp.repeat(jnp.repeat(values, 2, axis=1), 2, axis=2)


def down_sum(values):
    shape_now = values.shape
    return values.reshape(
        shape_now[0], shape_now[1] // 2, 2, shape_now[2] // 2, 2, shape_now[3]
    ).sum(axis=(2, 4))


def weight_grad(values, cot_values):
    padded = jnp.pad(values, ((0, 0), (0, 0), (1, 1), (0, 0)))
    frames_out, rows_out, width_out = (
        cot_values.shape[0],
        cot_values.shape[1],
        cot_values.shape[2],
    )
    tap_terms = []
    for depth_tap in range(3):
        for height in range(3):
            for across in range(3):
                window = padded[
                    depth_tap : depth_tap + frames_out,
                    height : height + rows_out,
                    across : across + width_out,
                ]
                tap_terms.append(
                    jnp.einsum(
                        "fhwi,fhwo->io", window, cot_values, preferred_element_type=jnp.float32
                    )
                )
    return jnp.stack(tap_terms).reshape(3, 3, 3, values.shape[3], cot_values.shape[3])


def eff_inputs(extended, from_start):
    first_frame = extended[4]
    head_frames = jnp.where(
        from_start, jnp.broadcast_to(first_frame, extended[:4].shape), extended[:4]
    )
    return jnp.concatenate([head_frames, extended[4:]], 0)


def finish_grad(act_grad, core_float, col_low, from_start):
    pre_input = act_grad * silu_slope(core_float) * col_low[None, None, :, None]
    carried = jnp.sum(pre_input[:4], axis=0)
    moved_grad = jnp.concatenate(
        [jnp.zeros_like(pre_input[:4]), (pre_input[4] + carried)[None], pre_input[5:]], 0
    )
    return jnp.where(from_start, moved_grad, pre_input).astype(jnp.bfloat16)


def deep_tile(
    local_in,
    local_cot,
    first_weight,
    second_weight,
    up_same,
    down_same,
    col_low,
    col_high,
    from_start,
):
    tile_rows = local_in.shape[1]
    ext_in = padded_2(local_in, (("tile", 1),), 2)
    ext_cot = padded_2(local_cot, (("tile", 1),), 3)
    eff = eff_inputs(ext_in, from_start).astype(jnp.float32)
    mask_act = (
        row_flags(-2, tile_rows + 4, tile_rows, up_same, down_same)[:, None] * col_low[None, :]
    )
    activated = (jax.nn.silu(eff) * mask_act[None, :, :, None]).astype(jnp.bfloat16)
    first_out = conv_rows(activated, first_weight)
    upsampled = upsample(first_out)
    mask_second = (
        row_flags(-2, 2 * tile_rows + 4, 2 * tile_rows, up_same, down_same)[:, None]
        * col_high[None, :]
    )
    second_in = (jax.nn.silu(upsampled) * mask_second[None, :, :, None]).astype(jnp.bfloat16)
    mask_cot = (
        row_flags(-3, 2 * tile_rows + 6, 2 * tile_rows, up_same, down_same)[:, None]
        * col_high[None, :]
    )
    cot_masked = (ext_cot.astype(jnp.float32) * mask_cot[None, :, :, None]).astype(jnp.bfloat16)
    second_grad = conv_rows(frame_pad(cot_masked, 2, 2, 0), flipped(second_weight))
    pre_grad = second_grad * silu_slope(upsampled) * mask_second[None, :, :, None]
    first_grad = down_sum(pre_grad).astype(jnp.bfloat16)
    grad_second = weight_grad(
        second_in[:, 1 : 2 * tile_rows + 3], cot_masked[:, 3 : 3 + 2 * tile_rows]
    )
    grad_first = weight_grad(activated[:, 1 : tile_rows + 3], first_grad[:, 1 : tile_rows + 1])
    act_grad = conv_rows(frame_pad(first_grad, 2, 2, 0), flipped(first_weight))
    input_grad = finish_grad(act_grad, eff[:, 2 : tile_rows + 2], col_low, from_start)
    return (input_grad, grad_first, grad_second)


def body(inputs, cotangent, first_weight, second_weight, tile_clip, clip_cols, clip_start):
    tile_index = lax.axis_index("tile")
    tile_count = lax.axis_size("tile")
    tile_order = jnp.arange(tile_count)
    clip_row = tile_clip[0]
    own_clip = jnp.sum(jnp.where(tile_order == tile_index, clip_row, 0))
    clip_above = jnp.sum(jnp.where(tile_order == tile_index - 1, clip_row, 0))
    clip_below = jnp.sum(jnp.where(tile_order == tile_index + 1, clip_row, 0))
    up_same = (tile_index > 0) & (clip_above == own_clip)
    down_same = (tile_index + 1 < tile_count) & (clip_below == own_clip)
    clip_order = jnp.arange(clip_cols.shape[1])
    columns = jnp.sum(jnp.where(clip_order == own_clip, clip_cols[0], 0))
    from_start = jnp.sum(jnp.where(clip_order == own_clip, clip_start[0], 0)) == 0
    tile_width = inputs.shape[3]
    col_low = (jnp.arange(tile_width) < columns).astype(jnp.float32)
    col_high = (jnp.arange(2 * tile_width) < 2 * columns).astype(jnp.float32)
    input_grad, grad_first, grad_second = deep_tile(
        inputs[0],
        cotangent[0],
        first_weight,
        second_weight,
        up_same,
        down_same,
        col_low,
        col_high,
        from_start,
    )
    quarter_first, quarter_second = (
        lax.psum_scatter(
            grad_first.astype(jnp.bfloat16), "rep", scatter_dimension=4, tiled=True
        ).astype(jnp.float32),
        lax.psum_scatter(
            grad_second.astype(jnp.bfloat16), "rep", scatter_dimension=4, tiled=True
        ).astype(jnp.float32),
    )
    whole_first, whole_second = lax.psum((quarter_first, quarter_second), "tile")
    cell_total = (
        tile_count
        * lax.axis_size("rep")
        * cotangent.shape[1]
        * cotangent.shape[2]
        * cotangent.shape[3]
    )
    grad_scale = 1.0 / math.sqrt(cell_total)
    return (input_grad[None], whole_first * grad_scale, whole_second * grad_scale)


def solution(mesh):
    in_specs = (
        P("rep", None, "tile", None, None),
        P("rep", None, "tile", None, None),
        P(),
        P(),
        P("rep", None),
        P("rep", None),
        P("rep", None),
    )
    out_specs = (
        P("rep", None, "tile", None, None),
        P(None, None, None, None, "rep"),
        P(None, None, None, None, "rep"),
    )
    return jax.shard_map(body, mesh=mesh, in_specs=in_specs, out_specs=out_specs, check_vma=False)
```

profile of v0, /device:TPU:1, one launch (start us, length us, event | category | flops | bytes accessed | tf_op | source)
XLA Modules:
  0.0 650.9 jit_solution(3436244910881609579)
XLA Ops:
  7.2 1.1 fusion.314
  8.3 5.4 collective-permute-start.2
  13.7 4.7 collective-permute-start.3
  19.2 1.9 collective-permute-start
  21.2 2.4 collective-permute-start.1
  23.6 1.3 fusion.216
  27.6 2.0 fusion.213
  32.5 1.1 multiply_convert_fusion.2
  36.4 6.4 fusion.17
  42.8 1.1 copy.30
  46.8 1.4 pad.22
  48.2 3.1 reshape.236
  51.3 1.5 copy.32
  53.0 3.6 fusion.20
  56.8 1.0 add_multiply_fusion
  68.4 2.3 copy.42
  70.8 2.1 multiply_reduce_fusion
  80.5 0.9 fusion.98
  81.4 0.9 fusion.96
  97.6 3.9 copy.40
  101.9 2.4 convolution_select_fusion
  106.7 32.0 %reduce-scatter.3.cloned.1.call-done = bf16[3,3,3,256,32]{3,4,2,1,0:T(8,128)(2,1)} async-done(((bf16[3,3,3,256,128]{3,4,2,1,0:T(8,128)(2,1)}), bf16[3,3,3,256,32]{3,4,2,1,0:T(8,128)(2,1)}) %reduce-scatter.3.cloned.1.call-update) | async-done | bytes 442384 | tf_op jit(solution)/shard_map/reduce_scatter | solution.py:180
  138.7 503.6 %all-reduce.6 = (f32[3,3,3,256,32]{3,4,2,1,0:T(8,128)S(1)}, f32[3,3,3,128,32]{3,4,2,1,0:T(8,128)S(1)}) all-reduce(bf16[3,3,3,256,32]{3,4,2,1,0:T(8,128)(2,1)} %reduce-scatter.3.cloned.1.call-done, bf16[3,3,3,128,32]{3,4,2,1,0:T(8,128)(2,1)} %reduce-scatter.5.cloned.1.call-done), channel_id=1, replica_groups=mesh['tile'=128,'rep'=4] {'tile'}, use_global_device_ids=true, to_apply=%region_8.9 | all-reduce | flops 331776 | bytes 1990656 | tf_op jit(solution)/shard_map/psum | solution.py:187
  642.3 1.0 broadcast_multiply_fusion
  (141 shorter events, 45.4 us)
Async XLA Ops:
  7.2 45.8 %copy-start = (bf16[3,3,3,256,128]{4,3,2,1,0:T(8,128)(2,1)S(1)}, bf16[3,3,3,256,128]{4,3,2,1,0:T(8,128)(2,1)}, u32[]{:S(2)}) copy-start(bf16[3,3,3,256,128]{4,3,2,1,0:T(8,128)(2,1)} %param.9) | copy-start | bytes 5308420
  7.2 99.5 %reduce-scatter.5.cloned.1.call-start = ((), (), s32[]{:S(2)}) async-start(), calls=%async_computation.3 | async-start | bytes 1105920 | tf_op jit(solution)/shard_map/reduce_scatter | solution.py:183
  8.3 35.7 %collective-permute-start.2 = (bf16[6,2,16,256]{3,2,1,0:T(8,128)(2,1)S(1)}, bf16[6,2,16,256]{3,2,1,0:T(8,128)(2,1)S(1)}, u32[]{:S(2)}, u32[]{:S(2)}) collective-permute-start(bf16[6,2,16,256]{3,2,1,0:T(8,128)(2,1)S(1)} %get-tuple-element.10), channel_id=1, source_target_pairs={{0,4},{4,8},{8,12},{12,16},{16,20},{20,24},{24,28},{28,32},{32,36}... | collective-permute-start | bytes 294920 | tf_op jit(solution)/shard_map/ppermute | solution.py:17
  13.7 30.3 %collective-permute-start.3 = (bf16[6,2,16,256]{3,2,1,0:T(8,128)(2,1)S(1)}, bf16[6,2,16,256]{3,2,1,0:T(8,128)(2,1)S(1)}, u32[]{:S(2)}, u32[]{:S(2)}) collective-permute-start(bf16[6,2,16,256]{3,2,1,0:T(8,128)(2,1)S(1)} %get-tuple-element.11), channel_id=1, source_target_pairs={{4,0},{8,4},{12,8},{16,12},{20,16},{24,20},{28,24},{32,28},{36,32}... | collective-permute-start | bytes 294920 | tf_op jit(solution)/shard_map/ppermute | solution.py:19
  19.2 13.2 %collective-permute-start = (bf16[2,3,32,128]{3,2,1,0:T(8,128)(2,1)S(1)}, bf16[2,3,32,128]{3,2,1,0:T(8,128)(2,1)S(1)}, u32[]{:S(2)}, u32[]{:S(2)}) collective-permute-start(bf16[2,3,32,128]{3,2,1,0:T(8,128)(2,1)S(1)} %get-tuple-element.12), channel_id=1, source_target_pairs={{0,4},{4,8},{8,12},{12,16},{16,20},{20,24},{24,28},{28,32},{32,36}... | collective-permute-start | bytes 147464 | tf_op jit(solution)/shard_map/ppermute | solution.py:17
  21.2 11.3 %collective-permute-start.1 = (bf16[2,3,32,128]{3,2,1,0:T(8,128)(2,1)S(1)}, bf16[2,3,32,128]{3,2,1,0:T(8,128)(2,1)S(1)}, u32[]{:S(2)}, u32[]{:S(2)}) collective-permute-start(bf16[2,3,32,128]{3,2,1,0:T(8,128)(2,1)S(1)} %get-tuple-element.13), channel_id=1, source_target_pairs={{4,0},{8,4},{12,8},{16,12},{20,16},{24,20},{28,24},{32,28},{36,32}... | collective-permute-start | bytes 147464 | tf_op jit(solution)/shard_map/ppermute | solution.py:19
  33.6 0.7 copy-start.7
  35.2 1.2 copy-start.12
  35.2 1.2 copy-start.13
  43.9 1.0 copy-start.1
  44.9 0.9 copy-start.2
  45.0 3.2 copy-start.10
  45.8 0.7 copy-start.4
  51.3 1.6 copy-start.14
  56.6 1.2 copy-start.3
  56.6 1.2 copy-start.11
  58.6 1.0 copy-start.8
  67.5 0.9 copy-start.9
  70.7 68.0 %reduce-scatter.3.cloned.1.call-start = ((), (), s32[]{:S(2)}) async-start(), calls=%async_computation.2 | async-start | bytes 2211840 | tf_op jit(solution)/shard_map/reduce_scatter | solution.py:180
  70.7 2.2 copy-start.5
  104.3 0.9 copy-start.6
Sparse Core Ops, SparseCore 0:
  70.8 31.5 reduce-scatter.4
  105.2 33.3 reduce-scatter.2
where the time goes:
time: 655 us; the launch traced here: 651 us
  blocking collectives  504 us (77%)
  matrix products  44.3 us (7%)
  waiting for transfers between devices  32 us (5%)
  local copies, waits for them, and re-layouts  24.2 us (4%)
  between operations  18.7 us (3%)
  starting transfers between devices  14.5 us (2%)
  other arithmetic  13.6 us (2%)
    psum x1, blocking collectives, body(): lax.psum((quarter_first, quarter_second), 'tile')  504 us
    dot_general x54, matrix products, weight_grad(): jnp.einsum('fhwi,fhwo->io', window, cot_values, preferred_element_type=jn...  32 us
    reduce_scatter x1, waiting for transfers between devices, body(): lax.psum_scatter(grad_first.astype(jnp.bfloat16), 'rep', scatter_dimensio...  32 us
  transfers between devices with their start and end apart: 6, of which 1 were waited for; matrix products, arithmetic and copies ran while one was open for 8% of the time, Pallas kernels for 0%

commit v1 on v0

v1 whole, which is shorter than its diff:
```python
import math

import jax
import jax.numpy as jnp
from jax import lax
from jax.experimental import pallas as pl
from jax.experimental.pallas import tpu as pltpu
from jax.sharding import Mesh
from jax.sharding import PartitionSpec as P

TILE_AXES = ("y", "z", "core")
PLANE_AXES = ("y", "z")
BF = jnp.bfloat16
F32 = jnp.float32
NT = (((1,), (1,)), ((), ()))
TN = (((0,), (0,)), ((), ()))
LAST = 128
IN_BLOCKS = 24
HALO_BLOCKS = 36


def dot(lhs, rhs, dims=(((1,), (0,)), ((), ()))):
    return lax.dot_general(lhs, rhs, dims, preferred_element_type=F32)


def pack_kernel(in_ref, cot_ref, to_next, to_previous):
    for out, row_in, row_cot in ((to_next, 6, 13), (to_previous, 0, 0)):
        for frame in range(6):
            for row in range(2):
                for half in range(2):
                    out[frame * 4 + row * 2 + half] = in_ref[
                        frame, row_in + row, :, half * LAST : (half + 1) * LAST
                    ]
        for frame in range(2):
            for row in range(3):
                for half in range(2):
                    out[IN_BLOCKS + frame * 6 + row * 2 + half] = cot_ref[
                        frame, row_cot + row, half * 16 : (half + 1) * 16, :
                    ]


def sigmoid(values):
    return 1.0 / (1.0 + jnp.exp(-values))


def column_shifts(values, column):
    left = jnp.where(column == 0, 0.0, pltpu.roll(values, 1, 1))
    right = jnp.where(column == 15, 0.0, pltpu.roll(values, 15, 1))
    return left, right


def main_kernel(
    clip_ref,
    cols_ref,
    start_ref,
    in_ref,
    cot_ref,
    above_ref,
    below_ref,
    w1_ref,
    w2_ref,
    grad_ref,
    part_ref,
    act,
    pair,
    cots,
    seconds,
    firsts,
):
    tile = lax.axis_index(TILE_AXES)
    tiles = lax.axis_size(TILE_AXES)
    own = clip_ref[0, tile]
    up_same = (tile > 0) & (clip_ref[0, jnp.maximum(tile - 1, 0)] == own)
    down_same = (tile + 1 < tiles) & (clip_ref[0, jnp.minimum(tile + 1, tiles - 1)] == own)
    up_scale = jnp.where(up_same, 1.0, 0.0)
    down_scale = jnp.where(down_same, 1.0, 0.0)
    columns = cols_ref[0, own]
    from_start = start_ref[0, own] == 0

    col_256 = lax.broadcasted_iota(jnp.int32, (1, 16, 256), 1)
    low_256 = jnp.where(col_256 < columns, 1.0, 0.0)

    def activated(values, scale):
        wide = values.astype(F32)
        return wide * sigmoid(wide) * (low_256 * scale)

    def frame_of(frame):
        return jnp.where(from_start, 4, frame) if frame < 4 else frame

    for frame in range(6):
        source = frame_of(frame)

        def halo(ref):
            blocks = ref[pl.ds(source * 4, 4)]
            return jnp.concatenate(
                [
                    jnp.concatenate([blocks[0:1], blocks[1:2]], 2),
                    jnp.concatenate([blocks[2:3], blocks[3:4]], 2),
                ],
                0,
            )

        for first, count, raw, scale in (
            (0, 2, halo(above_ref), up_scale),
            (2, 8, in_ref[source], 1.0),
            (10, 2, halo(below_ref), down_scale),
        ):
            values = activated(raw, scale)
            left, right = column_shifts(values, col_256)
            act[0, frame, first : first + count] = left.astype(BF)
            act[1, frame, first : first + count] = values.astype(BF)
            act[2, frame, first : first + count] = right.astype(BF)

    first_out = None
    for step in range(9):
        kt, kh = step // 3, step % 3
        window = jnp.concatenate(
            [act[kw, kt : kt + 4, kh : kh + 10].reshape(640, 256) for kw in range(3)], 1
        )
        term = dot(window, w1_ref[step * 3 : step * 3 + 3].reshape(768, LAST))
        first_out = term if first_out is None else first_out + term
    first_out = first_out.reshape(40, 16, LAST)
    column = lax.broadcasted_iota(jnp.int32, (1, 16, LAST), 1)
    low = jnp.where(column < columns, 1.0, 0.0)
    row = lax.broadcasted_iota(jnp.int32, (40, 1, 1), 0) % 10
    row_scale = jnp.where(row == 0, up_scale, jnp.where(row == 9, down_scale, 1.0))
    gate = sigmoid(first_out)
    second_in = (first_out * gate * low).astype(BF).reshape(4, 10, 16, LAST)
    seconds[...] = second_in[:, 1:9]
    slope = gate * (1.0 + first_out * (1.0 - gate)) * (low * row_scale)

    wide_column = lax.broadcasted_iota(jnp.int32, (1, 32, LAST), 1)
    high = jnp.where(wide_column < 2 * columns, 1.0, 0.0)
    pair[:, :, 0:8] = jnp.zeros((2, 21, 8, LAST), F32)
    pair[:, :, 40:48] = jnp.zeros((2, 21, 8, LAST), F32)
    for frame in range(2):
        rows = []
        for ref, scale in ((above_ref, up_scale), (None, 1.0), (below_ref, down_scale)):
            if ref is None:
                rows += [cot_ref[frame, r : r + 1].astype(F32) * high for r in range(16)]
                continue
            for r in range(3):
                at = IN_BLOCKS + frame * 6 + r * 2
                block = ref[at : at + 2].reshape(1, 32, LAST)
                rows.append(block.astype(F32) * (high * scale))
        for i in range(-2, 9):
            pair[frame, i + 2 : i + 3, 8:40] = rows[2 * i + 4] + rows[2 * i + 5]
        for i in range(-1, 9):
            pair[frame, i + 12 : i + 13, 8:40] = rows[2 * i + 3] + rows[2 * i + 4]
        for slot in range(21):
            before, even, odd, after = (
                pair[frame, slot, pl.ds(begin, 16, 2), :] for begin in (7, 8, 9, 10)
            )
            for kw, value in ((0, odd + after), (1, even + odd), (2, before + even)):
                rounded = value.astype(BF)
                if slot >= 11:
                    targets = ((1, slot - 11),)
                else:
                    targets = ((0, slot - 1), (2, slot))
                for kh, place in targets:
                    if 0 <= place < 10:
                        tap = kh * 3 + kw
                        cots[frame, place, :, tap * LAST : (tap + 1) * LAST] = rounded

    flat = jnp.concatenate(
        [
            jnp.concatenate([w2_ref[kt * 9 + tap] for tap in range(9)], 1)
            for kt in range(3)
        ],
        0,
    )
    spread = dot(cots[...].reshape(320, 1152), flat, NT)
    for frame in range(4):
        total = None
        for kt in range(3):
            if 0 <= frame - kt < 2:
                term = spread[
                    (frame - kt) * 160 : (frame - kt + 1) * 160, kt * LAST : (kt + 1) * LAST
                ]
                total = term if total is None else total + term
        first_grad = total.reshape(10, 16, LAST) * slope[frame * 10 : frame * 10 + 10]
        before, after = column_shifts(first_grad, column)
        for kw, value in ((0, after), (1, first_grad), (2, before)):
            rounded = value.astype(BF)
            for kh in range(3):
                tap = kh * 3 + kw
                firsts[frame, :, :, tap * LAST : (tap + 1) * LAST] = rounded[2 - kh : 10 - kh]

    cores, reps = part_ref.shape[0], part_ref.shape[1]
    depth = LAST // cores // reps

    def put(block, tap, third):
        part = block.astype(BF).reshape(reps, cores, depth, LAST)
        for core in range(cores):
            part_ref[core, :, tap * 3 + third] = part[:, core]

    seconds_all = jnp.concatenate([seconds[kt : kt + 2].reshape(256, LAST) for kt in range(3)], 1)
    act_all = jnp.concatenate([act[1, kt : kt + 4, 2:10].reshape(512, 256) for kt in range(3)], 1)
    for tap in range(9):
        here = slice(tap * LAST, (tap + 1) * LAST)
        block = dot(cots[:, 1:9, :, here].reshape(256, LAST), seconds_all, TN)
        for kt in range(3):
            put(block[:, kt * LAST : (kt + 1) * LAST], kt * 9 + tap, 2)
        block = dot(firsts[:, :, :, here].reshape(512, LAST), act_all, TN)
        for kt in range(3):
            for half in range(2):
                at = kt * 256 + half * LAST
                put(block[:, at : at + LAST], kt * 9 + tap, half)

    shifted = firsts[...].reshape(512, 1152)
    by_depth = [
        dot(shifted, jnp.concatenate([w1_ref[kt * 9 + tap] for tap in range(9)], 1), NT)
        for kt in range(3)
    ]
    keep = jnp.where(from_start, 0.0, 1.0)
    carried = None
    for frame in range(6):
        total = None
        for kt in range(3):
            if 0 <= frame - kt < 4:
                term = by_depth[kt][(frame - kt) * 128 : (frame - kt + 1) * 128]
                total = term if total is None else total + term
        wide = in_ref[frame_of(frame)].astype(F32)
        gate = sigmoid(wide)
        pre = total.reshape(8, 16, 256) * (gate * (1.0 + wide * (1.0 - gate)) * low_256)
        if frame < 4:
            carried = pre if carried is None else carried + pre
            grad_ref[frame] = (pre * keep).astype(BF)
        elif frame == 4:
            grad_ref[frame] = (pre + carried * (1.0 - keep)).astype(BF)
        else:
            grad_ref[frame] = pre.astype(BF)


def finish_kernel(scale, whole_ref, first_ref, second_ref):
    cores, depth = whole_ref.shape[0], whole_ref.shape[2]
    for tap in range(27):
        for third in range(3):
            for core in range(cores):
                block = whole_ref[core, tap * 3 + third].astype(F32) * scale
                rows = slice(core * depth, (core + 1) * depth)
                if third == 2:
                    second_ref[tap, rows, :] = block
                else:
                    first_ref[tap, rows, third * LAST : (third + 1) * LAST] = block


VMEM = pl.BlockSpec(memory_space=pltpu.VMEM)
SMEM = pl.BlockSpec(memory_space=pltpu.SMEM)


def wide_sum(parts):
    return jnp.sum(parts.astype(F32), axis=0).astype(BF)


def body(inputs, cotangent, first_weight, second_weight, tile_clip, clip_cols, clip_start):
    tiles = lax.axis_size(TILE_AXES)
    cores, reps, plane = lax.axis_size("core"), lax.axis_size("x"), lax.axis_size(PLANE_AXES)
    local_in, local_cot = inputs[0], cotangent[0]
    halo_shape = jax.ShapeDtypeStruct((HALO_BLOCKS, 16, LAST), BF)
    to_next, to_previous = pl.pallas_call(
        pack_kernel,
        out_shape=(halo_shape, halo_shape),
        in_specs=[VMEM, VMEM],
        out_specs=(VMEM, VMEM),
        compiler_params=pltpu.CompilerParams(vmem_limit_bytes=8 << 20),
    )(local_in, local_cot)
    above = lax.ppermute(to_next, TILE_AXES, [(i, (i + 1) % tiles) for i in range(tiles)])
    below = lax.ppermute(to_previous, TILE_AXES, [((i + 1) % tiles, i) for i in range(tiles)])

    depth = LAST // cores // reps
    input_grad, parts = pl.pallas_call(
        main_kernel,
        out_shape=(
            jax.ShapeDtypeStruct(local_in.shape, BF),
            jax.ShapeDtypeStruct((cores, reps, 81, depth, LAST), BF),
        ),
        in_specs=[SMEM, SMEM, SMEM] + [VMEM] * 6,
        out_specs=(VMEM, VMEM),
        scratch_shapes=[
            pltpu.VMEM((3, 6, 12, 16, 256), BF),
            pltpu.VMEM((2, 21, 48, LAST), F32),
            pltpu.VMEM((2, 10, 16, 9 * LAST), BF),
            pltpu.VMEM((4, 8, 16, LAST), BF),
            pltpu.VMEM((4, 8, 16, 9 * LAST), BF),
        ],
        compiler_params=pltpu.CompilerParams(vmem_limit_bytes=48 << 20),
    )(
        tile_clip,
        clip_cols,
        clip_start,
        local_in,
        local_cot,
        above,
        below,
        first_weight.reshape(27, 256, LAST),
        second_weight.reshape(27, LAST, LAST),
    )

    rows = 81 * depth
    parts = parts.reshape(cores, reps, rows, LAST)
    of_core = wide_sum(lax.all_to_all(parts, "core", 0, 0, tiled=True))
    of_rep = wide_sum(lax.all_to_all(of_core, "x", 0, 0, tiled=True))
    share = -(-rows // plane // 8) * 8
    of_rep = jnp.pad(of_rep, ((0, share * plane - rows), (0, 0))).reshape(plane, share, LAST)
    own = wide_sum(lax.all_to_all(of_rep, PLANE_AXES, 0, 0, tiled=True))
    own = jnp.broadcast_to(own[None], (plane, share, LAST))
    half = lax.all_to_all(own, PLANE_AXES, 0, 0, tiled=True)
    half = half.reshape(plane * share, LAST)[:rows]
    whole = lax.all_gather(half, "core", axis=0).reshape(cores, 81, depth, LAST)

    cell_total = tiles * reps * cotangent.shape[1] * cotangent.shape[2] * cotangent.shape[3]
    scale = 1.0 / math.sqrt(cell_total)
    first, second = pl.pallas_call(
        lambda *refs: finish_kernel(scale, *refs),
        out_shape=(
            jax.ShapeDtypeStruct((27, LAST // reps, 256), F32),
            jax.ShapeDtypeStruct((27, LAST // reps, LAST), F32),
        ),
        in_specs=[VMEM],
        out_specs=(VMEM, VMEM),
        compiler_params=pltpu.CompilerParams(vmem_limit_bytes=16 << 20),
    )(whole)
    first = jnp.swapaxes(first, 1, 2).reshape(3, 3, 3, 256, LAST // reps)
    second = jnp.swapaxes(second, 1, 2).reshape(3, 3, 3, LAST, LAST // reps)
    return input_grad[None], first, second


def solution(mesh):
    devices = mesh.devices
    tiles, reps = devices.shape
    side = math.isqrt(tiles // 2)
    wide_mesh = Mesh(devices.reshape(side, tiles // 2 // side, 2, reps), ("y", "z", "core", "x"))
    in_specs = (
        P("x", None, TILE_AXES, None, None),
        P("x", None, TILE_AXES, None, None),
        P(),
        P(),
        P("x", None),
        P("x", None),
        P("x", None),
    )
    out_specs = (
        P("x", None, TILE_AXES, None, None),
        P(None, None, None, None, "x"),
        P(None, None, None, None, "x"),
    )
    return jax.shard_map(
        body, mesh=wide_mesh, in_specs=in_specs, out_specs=out_specs, check_vma=False
    )
```

time: 655 us -> 121 us (0.18)
  blocking collectives: 504 us -> 84.7 us
  matrix products: 44.3 us -> 0 us
  waiting for transfers between devices: 32 us -> 1.13 us
  between operations: 18.7 us -> 0.69 us
  local copies, waits for them, and re-layouts: 24.2 us -> 8.61 us
  Pallas kernels: 0 us -> 11.8 us
  other arithmetic: 13.6 us -> 2.43 us
    psum x1 -> x0, blocking collectives: 504 us -> none  [body(): lax.psum((quarter_first, quarter_second), 'tile')]
    all_to_all x0 -> x4, blocking collectives: none -> 78.5 us  [the longest x1 21.7 us: body(): own = wide_sum(lax.all_to_all(of_rep, PLANE_AXES, 0, 0, tiled=True))]
    dot_general x54 -> x0, matrix products: 32 us -> none  [weight_grad(): jnp.einsum('fhwi,fhwo->io', window, cot_values, preferred_element_type=jn...]
    reduce_scatter x2 -> x0, waiting for transfers between devices: 32 us -> none  [the longest x1 32 us: body(): lax.psum_scatter(grad_first.astype(jnp.bfloat16), 'rep', scatter_dimensio...]
    conv_general_dilated x3 -> x0, matrix products: 12.4 us -> none  [conv_rows(): lax.conv_general_dilated(values[None], kernel, (1, 1, 1), ((0, 0), (0, 0)...]
    pallas_call x0 -> x3, Pallas kernels: none -> 11.8 us  [the longest x1 10.6 us: body(): pl.pallas_call(main_kernel, out_shape=(jax.ShapeDtypeStruct(local_in.shap...]
    convert_element_type x3 -> x0, local copies, waits for them, and re-layouts: 7.49 us -> none  [the longest x1 3.88 us: body(): grad_first.astype(jnp.bfloat16)]
    conv_general_dilated x12 -> x0, local copies, waits for them, and re-layouts: 7.01 us -> none  [conv_rows(): lax.conv_general_dilated(values[None], kernel, (1, 1, 1), ((0, 0), (0, 0)...]
  transfers between devices with their start and end apart: 6 -> 2, of which waited for: 1 -> 1; matrix products, arithmetic and copies ran while one was open for 8% -> 0% of each run, Pallas kernels for 0% -> 0%
where the time goes in v1:
time: 121 us; the launch traced here: 120 us
  blocking collectives  84.7 us (70%)
  Pallas kernels  11.8 us (10%)
  starting transfers between devices  10.7 us (9%)
  local copies, waits for them, and re-layouts  8.61 us (7%)
  other arithmetic  2.43 us (2%)
    all_to_all x1, blocking collectives, body(): own = wide_sum(lax.all_to_all(of_rep, PLANE_AXES, 0, 0, tiled=True))  21.7 us
    all_to_all x1, blocking collectives, body(): of_rep = wide_sum(lax.all_to_all(of_core, 'x', 0, 0, tiled=True))  21.5 us
    all_to_all x1, blocking collectives, body(): half = lax.all_to_all(own, PLANE_AXES, 0, 0, tiled=True)  21 us
    all_to_all x1, blocking collectives, body(): of_core = wide_sum(lax.all_to_all(parts, 'core', 0, 0, tiled=True))  14.3 us
    pallas_call x1, Pallas kernels, body(): pl.pallas_call(main_kernel, out_shape=(jax.ShapeDtypeStruct(local_in.shap...  10.6 us
    unnamed x18, local copies, waits for them, and re-layouts  8.49 us
    all_gather x1, blocking collectives, body(): whole = lax.all_gather(half, 'core', axis=0).reshape(cores, 81, depth, LAST)  6.19 us
    ppermute x1, starting transfers between devices, body(): lax.ppermute(to_next, TILE_AXES, [(i, (i + 1) % tiles) for i in range(til...  5.39 us
  transfers between devices with their start and end apart: 2, of which 1 were waited for; matrix products, arithmetic and copies ran while one was open for 0% of the time, Pallas kernels for 0%

profile of v1, /device:TPU:1, one launch (start us, length us, event | category | flops | bytes accessed | tf_op | source)
XLA Modules:
  0.0 120.1 jit_solution(17456671605752132372)
XLA Ops:
  0.6 0.0 copy-start.1
  0.6 1.0 copy-done.1
  1.6 0.9 copy-done.3
  2.6 5.4 %collective-permute-start = (bf16[36,16,128]{2,1,0:T(8,128)(2,1)S(1)}, bf16[36,16,128]{2,1,0:T(8,128)(2,1)S(1)}, u32[]{:S(2)}, u32[]{:S(2)}) collective-permute-start(bf16[36,16,128]{2,1,0:T(8,128)(2,1)S(1)} %get-tuple-element.9), channel_id=1, source_target_pairs={{0,4},{4,8},{8,12},{12,16},{16,20},{20,24},{24,28},{28,32},{32,36}... | collective-permute-start | bytes 442376 | tf_op jit(solution)/shard_map/ppermute | solution.py:268
  8.0 5.3 %collective-permute-start.1 = (bf16[36,16,128]{2,1,0:T(8,128)(2,1)S(1)}, bf16[36,16,128]{2,1,0:T(8,128)(2,1)S(1)}, u32[]{:S(2)}, u32[]{:S(2)}) collective-permute-start(bf16[36,16,128]{2,1,0:T(8,128)(2,1)S(1)} %get-tuple-element.10), channel_id=1, source_target_pairs={{4,0},{8,4},{12,8},{16,12},{20,16},{24,20},{28,24},{32,28},{36,32}... | collective-permute-start | bytes 442376 | tf_op jit(solution)/shard_map/ppermute | solution.py:269
  13.3 1.1 collective-permute-done.1.below_ref
  14.5 1.5 %copy-done = bf16[3,3,3,256,128]{4,3,2,1,0:T(8,128)(2,1)S(1)} copy-done((bf16[3,3,3,256,128]{4,3,2,1,0:T(8,128)(2,1)S(1)}, bf16[3,3,3,256,128]{4,3,2,1,0:T(8,128)(2,1)}, u32[]{:S(2)}) %copy-start) | copy-done | bytes 1769496
  16.0 1.0 copy-done.2
  17.0 0.9 copy-done.4
  17.9 1.2 copy-done.5
  19.1 0.7 copy-done.6
  19.7 0.7 copy-done.7
  20.4 0.7 copy-done.8
  21.0 10.6 %shard_map.95 = (bf16[6,8,16,256]{3,2,1,0:T(8,128)(2,1)}, bf16[2,4,81,16,128]{4,3,2,1,0:T(8,128)(2,1)}) custom-call(s32[1,128]{1,0:T(1,128)S(1)} %copy-done.6, s32[1,8]{1,0:T(1,128)S(1)} %copy-done.7, s32[1,8]{1,0:T(1,128)S(1)} %copy-done.8, bf16[6,8,16,256]{3,2,1,0:T(8,128)(2,1)S(1)} %bitcast.18, bf16[2,16,32,128]{3,2,1,0:T(8,128)(2,1)S(1)} %bitcast.20, ...), custom_call_target="tpu_custom_call" | custom-call | tf_op jit(solution)/shard_map/pallas_call | solution.py:272
  31.7 14.3 %all_to_all.20 = bf16[2,4,1296,128]{3,2,1,0:T(8,128)(2,1)S(1)} all-to-all(bf16[2,4,1296,128]{3,2,1,0:T(8,128)(2,1)} %bitcast.22), channel_id=1, replica_groups=mesh['y'=8,'z'=8,'core'=2,'x'=4] {'core'}, dimensions={0} | all-to-all | bytes 5308416 | tf_op jit(solution)/shard_map/all_to_all | solution.py:302
  45.9 2.0 %reduce_sum.36 = bf16[4,1296,128]{2,1,0:T(8,128)(2,1)} reduce(bf16[2,4,1296,128]{3,2,1,0:T(8,128)(2,1)S(1)} %all_to_all.20, bf16[]{:T(256)} %constant.6.clone.1), dimensions={0}, to_apply=%region_0.0 | reduce | flops 663552 | bytes 3981314 | tf_op jit(solution)/shard_map/reduce_sum | solution.py:253
  47.9 21.5 %all_to_all.21 = bf16[4,1296,128]{2,1,0:T(8,128)(2,1)S(1)} all-to-all(bf16[4,1296,128]{2,1,0:T(8,128)(2,1)} %reduce_sum.36), channel_id=1, replica_groups=mesh['y'=8,'z'=8,'core'=2,'x'=4] {'x'}, dimensions={0} | all-to-all | bytes 2654208 | tf_op jit(solution)/shard_map/all_to_all | solution.py:303
  69.4 0.4 reduce_sum.37
  69.8 21.7 %all_to_all.22 = bf16[64,24,128]{2,1,0:T(8,128)(2,1)S(1)} all-to-all(bf16[64,24,128]{2,1,0:T(8,128)(2,1)S(1)} %bitcast.23), channel_id=1, replica_groups=mesh['y'=8,'z'=8,'core'=2,'x'=4] {'y','z'}, dimensions={0} | all-to-all | bytes 786432 | tf_op jit(solution)/shard_map/all_to_all | solution.py:306
  91.6 0.1 reduce_sum.38
  91.7 0.1 broadcast_in_dim.10
  91.7 21.0 %all_to_all.23 = bf16[64,24,128]{2,1,0:T(8,128)(2,1)S(1)} all-to-all(bf16[64,24,128]{2,1,0:T(8,128)(2,1)S(1)} %broadcast_in_dim.10), channel_id=1, replica_groups=mesh['y'=8,'z'=8,'core'=2,'x'=4] {'y','z'}, dimensions={0} | all-to-all | bytes 786432 | tf_op jit(solution)/shard_map/all_to_all | solution.py:308
  112.8 6.2 %all_gather.7 = bf16[2,1296,128]{2,1,0:T(8,128)(2,1)S(1)} all-gather(bf16[1,1296,128]{2,1,0:T(8,128)(2,1)S(1)} %bitcast.24), channel_id=1, replica_groups=mesh['y'=8,'z'=8,'core'=2,'x'=4] {'core'}, dimensions={0}, use_global_device_ids=true | all-gather | bytes 995328 | tf_op jit(solution)/shard_map/all_gather | solution.py:310
  119.0 1.2 shard_map.96
  (12 shorter events, 0.1 us)
Async XLA Ops:
  0.6 1.0 copy-start.1
  1.6 0.9 copy-start.3
  2.6 10.7 %collective-permute-start = (bf16[36,16,128]{2,1,0:T(8,128)(2,1)S(1)}, bf16[36,16,128]{2,1,0:T(8,128)(2,1)S(1)}, u32[]{:S(2)}, u32[]{:S(2)}) collective-permute-start(bf16[36,16,128]{2,1,0:T(8,128)(2,1)S(1)} %get-tuple-element.9), channel_id=1, source_target_pairs={{0,4},{4,8},{8,12},{12,16},{16,20},{20,24},{24,28},{28,32},{32,36}... | collective-permute-start | bytes 442376 | tf_op jit(solution)/shard_map/ppermute | solution.py:268
  8.0 6.5 %collective-permute-start.1 = (bf16[36,16,128]{2,1,0:T(8,128)(2,1)S(1)}, bf16[36,16,128]{2,1,0:T(8,128)(2,1)S(1)}, u32[]{:S(2)}, u32[]{:S(2)}) collective-permute-start(bf16[36,16,128]{2,1,0:T(8,128)(2,1)S(1)} %get-tuple-element.10), channel_id=1, source_target_pairs={{4,0},{8,4},{12,8},{16,12},{20,16},{24,20},{28,24},{32,28},{36,32}... | collective-permute-start | bytes 442376 | tf_op jit(solution)/shard_map/ppermute | solution.py:269
  14.5 1.5 %copy-start = (bf16[3,3,3,256,128]{4,3,2,1,0:T(8,128)(2,1)S(1)}, bf16[3,3,3,256,128]{4,3,2,1,0:T(8,128)(2,1)}, u32[]{:S(2)}) copy-start(bf16[3,3,3,256,128]{4,3,2,1,0:T(8,128)(2,1)} %param.9) | copy-start | bytes 5308420
  16.0 1.0 copy-start.2
  17.0 0.9 copy-start.4
  17.9 1.2 copy-start.5
  19.1 0.7 copy-start.6
  19.7 0.7 copy-start.7
  20.4 0.7 copy-start.8

commit v2 on v1

v2 whole, which is shorter than its diff:
```python
import math

import jax
import jax.numpy as jnp
from jax import lax
from jax.experimental import pallas as pl
from jax.experimental.pallas import tpu as pltpu
from jax.sharding import Mesh
from jax.sharding import PartitionSpec as P

TILE_AXES = ("y", "z", "core")
PLANE_AXES = ("y", "z")
BF = jnp.bfloat16
F32 = jnp.float32
NT = (((1,), (1,)), ((), ()))
TN = (((0,), (0,)), ((), ()))
LAST = 128
TILE_COT = 96
TILE_BLOCKS = 160
RIM_COT = 24
RIM_BLOCKS = 36
PACK_SECOND = 40
PACK_ROW = 72
PACK_BLOCKS = 76
UP, DOWN, COLS, KEEP, SIB_COLS, SIB_KEEP, RIM_SCALE, SIB_SCALE = range(8)
SECOND_AT = 24
EXTRA_AT = 36
GRAD_BLOCKS = 42


def dot(lhs, rhs, dims=(((1,), (0,)), ((), ()))):
    return lax.dot_general(lhs, rhs, dims, preferred_element_type=F32)


def sigmoid(values):
    return 1.0 / (1.0 + jnp.exp(-values))


def column_shifts(values):
    column = lax.broadcasted_iota(jnp.int32, (1, 16, values.shape[2]), 1)
    left = jnp.where(column == 0, 0.0, pltpu.roll(values, 1, 1))
    right = jnp.where(column == 15, 0.0, pltpu.roll(values, 15, 1))
    return left, right


def scale_of(scales, which):
    return scales[which : which + 1].reshape(1, 1, LAST)


def low_mask(scales, which):
    column = lax.broadcasted_iota(jnp.int32, (1, 16, LAST), 1).astype(F32)
    return jnp.where(column < scale_of(scales, which), 1.0, 0.0)


def high_mask(scales, which):
    column = lax.broadcasted_iota(jnp.int32, (1, 32, LAST), 1).astype(F32)
    return jnp.where(column < 2.0 * scale_of(scales, which), 1.0, 0.0)


def twice(values):
    return jnp.concatenate([values, values], 2)


def joined(blocks):
    halves = blocks.reshape(blocks.shape[0] // 2, 2, 16, LAST)
    return jnp.concatenate([halves[:, 0], halves[:, 1]], 2)


def tile_rows(tile_ref, frame):
    return joined(tile_ref[frame * 16 : frame * 16 + 16]).astype(F32)


def eff_frame(read, frame, keep):
    values = read(frame)
    return jnp.where(keep > 0.5, values, read(4)) if frame < 4 else values


def load_scales(clip_ref, cols_ref, start_ref):
    tile = lax.axis_index(TILE_AXES)
    tiles = lax.axis_size(TILE_AXES)
    even = lax.axis_index("core") == 0
    own = clip_ref[0, tile]
    up_same = (tile > 0) & (clip_ref[0, jnp.maximum(tile - 1, 0)] == own)
    down_same = (tile + 1 < tiles) & (clip_ref[0, jnp.minimum(tile + 1, tiles - 1)] == own)
    sibling = clip_ref[0, jnp.where(even, tile + 1, tile - 1)]
    up = jnp.where(up_same, 1.0, 0.0)
    down = jnp.where(down_same, 1.0, 0.0)
    return (
        up,
        down,
        cols_ref[0, own].astype(F32),
        jnp.where(start_ref[0, own] == 0, 0.0, 1.0),
        cols_ref[0, sibling].astype(F32),
        jnp.where(start_ref[0, sibling] == 0, 0.0, 1.0),
        jnp.where(even, up, down),
        jnp.where(even, down, up),
    )


def pack_kernel(
    clip_any, cols_any, start_any, in_any, cot_any, tile_ref, rim_ref, scales_ref,
    clip_ref, cols_ref, start_ref, in_ref, cot_ref, sems,
):
    copies = [
        pltpu.make_async_copy(source, target, sems.at[n])
        for n, (source, target) in enumerate(
            (
                (clip_any, clip_ref),
                (cols_any, cols_ref),
                (start_any, start_ref),
                (in_any, in_ref),
                (cot_any, cot_ref),
            )
        )
    ]
    for copy in copies:
        copy.start()
    for copy in copies[:3]:
        copy.wait()
    for row, value in enumerate(load_scales(clip_ref, cols_ref, start_ref)):
        scales_ref[row : row + 1] = jnp.full((1, LAST), value, F32)
    odd = lax.axis_index("core")
    copies[3].wait()
    for frame in range(6):
        for row in range(8):
            for half in range(2):
                tile_ref[frame * 16 + row * 2 + half] = in_ref[
                    frame, row, :, half * LAST : (half + 1) * LAST
                ]
    copies[4].wait()
    for frame in range(2):
        for half in range(2):
            for row in range(16):
                tile_ref[TILE_COT + frame * 32 + row * 2 + half] = cot_ref[
                    frame, row, half * 16 : (half + 1) * 16, :
                ]
    for frame in range(6):
        rim_ref[frame * 4 : frame * 4 + 4] = tile_ref[pl.ds(frame * 16 + odd * 12, 4)]
    for frame in range(2):
        at = RIM_COT + frame * 6
        rim_ref[at : at + 6] = tile_ref[pl.ds(TILE_COT + frame * 32 + odd * 26, 6)]


def pair_sums(rows, first, pair, put):
    zeros = jnp.zeros((pair.shape[0], 8, LAST), F32)
    pair[:, 0:8] = zeros
    pair[:, 40:48] = zeros
    count = rows.shape[0] - 1
    pair[0:count, 8:40] = rows[0:count] + rows[1 : count + 1]
    before, even, odd, after = (pair[0:count, pl.ds(begin, 16, 2), :] for begin in (7, 8, 9, 10))
    for kw, value in ((0, odd + after), (1, even + odd), (2, before + even)):
        put(kw, value.astype(BF))


def first_kernel(
    scales, tile_ref, sib_ref, rim_ref, w1_any, w2_any, packet_ref,
    w1_ref, w2_ref, act, rows, pair, cots, sems,
):
    load_w1 = pltpu.make_async_copy(w1_any, w1_ref, sems.at[0])
    load_w2 = pltpu.make_async_copy(w2_any, w2_ref, sems.at[1])
    load_w1.start()
    load_w2.start()
    odd = lax.axis_index("core")
    keep = twice(scale_of(scales, KEEP))
    low = low_mask(scales, COLS)
    wide_low = twice(low)
    rim_scale, sib_scale = scale_of(scales, RIM_SCALE), scale_of(scales, SIB_SCALE)
    rim_at = odd * 10
    sib_at = 10 - odd * 10

    for frame in range(6):
        for at, count, read, mask in (
            (rim_at, 2, lambda f: joined(rim_ref[f * 4 : f * 4 + 4]).astype(F32), wide_low * twice(rim_scale)),
            (2, 8, lambda f: tile_rows(tile_ref, f), wide_low),
            (sib_at, 2, lambda f: joined(sib_ref[pl.ds(f * 16 + odd * 12, 4)]).astype(F32), wide_low * twice(sib_scale)),
        ):
            values = eff_frame(read, frame, keep)
            values = values * sigmoid(values) * mask
            left, right = column_shifts(values)
            act[0, frame, pl.ds(at, count)] = left.astype(BF)
            act[1, frame, pl.ds(at, count)] = values.astype(BF)
            act[2, frame, pl.ds(at, count)] = right.astype(BF)

    high = high_mask(scales, COLS)
    for frame in range(2):
        at = TILE_COT + frame * 32
        rows[frame, 3:19] = tile_ref[at : at + 32].reshape(16, 32, LAST).astype(F32) * high
        raw = rim_ref[RIM_COT + frame * 6 : RIM_COT + frame * 6 + 6].reshape(3, 32, LAST)
        rows[frame, pl.ds(odd * 19, 3)] = raw.astype(F32) * (high * rim_scale)
        raw = sib_ref[pl.ds(at + odd * 26, 6)].reshape(3, 32, LAST)
        rows[frame, pl.ds(19 - odd * 19, 3)] = raw.astype(F32) * (high * sib_scale)
        far = rows[frame, pl.ds(2 + odd * 17, 1)].reshape(2, 16, LAST)
        packet_ref[PACK_ROW + frame * 2 : PACK_ROW + frame * 2 + 2] = far.astype(BF)

    load_w1.wait()
    first_out = None
    for step in range(9):
        kt, kh = step // 3, step % 3
        window = jnp.concatenate(
            [act[kw, kt : kt + 4, kh : kh + 10].reshape(640, 256) for kw in range(3)], 1
        )
        term = dot(window, w1_ref[step * 3 : step * 3 + 3].reshape(768, LAST))
        first_out = term if first_out is None else first_out + term
    first_out = first_out.reshape(40, 16, LAST)
    row = lax.broadcasted_iota(jnp.int32, (40, 1, 1), 0) % 10
    row_scale = jnp.where(
        row == 0, scale_of(scales, UP), jnp.where(row == 9, scale_of(scales, DOWN), 1.0)
    )
    gate = sigmoid(first_out)
    second_in = (first_out * gate * low).astype(BF).reshape(4, 10, 16, LAST)
    packet_ref[PACK_SECOND:PACK_ROW] = second_in[:, 1:9].reshape(32, 16, LAST)
    slope = gate * (1.0 + first_out * (1.0 - gate)) * (low * row_scale)

    for frame in range(2):

        def put(kw, sums):
            for n in range(21):
                if n % 2 == 1:
                    targets = ((1, n // 2),)
                else:
                    targets = ((0, n // 2 - 1), (2, n // 2))
                for kh, place in targets:
                    if 0 <= place < 10:
                        tap = kh * 3 + kw
                        cots[frame, place, :, tap * LAST : (tap + 1) * LAST] = sums[n]

        pair_sums(rows[frame], -3, pair, put)

    load_w2.wait()
    flat = jnp.concatenate(
        [
            jnp.concatenate([w2_ref[kt * 9 + tap] for tap in range(9)], 1)
            for kt in range(3)
        ],
        0,
    )
    spread = dot(cots[...].reshape(320, 1152), flat, NT)
    for frame in range(4):
        total = None
        for kt in range(3):
            if 0 <= frame - kt < 2:
                term = spread[
                    (frame - kt) * 160 : (frame - kt + 1) * 160, kt * LAST : (kt + 1) * LAST
                ]
                total = term if total is None else total + term
        first_grad = total.reshape(10, 16, LAST) * slope[frame * 10 : frame * 10 + 10]
        packet_ref[frame * 10 : frame * 10 + 10] = first_grad.astype(BF)


def input_kernel(
    scales, tile_ref, sib_ref, packet_ref, w1_any, grad_ref, act_ref, w1_ref, firsts, sems
):
    load_w1 = pltpu.make_async_copy(w1_any, w1_ref, sems.at[0])
    load_w1.start()
    for frame in range(4):
        first_grad = packet_ref[frame * 10 : frame * 10 + 10]
        before, after = column_shifts(first_grad.astype(F32))
        for kw, value in ((0, after.astype(BF)), (1, first_grad), (2, before.astype(BF))):
            for kh in range(3):
                tap = kh * 3 + kw
                firsts[frame, :, :, tap * LAST : (tap + 1) * LAST] = value[2 - kh : 10 - kh]
    load_w1.wait()
    shifted = firsts[...].reshape(512, 1152)
    by_depth = [
        dot(shifted, jnp.concatenate([w1_ref[kt * 9 + tap] for tap in range(9)], 1), NT)
        for kt in range(3)
    ]
    keep = twice(scale_of(scales, KEEP))
    low = twice(low_mask(scales, COLS))
    carried = None
    for frame in range(6):
        total = None
        for kt in range(3):
            if 0 <= frame - kt < 4:
                term = by_depth[kt][(frame - kt) * 128 : (frame - kt + 1) * 128]
                total = term if total is None else total + term
        values = eff_frame(lambda f: tile_rows(tile_ref, f), frame, keep)
        gate = sigmoid(values)
        act_ref[0, frame] = (values * gate * low).astype(BF)
        pre = total.reshape(8, 16, 256) * (gate * (1.0 + values * (1.0 - gate)) * low)
        if frame < 4:
            carried = pre if carried is None else carried + pre
            grad_ref[frame] = (pre * keep).astype(BF)
        elif frame == 4:
            grad_ref[frame] = (pre + carried * (1.0 - keep)).astype(BF)
        else:
            grad_ref[frame] = pre.astype(BF)
    keep = twice(scale_of(scales, SIB_KEEP))
    low = twice(low_mask(scales, SIB_COLS))
    for frame in range(6):
        values = eff_frame(lambda f: tile_rows(sib_ref, f), frame, keep)
        act_ref[1, frame] = (values * sigmoid(values) * low).astype(BF)


def weight_kernel(
    scales, tile_ref, sib_ref, packet_ref, sib_packet_ref, act_ref, part_ref, rows, pair, sums, cols
):
    odd = lax.axis_index("core")
    reps = part_ref.shape[0]
    link = scale_of(scales, SIB_SCALE)
    for own, tile, other, packet, which in (
        (True, tile_ref, sib_ref, packet_ref, COLS),
        (False, sib_ref, tile_ref, sib_packet_ref, SIB_COLS),
    ):
        slot = 0 if own else 1
        lower = odd if own else 1 - odd
        high = high_mask(scales, which)
        for frame in range(2):
            at = TILE_COT + frame * 32
            rows[1:17] = tile[at : at + 32].reshape(16, 32, LAST).astype(F32) * high
            far = packet[PACK_ROW + frame * 2 : PACK_ROW + frame * 2 + 2].reshape(1, 32, LAST)
            rows[pl.ds(lower * 17, 1)] = far.astype(F32)
            near = other[pl.ds(at + lower * 30, 2)].reshape(1, 32, LAST)
            rows[pl.ds(17 - lower * 17, 1)] = near.astype(F32) * (high * link)

            def put(kw, values):
                for n in range(17):
                    place = n // 2 if n % 2 == 0 else 9 + n // 2
                    sums[kw, slot, frame, place] = values[n]

            pair_sums(rows[...], -1, pair, put)
        for frame in range(4):
            first_grad = packet[frame * 10 : frame * 10 + 10]
            before, after = column_shifts(first_grad.astype(F32))
            cols[0, slot, frame] = after.astype(BF)
            cols[1, slot, frame] = first_grad
            cols[2, slot, frame] = before.astype(BF)

    act_all = jnp.concatenate([act_ref[:, kt : kt + 4].reshape(1024, 256) for kt in range(3)], 1)
    seconds = [
        ref[PACK_SECOND:PACK_ROW].reshape(4, 8, 16, LAST) for ref in (packet_ref, sib_packet_ref)
    ]
    second_all = jnp.concatenate(
        [
            jnp.concatenate([part[kt : kt + 2].reshape(256, LAST) for part in seconds], 0)
            for kt in range(3)
        ],
        1,
    )

    def put_block(block, at):
        part_ref[:, at] = block.astype(BF).reshape(reps, LAST // reps, LAST)

    def first_taps(step, at):
        tap = 5 * odd + step
        window = cols[tap % 3, :, :, pl.ds(2 - tap // 3, 8)].reshape(1024, LAST)
        block = dot(window, act_all, TN)
        for n in range(6):
            put_block(block[:, n * LAST : (n + 1) * LAST], at + n)

    def second_taps(step, at):
        tap = 4 * odd + step
        kh = tap // 3
        begin = jnp.where(kh == 0, 1, jnp.where(kh == 1, 9, 0))
        window = sums[tap % 3, :, :, pl.ds(begin, 8)].reshape(512, LAST)
        block = dot(window, second_all, TN)
        for n in range(3):
            put_block(block[:, n * LAST : (n + 1) * LAST], at + n)

    for step in range(4):
        first_taps(step, step * 6)
        second_taps(step, SECOND_AT + step * 3)

    @pl.when(odd == 0)
    def _():
        first_taps(4, EXTRA_AT)

    @pl.when(odd == 1)
    def _():
        second_taps(4, EXTRA_AT)
        part_ref[:, EXTRA_AT + 3 : EXTRA_AT + 6] = jnp.zeros((reps, 3, LAST // reps, LAST), BF)


def finish_kernel(scale, whole_ref, first_ref, second_ref):
    for core in range(2):

        def block(at):
            return whole_ref[core, at].astype(F32) * scale

        for step in range(5 - core):
            for kt in range(3):
                for half in range(2):
                    at = (step * 6 if step < 4 else EXTRA_AT) + kt * 2 + half
                    tap = kt * 9 + 5 * core + step
                    first_ref[tap, :, half * LAST : (half + 1) * LAST] = block(at)
        for step in range(4 + core):
            for kt in range(3):
                at = (SECOND_AT + step * 3 if step < 4 else EXTRA_AT) + kt
                second_ref[kt * 9 + 4 * core + step] = block(at)


VMEM = pl.BlockSpec(memory_space=pltpu.VMEM)
HBM = pl.BlockSpec(memory_space=pltpu.HBM)


def params(mebibytes):
    return pltpu.CompilerParams(vmem_limit_bytes=mebibytes << 20)


def cost(flops, moved):
    return pl.CostEstimate(flops=flops, bytes_accessed=moved, transcendentals=0)


def wide_sum(parts):
    return jnp.sum(parts.astype(F32), axis=0).astype(BF)


def blocks(count):
    return jax.ShapeDtypeStruct((count, 16, LAST), BF)


def body(inputs, cotangent, first_weight, second_weight, tile_clip, clip_cols, clip_start):
    tiles = lax.axis_size(TILE_AXES)
    reps, plane = lax.axis_size("x"), lax.axis_size(PLANE_AXES)
    local_in, local_cot, tile_clip, clip_cols, clip_start, w1, w2 = (
        pltpu.with_memory_space_constraint(array, pltpu.HBM)
        for array in (
            inputs[0],
            cotangent[0],
            tile_clip,
            clip_cols,
            clip_start,
            first_weight.reshape(27, 256, LAST),
            second_weight.reshape(27, LAST, LAST),
        )
    )
    tile, rim, scales = pl.pallas_call(
        pack_kernel,
        out_shape=(blocks(TILE_BLOCKS), blocks(RIM_BLOCKS), jax.ShapeDtypeStruct((8, LAST), F32)),
        in_specs=[HBM] * 5,
        out_specs=(VMEM, VMEM, VMEM),
        scratch_shapes=[
            pltpu.SMEM(tile_clip.shape, jnp.int32),
            pltpu.SMEM(clip_cols.shape, jnp.int32),
            pltpu.SMEM(clip_start.shape, jnp.int32),
            pltpu.VMEM(local_in.shape, BF),
            pltpu.VMEM(local_cot.shape, BF),
            pltpu.SemaphoreType.DMA((5,)),
        ],
        compiler_params=params(8),
    )(tile_clip, clip_cols, clip_start, local_in, local_cot)

    swap = [(0, 1), (1, 0)]
    across = [(i, (i + 1) % tiles) for i in range(1, tiles, 2)]
    across += [(b, a) for a, b in across]
    rim = lax.ppermute(rim, TILE_AXES, across)
    sibling = lax.ppermute(tile, "core", swap)

    packet = pl.pallas_call(
        first_kernel,
        out_shape=blocks(PACK_BLOCKS),
        in_specs=[VMEM] * 4 + [HBM] * 2,
        out_specs=VMEM,
        scratch_shapes=[
            pltpu.VMEM((27, 256, LAST), BF),
            pltpu.VMEM((27, LAST, LAST), BF),
            pltpu.VMEM((3, 6, 12, 16, 256), BF),
            pltpu.VMEM((2, 22, 32, LAST), F32),
            pltpu.VMEM((21, 48, LAST), F32),
            pltpu.VMEM((2, 10, 16, 9 * LAST), BF),
            pltpu.SemaphoreType.DMA((2,)),
        ],
        compiler_params=params(32),
        cost_estimate=cost(2 * 10**9, 4 * 10**6),
    )(scales, tile, sibling, rim, w1, w2)

    sib_packet = lax.ppermute(packet, "core", swap)

    input_grad, act = pl.pallas_call(
        input_kernel,
        out_shape=(
            jax.ShapeDtypeStruct(local_in.shape, BF),
            jax.ShapeDtypeStruct((2, 6, 8, 16, 256), BF),
        ),
        in_specs=[VMEM] * 4 + [HBM],
        out_specs=(VMEM, VMEM),
        scratch_shapes=[
            pltpu.VMEM((27, 256, LAST), BF),
            pltpu.VMEM((4, 8, 16, 9 * LAST), BF),
            pltpu.SemaphoreType.DMA((1,)),
        ],
        compiler_params=params(32),
        cost_estimate=cost(2 * 10**9, 4 * 10**6),
    )(scales, tile, sibling, packet, w1)

    depth = LAST // reps
    parts = pl.pallas_call(
        weight_kernel,
        out_shape=jax.ShapeDtypeStruct((reps, GRAD_BLOCKS, depth, LAST), BF),
        in_specs=[VMEM] * 6,
        out_specs=VMEM,
        scratch_shapes=[
            pltpu.VMEM((18, 32, LAST), F32),
            pltpu.VMEM((17, 48, LAST), F32),
            pltpu.VMEM((3, 2, 2, 17, 16, LAST), BF),
            pltpu.VMEM((3, 2, 4, 10, 16, LAST), BF),
        ],
        compiler_params=params(32),
        cost_estimate=cost(2 * 10**9, 4 * 10**6),
    )(scales, tile, sibling, packet, sib_packet, act)

    count = GRAD_BLOCKS * depth
    parts = parts.reshape(reps, count, LAST)
    of_rep = wide_sum(lax.all_to_all(parts, "x", 0, 0, tiled=True))
    share = -(-count // plane // 8) * 8
    of_rep = jnp.pad(of_rep, ((0, share * plane - count), (0, 0))).reshape(plane, share, LAST)
    own = wide_sum(lax.all_to_all(of_rep, PLANE_AXES, 0, 0, tiled=True))
    own = jnp.broadcast_to(own[None], (plane, share, LAST))
    half = lax.all_to_all(own, PLANE_AXES, 0, 0, tiled=True)
    half = half.reshape(plane * share, LAST)[:count]
    whole = lax.all_gather(half, "core", axis=0).reshape(2, GRAD_BLOCKS, depth, LAST)

    cell_total = tiles * reps * cotangent.shape[1] * cotangent.shape[2] * cotangent.shape[3]
    scale = 1.0 / math.sqrt(cell_total)
    first, second = pl.pallas_call(
        lambda *refs: finish_kernel(scale, *refs),
        out_shape=(
            jax.ShapeDtypeStruct((27, depth, 256), F32),
            jax.ShapeDtypeStruct((27, depth, LAST), F32),
        ),
        in_specs=[VMEM],
        out_specs=(VMEM, VMEM),
        compiler_params=params(16),
    )(whole)
    first = jnp.swapaxes(first, 1, 2).reshape(3, 3, 3, 256, depth)
    second = jnp.swapaxes(second, 1, 2).reshape(3, 3, 3, LAST, depth)
    return input_grad[None], first, second


def solution(mesh):
    devices = mesh.devices
    tiles, reps = devices.shape
    side = math.isqrt(tiles // 2)
    wide_mesh = Mesh(devices.reshape(side, tiles // 2 // side, 2, reps), ("y", "z", "core", "x"))
    in_specs = (
        P("x", None, TILE_AXES, None, None),
        P("x", None, TILE_AXES, None, None),
        P(),
        P(),
        P("x", None),
        P("x", None),
        P("x", None),
    )
    out_specs = (
        P("x", None, TILE_AXES, None, None),
        P(None, None, None, None, "x"),
        P(None, None, None, None, "x"),
    )
    return jax.shard_map(
        body, mesh=wide_mesh, in_specs=in_specs, out_specs=out_specs, check_vma=False
    )
```

time: 121 us -> 107 us (0.88)
  blocking collectives: 84.7 us -> 69.6 us
  local copies, waits for them, and re-layouts: 8.61 us -> 0.12 us
  starting transfers between devices: 10.7 us -> 17.6 us
  waiting for transfers between devices: 1.13 us -> 4.54 us
  other arithmetic: 2.43 us -> 0.47 us
  Pallas kernels: 11.8 us -> 13.6 us
    all_to_all x2 -> x1, blocking collectives: 35.8 us -> 21.8 us  [body(): of_rep = wide_sum(lax.all_to_all(parts, 'x', 0, 0, tiled=True))]
    unnamed x18 -> x0, local copies, waits for them, and re-layouts: 8.49 us -> none
    ppermute x2 -> x3, starting transfers between devices: 10.7 us -> 17.6 us  [the longest x1 8.79 us: body(): sibling = lax.ppermute(tile, 'core', swap)]
    ppermute x2 -> x3, waiting for transfers between devices: 1.13 us -> 4.54 us  [the longest x1 4.53 us: body(): rim = lax.ppermute(rim, TILE_AXES, across)]
    reduce_sum x3 -> x2, other arithmetic: 2.43 us -> 0.47 us  [wide_sum(): return jnp.sum(parts.astype(F32), axis=0).astype(BF)]
    pallas_call x2 -> x4, Pallas kernels: 10.7 us -> 12.5 us  [the longest x1 5.57 us: body(): pl.pallas_call(first_kernel, out_shape=blocks(PACK_BLOCKS), in_specs=[VME...]
  transfers between devices with their start and end apart: 2 -> 3, of which waited for: 1 -> 1; matrix products, arithmetic and copies ran while one was open for 0% -> 0% of each run, Pallas kernels for 0% -> 3%
where the time goes in v2:
time: 107 us
  blocking collectives  69.6 us (65%)
  starting transfers between devices  17.6 us (16%)
  Pallas kernels  13.6 us (13%)
  waiting for transfers between devices  4.54 us (4%)
    all_to_all x1, blocking collectives, body(): of_rep = wide_sum(lax.all_to_all(parts, 'x', 0, 0, tiled=True))  21.8 us
    all_to_all x1, blocking collectives, body(): own = wide_sum(lax.all_to_all(of_rep, PLANE_AXES, 0, 0, tiled=True))  21.1 us
    all_to_all x1, blocking collectives, body(): half = lax.all_to_all(own, PLANE_AXES, 0, 0, tiled=True)  20.2 us
    ppermute x1, starting transfers between devices, body(): sibling = lax.ppermute(tile, 'core', swap)  8.79 us
    ppermute x1, starting transfers between devices, body(): sib_packet = lax.ppermute(packet, 'core', swap)  6.86 us
    all_gather x1, blocking collectives, body(): lax.all_gather(half, 'core', axis=0).reshape(2, GRAD_BLOCKS, depth, LAST)  6.57 us
    pallas_call x1, Pallas kernels, body(): pl.pallas_call(first_kernel, out_shape=blocks(PACK_BLOCKS), in_specs=[VME...  5.57 us
    ppermute x1, waiting for transfers between devices, body(): rim = lax.ppermute(rim, TILE_AXES, across)  4.53 us
  transfers between devices with their start and end apart: 3, of which 1 were waited for; matrix products, arithmetic and copies ran while one was open for 0% of the time, Pallas kernels for 3%

profile of v2, /device:TPU:1, one launch (start us, length us, event | category | flops | bytes accessed | tf_op | source)
XLA Modules:
  0.0 106.6 jit_solution(12018064082434461668)
XLA Ops:
  0.6 1.1 %shard_map.94 = (bf16[160,16,128]{2,1,0:T(8,128)(2,1)S(1)}, bf16[36,16,128]{2,1,0:T(8,128)(2,1)S(1)}, f32[8,128]{1,0:T(8,128)S(1)}) custom-call(s32[1,128]{1,0:T(1,128)} %clip_any.1, s32[1,8]{1,0:T(1,128)} %cols_any.1, s32[1,8]{1,0:T(1,128)} %start_any.1, bf16[6,8,16,256]{3,2,1,0:T(8,128)(2,1)} %bitcast.19, bf16[2,16,32,128]{3,2,1,0:T(8,128)(2,1)} %bitcast.20), custom_call_target="tpu_custom_call" | custom-call | tf_op jit(solution)/shard_map/pallas_call | solution.py:427
  1.8 8.8 %collective-permute-start = (bf16[160,16,128]{2,1,0:T(8,128)(2,1)S(1)}, bf16[160,16,128]{2,1,0:T(8,128)(2,1)S(1)}, u32[]{:S(2)}, u32[]{:S(2)}) collective-permute-start(bf16[160,16,128]{2,1,0:T(8,128)(2,1)S(1)} %get-tuple-element.11.tile_ref), channel_id=1, source_target_pairs={{0,4},{4,0},{1,5},{5,1},{2,6},{6,2},{3,7},{7,3},{8,12},{12,8},{9,1... | collective-permute-start | bytes 1966088 | tf_op jit(solution)/shard_map/ppermute | solution.py:447
  10.6 1.9 %collective-permute-start.1 = (bf16[36,16,128]{2,1,0:T(8,128)(2,1)S(1)}, bf16[36,16,128]{2,1,0:T(8,128)(2,1)S(1)}, u32[]{:S(2)}, u32[]{:S(2)}) collective-permute-start(bf16[36,16,128]{2,1,0:T(8,128)(2,1)S(1)} %get-tuple-element.12), channel_id=1, source_target_pairs={{4,8},{12,16},{20,24},{28,32},{36,40},{44,48},{52,56},{60,64},{68,... | collective-permute-start | bytes 442376 | tf_op jit(solution)/shard_map/ppermute | solution.py:446
  12.5 4.5 %collective-permute-done.1.rim_ref = bf16[36,16,128]{2,1,0:T(8,128)(2,1)S(1)} collective-permute-done((bf16[36,16,128]{2,1,0:T(8,128)(2,1)S(1)}, bf16[36,16,128]{2,1,0:T(8,128)(2,1)S(1)}, u32[]{:S(2)}, u32[]{:S(2)}) %collective-permute-start.1) | collective-permute-done | bytes 147488 | tf_op jit(solution)/shard_map/ppermute | solution.py:446
  17.0 0.0 collective-permute-done.sib_ref
  17.0 5.6 %shard_map.95.packet_ref = bf16[76,16,128]{2,1,0:T(8,128)(2,1)S(1)} custom-call(f32[8,128]{1,0:T(8,128)S(1)} %get-tuple-element.10.scales, bf16[160,16,128]{2,1,0:T(8,128)(2,1)S(1)} %get-tuple-element.11.tile_ref, bf16[160,16,128]{2,1,0:T(8,128)(2,1)S(1)} %collective-permute-done.sib_ref, bf16[36,16,128]{2,1,0:T(8,128)(2,1)S(1)} %collective-permute-done.1.rim_ref, ...), custom_call_target="tpu_custom_call" | custom-call | flops 2000000000 | bytes 4000000 | tf_op jit(solution)/shard_map/pallas_call | solution.py:449
  22.6 6.9 %collective-permute-start.2 = (bf16[76,16,128]{2,1,0:T(8,128)(2,1)S(1)}, bf16[76,16,128]{2,1,0:T(8,128)(2,1)S(1)}, u32[]{:S(2)}, u32[]{:S(2)}) collective-permute-start(bf16[76,16,128]{2,1,0:T(8,128)(2,1)S(1)} %shard_map.95.packet_ref), channel_id=1, source_target_pairs={{0,4},{4,0},{1,5},{5,1},{2,6},{6,2},{3,7},{7,3},{8,12},{12,8},{9,1... | collective-permute-start | bytes 933896 | tf_op jit(solution)/shard_map/ppermute | solution.py:467
  29.5 3.6 %shard_map.96 = (bf16[6,8,16,256]{3,2,1,0:T(8,128)(2,1)}, bf16[2,6,8,16,256]{4,3,2,1,0:T(8,128)(2,1)S(1)}) custom-call(f32[8,128]{1,0:T(8,128)S(1)} %get-tuple-element.10.scales, bf16[160,16,128]{2,1,0:T(8,128)(2,1)S(1)} %get-tuple-element.11.tile_ref, bf16[160,16,128]{2,1,0:T(8,128)(2,1)S(1)} %collective-permute-done.sib_ref, ...), custom_call_target="tpu_custom_call" | custom-call | flops 2000000000 | bytes 4000000 | tf_op jit(solution)/shard_map/pallas_call | solution.py:469
  33.1 0.0 collective-permute-done.2.sib_packet_ref
  33.1 2.1 %shard_map.97 = bf16[4,42,32,128]{3,2,1,0:T(8,128)(2,1)S(1)} custom-call(f32[8,128]{1,0:T(8,128)S(1)} %get-tuple-element.10.scales, bf16[160,16,128]{2,1,0:T(8,128)(2,1)S(1)} %get-tuple-element.11.tile_ref, bf16[160,16,128]{2,1,0:T(8,128)(2,1)S(1)} %collective-permute-done.sib_ref, bf16[76,16,128]{2,1,0:T(8,128)(2,1)S(1)} %shard_map.95.packet_ref, ...), custom_call_target="tpu_custom_call" | custom-call | flops 2000000000 | bytes 4000000 | tf_op jit(solution)/shard_map/pallas_call | solution.py:487
  35.3 21.8 %all_to_all.15 = bf16[4,1344,128]{2,1,0:T(8,128)(2,1)S(1)} all-to-all(bf16[4,1344,128]{2,1,0:T(8,128)(2,1)S(1)} %bitcast.16), channel_id=1, replica_groups=mesh['y'=8,'z'=8,'core'=2,'x'=4] {'x'}, dimensions={0} | all-to-all | bytes 2752512 | tf_op jit(solution)/shard_map/all_to_all | solution.py:504
  57.0 0.4 reduce_sum.24
  57.5 21.1 %all_to_all.16 = bf16[64,24,128]{2,1,0:T(8,128)(2,1)S(1)} all-to-all(bf16[64,24,128]{2,1,0:T(8,128)(2,1)S(1)} %bitcast.17), channel_id=1, replica_groups=mesh['y'=8,'z'=8,'core'=2,'x'=4] {'y','z'}, dimensions={0} | all-to-all | bytes 786432 | tf_op jit(solution)/shard_map/all_to_all | solution.py:507
  78.5 0.1 reduce_sum.25
  78.6 0.1 broadcast_in_dim.10
  78.7 20.2 %all_to_all.17 = bf16[64,24,128]{2,1,0:T(8,128)(2,1)S(1)} all-to-all(bf16[64,24,128]{2,1,0:T(8,128)(2,1)S(1)} %broadcast_in_dim.10), channel_id=1, replica_groups=mesh['y'=8,'z'=8,'core'=2,'x'=4] {'y','z'}, dimensions={0} | all-to-all | bytes 786432 | tf_op jit(solution)/shard_map/all_to_all | solution.py:509
  98.9 6.6 %all_gather.7 = bf16[2,1344,128]{2,1,0:T(8,128)(2,1)S(1)} all-gather(bf16[1,1344,128]{2,1,0:T(8,128)(2,1)S(1)} %bitcast.18), channel_id=1, replica_groups=mesh['y'=8,'z'=8,'core'=2,'x'=4] {'core'}, dimensions={0}, use_global_device_ids=true | all-gather | bytes 1032192 | tf_op jit(solution)/shard_map/all_gather | solution.py:511
  105.5 1.1 %shard_map.98 = (f32[27,32,256]{2,1,0:T(8,128)}, f32[27,32,128]{2,1,0:T(8,128)}) custom-call(bf16[2,42,32,128]{3,2,1,0:T(8,128)(2,1)S(1)} %bitcast.15), custom_call_target="tpu_custom_call" | custom-call | tf_op jit(solution)/shard_map/pallas_call | solution.py:515
  (2 shorter events, 0.1 us)
Async XLA Ops:
  1.8 15.3 %collective-permute-start = (bf16[160,16,128]{2,1,0:T(8,128)(2,1)S(1)}, bf16[160,16,128]{2,1,0:T(8,128)(2,1)S(1)}, u32[]{:S(2)}, u32[]{:S(2)}) collective-permute-start(bf16[160,16,128]{2,1,0:T(8,128)(2,1)S(1)} %get-tuple-element.11.tile_ref), channel_id=1, source_target_pairs={{0,4},{4,0},{1,5},{5,1},{2,6},{6,2},{3,7},{7,3},{8,12},{12,8},{9,1... | collective-permute-start | bytes 1966088 | tf_op jit(solution)/shard_map/ppermute | solution.py:447
  10.6 6.5 %collective-permute-start.1 = (bf16[36,16,128]{2,1,0:T(8,128)(2,1)S(1)}, bf16[36,16,128]{2,1,0:T(8,128)(2,1)S(1)}, u32[]{:S(2)}, u32[]{:S(2)}) collective-permute-start(bf16[36,16,128]{2,1,0:T(8,128)(2,1)S(1)} %get-tuple-element.12), channel_id=1, source_target_pairs={{4,8},{12,16},{20,24},{28,32},{36,40},{44,48},{52,56},{60,64},{68,... | collective-permute-start | bytes 442376 | tf_op jit(solution)/shard_map/ppermute | solution.py:446
  22.6 10.5 %collective-permute-start.2 = (bf16[76,16,128]{2,1,0:T(8,128)(2,1)S(1)}, bf16[76,16,128]{2,1,0:T(8,128)(2,1)S(1)}, u32[]{:S(2)}, u32[]{:S(2)}) collective-permute-start(bf16[76,16,128]{2,1,0:T(8,128)(2,1)S(1)} %shard_map.95.packet_ref), channel_id=1, source_target_pairs={{0,4},{4,0},{1,5},{5,1},{2,6},{6,2},{3,7},{7,3},{8,12},{12,8},{9,1... | collective-permute-start | bytes 933896 | tf_op jit(solution)/shard_map/ppermute | solution.py:467

commit v3 on v2

--- a/solution.py
+++ b/solution.py
@@ -97,8 +97,32 @@
     )
 
 
+def rim_kernel(in_any, cot_any, rim_ref, in_ref, cot_ref, sems):
+    odd = lax.axis_index("core")
+    copies = (
+        pltpu.make_async_copy(in_any.at[:, pl.ds(odd * 6, 2)], in_ref, sems.at[0]),
+        pltpu.make_async_copy(cot_any.at[:, pl.ds(odd * 13, 3)], cot_ref, sems.at[1]),
+    )
+    for copy in copies:
+        copy.start()
+    copies[0].wait()
+    for frame in range(6):
+        for row in range(2):
+            for half in range(2):
+                rim_ref[frame * 4 + row * 2 + half] = in_ref[
+                    frame, row, :, half * LAST : (half + 1) * LAST
+                ]
+    copies[1].wait()
+    for frame in range(2):
+        for row in range(3):
+            for half in range(2):
+                rim_ref[RIM_COT + frame * 6 + row * 2 + half] = cot_ref[
+                    frame, row, half * 16 : (half + 1) * 16, :
+                ]
+
+
 def pack_kernel(
-    clip_any, cols_any, start_any, in_any, cot_any, tile_ref, rim_ref, scales_ref,
+    clip_any, cols_any, start_any, in_any, cot_any, rim_any, tile_ref, scales_ref,
     clip_ref, cols_ref, start_ref, in_ref, cot_ref, sems,
 ):
     copies = [
@@ -119,7 +143,6 @@
         copy.wait()
     for row, value in enumerate(load_scales(clip_ref, cols_ref, start_ref)):
         scales_ref[row : row + 1] = jnp.full((1, LAST), value, F32)
-    odd = lax.axis_index("core")
     copies[3].wait()
     for frame in range(6):
         for row in range(8):
@@ -134,99 +157,51 @@
                 tile_ref[TILE_COT + frame * 32 + row * 2 + half] = cot_ref[
                     frame, row, half * 16 : (half + 1) * 16, :
                 ]
-    for frame in range(6):
-        rim_ref[frame * 4 : frame * 4 + 4] = tile_ref[pl.ds(frame * 16 + odd * 12, 4)]
-    for frame in range(2):
-        at = RIM_COT + frame * 6
-        rim_ref[at : at + 6] = tile_ref[pl.ds(TILE_COT + frame * 32 + odd * 26, 6)]
-
-
-def pair_sums(rows, first, pair, put):
-    zeros = jnp.zeros((pair.shape[0], 8, LAST), F32)
-    pair[:, 0:8] = zeros
-    pair[:, 40:48] = zeros
+
+
+def pair_sums(rows, pair, put):
     count = rows.shape[0] - 1
+    zeros = jnp.zeros((count, 8, LAST), F32)
+    pair[0:count, 0:8] = zeros
+    pair[0:count, 40:48] = zeros
     pair[0:count, 8:40] = rows[0:count] + rows[1 : count + 1]
     before, even, odd, after = (pair[0:count, pl.ds(begin, 16, 2), :] for begin in (7, 8, 9, 10))
     for kw, value in ((0, odd + after), (1, even + odd), (2, before + even)):
         put(kw, value.astype(BF))
 
 
-def first_kernel(
-    scales, tile_ref, sib_ref, rim_ref, w1_any, w2_any, packet_ref,
-    w1_ref, w2_ref, act, rows, pair, cots, sems,
-):
-    load_w1 = pltpu.make_async_copy(w1_any, w1_ref, sems.at[0])
-    load_w2 = pltpu.make_async_copy(w2_any, w2_ref, sems.at[1])
-    load_w1.start()
-    load_w2.start()
-    odd = lax.axis_index("core")
-    keep = twice(scale_of(scales, KEEP))
-    low = low_mask(scales, COLS)
-    wide_low = twice(low)
-    rim_scale, sib_scale = scale_of(scales, RIM_SCALE), scale_of(scales, SIB_SCALE)
-    rim_at = odd * 10
-    sib_at = 10 - odd * 10
-
-    for frame in range(6):
-        for at, count, read, mask in (
-            (rim_at, 2, lambda f: joined(rim_ref[f * 4 : f * 4 + 4]).astype(F32), wide_low * twice(rim_scale)),
-            (2, 8, lambda f: tile_rows(tile_ref, f), wide_low),
-            (sib_at, 2, lambda f: joined(sib_ref[pl.ds(f * 16 + odd * 12, 4)]).astype(F32), wide_low * twice(sib_scale)),
-        ):
-            values = eff_frame(read, frame, keep)
-            values = values * sigmoid(values) * mask
-            left, right = column_shifts(values)
-            act[0, frame, pl.ds(at, count)] = left.astype(BF)
-            act[1, frame, pl.ds(at, count)] = values.astype(BF)
-            act[2, frame, pl.ds(at, count)] = right.astype(BF)
-
-    high = high_mask(scales, COLS)
-    for frame in range(2):
-        at = TILE_COT + frame * 32
-        rows[frame, 3:19] = tile_ref[at : at + 32].reshape(16, 32, LAST).astype(F32) * high
-        raw = rim_ref[RIM_COT + frame * 6 : RIM_COT + frame * 6 + 6].reshape(3, 32, LAST)
-        rows[frame, pl.ds(odd * 19, 3)] = raw.astype(F32) * (high * rim_scale)
-        raw = sib_ref[pl.ds(at + odd * 26, 6)].reshape(3, 32, LAST)
-        rows[frame, pl.ds(19 - odd * 19, 3)] = raw.astype(F32) * (high * sib_scale)
-        far = rows[frame, pl.ds(2 + odd * 17, 1)].reshape(2, 16, LAST)
-        packet_ref[PACK_ROW + frame * 2 : PACK_ROW + frame * 2 + 2] = far.astype(BF)
-
-    load_w1.wait()
-    first_out = None
+def tap_sums(rows, first, begin, count, pair, cots):
+    def put(kw, sums):
+        for n in range(sums.shape[0]):
+            row = first + n
+            if row % 2 == 0:
+                targets = ((1, row // 2),)
+            else:
+                targets = ((0, (row - 1) // 2), (2, (row + 1) // 2))
+            for kh, place in targets:
+                if begin <= place < begin + count:
+                    tap = kh * 3 + kw
+                    cots[place - begin, :, tap * LAST : (tap + 1) * LAST] = sums[n]
+
+    pair_sums(rows, pair, put)
+
+
+def shifted_act(act, at, values):
+    left, right = column_shifts(values)
+    for kw, shifted in enumerate((left, values, right)):
+        act[(kw, *at)] = shifted.astype(BF)
+
+
+def first_conv(windows, w1_ref):
+    total = None
     for step in range(9):
-        kt, kh = step // 3, step % 3
-        window = jnp.concatenate(
-            [act[kw, kt : kt + 4, kh : kh + 10].reshape(640, 256) for kw in range(3)], 1
-        )
+        window = jnp.concatenate([windows(kw, step // 3, step % 3) for kw in range(3)], 1)
         term = dot(window, w1_ref[step * 3 : step * 3 + 3].reshape(768, LAST))
-        first_out = term if first_out is None else first_out + term
-    first_out = first_out.reshape(40, 16, LAST)
-    row = lax.broadcasted_iota(jnp.int32, (40, 1, 1), 0) % 10
-    row_scale = jnp.where(
-        row == 0, scale_of(scales, UP), jnp.where(row == 9, scale_of(scales, DOWN), 1.0)
-    )
-    gate = sigmoid(first_out)
-    second_in = (first_out * gate * low).astype(BF).reshape(4, 10, 16, LAST)
-    packet_ref[PACK_SECOND:PACK_ROW] = second_in[:, 1:9].reshape(32, 16, LAST)
-    slope = gate * (1.0 + first_out * (1.0 - gate)) * (low * row_scale)
-
-    for frame in range(2):
-
-        def put(kw, sums):
-            for n in range(21):
-                if n % 2 == 1:
-                    targets = ((1, n // 2),)
-                else:
-                    targets = ((0, n // 2 - 1), (2, n // 2))
-                for kh, place in targets:
-                    if 0 <= place < 10:
-                        tap = kh * 3 + kw
-                        cots[frame, place, :, tap * LAST : (tap + 1) * LAST] = sums[n]
-
-        pair_sums(rows[frame], -3, pair, put)
-
-    load_w2.wait()
+        total = term if total is None else total + term
+    return total
+
+
+def second_conv_back(cots, w2_ref, slope, put):
     flat = jnp.concatenate(
         [
             jnp.concatenate([w2_ref[kt * 9 + tap] for tap in range(9)], 1)
@@ -234,24 +209,142 @@
         ],
         0,
     )
-    spread = dot(cots[...].reshape(320, 1152), flat, NT)
+    spread = dot(cots, flat, NT)
+    cells = spread.shape[0] // 2
     for frame in range(4):
         total = None
         for kt in range(3):
             if 0 <= frame - kt < 2:
                 term = spread[
-                    (frame - kt) * 160 : (frame - kt + 1) * 160, kt * LAST : (kt + 1) * LAST
+                    (frame - kt) * cells : (frame - kt + 1) * cells, kt * LAST : (kt + 1) * LAST
                 ]
                 total = term if total is None else total + term
-        first_grad = total.reshape(10, 16, LAST) * slope[frame * 10 : frame * 10 + 10]
-        packet_ref[frame * 10 : frame * 10 + 10] = first_grad.astype(BF)
-
-
-def input_kernel(
-    scales, tile_ref, sib_ref, packet_ref, w1_any, grad_ref, act_ref, w1_ref, firsts, sems
+        put(frame, (total * slope[frame]).astype(BF))
+
+
+def inner_kernel(
+    scales, tile_ref, w1_any, w2_any, first_ref, second_ref, act_ref, w1_ref, w2_ref,
+    act, pair, cots, sems,
 ):
     load_w1 = pltpu.make_async_copy(w1_any, w1_ref, sems.at[0])
+    load_w2 = pltpu.make_async_copy(w2_any, w2_ref, sems.at[1])
     load_w1.start()
+    load_w2.start()
+    keep = twice(scale_of(scales, KEEP))
+    low = low_mask(scales, COLS)
+    for frame in range(6):
+        values = eff_frame(lambda f: tile_rows(tile_ref, f), frame, keep)
+        values = values * sigmoid(values) * twice(low)
+        shifted_act(act, (frame,), values)
+        act_ref[frame] = values.astype(BF)
+    load_w1.wait()
+    first_out = first_conv(
+        lambda kw, kt, kh: act[kw, kt : kt + 4, kh : kh + 6].reshape(384, 256), w1_ref
+    ).reshape(24, 16, LAST)
+    gate = sigmoid(first_out)
+    second_ref[...] = (first_out * gate * low).astype(BF).reshape(4, 6, 16, LAST)
+    slope = gate * (1.0 + first_out * (1.0 - gate)) * low
+    high = high_mask(scales, COLS)
+    for frame in range(2):
+        at = TILE_COT + frame * 32
+        rows = tile_ref[at + 2 : at + 30].reshape(14, 32, LAST).astype(F32) * high
+        tap_sums(rows, 1, 1, 6, pair, cots.at[frame])
+    load_w2.wait()
+
+    def put(frame, first_grad):
+        first_ref[frame] = first_grad.reshape(6, 16, LAST)
+
+    second_conv_back(cots[...].reshape(192, 1152), w2_ref, slope.reshape(4, 96, LAST), put)
+
+
+def edge_kernel(
+    scales, tile_ref, sib_ref, rim_ref, first_ref, second_ref, w1_ref, w2_ref, packet_ref,
+    act, rows, pair, cots,
+):
+    odd = lax.axis_index("core")
+    even = 1 - odd
+    keep = twice(scale_of(scales, KEEP))
+    low = low_mask(scales, COLS)
+    wide_low = twice(low)
+    rim_scale, sib_scale = scale_of(scales, RIM_SCALE), scale_of(scales, SIB_SCALE)
+    for frame in range(6):
+        for part, at, read, mask in (
+            (odd, odd * 2, lambda f: joined(rim_ref[f * 4 : f * 4 + 4]), wide_low * twice(rim_scale)),
+            (0, 2, lambda f: joined(tile_ref[f * 16 : f * 16 + 4]), wide_low),
+            (1, 0, lambda f: joined(tile_ref[f * 16 + 12 : f * 16 + 16]), wide_low),
+            (even, even * 2, lambda f: joined(sib_ref[pl.ds(f * 16 + odd * 12, 4)]), wide_low * twice(sib_scale)),
+        ):
+            values = eff_frame(lambda f, read=read: read(f).astype(F32), frame, keep)
+            shifted_act(act, (frame, part, pl.ds(at, 2)), values * sigmoid(values) * mask)
+    high = high_mask(scales, COLS)
+    for frame in range(2):
+        at = TILE_COT + frame * 32
+        own = tile_ref[at : at + 32].reshape(16, 32, LAST)
+        rows[frame, 0, 3:6] = own[0:3].astype(F32) * high
+        rows[frame, 1, 0:3] = own[13:16].astype(F32) * high
+        raw = rim_ref[RIM_COT + frame * 6 : RIM_COT + frame * 6 + 6].reshape(3, 32, LAST)
+        rows[frame, odd, pl.ds(odd * 3, 3)] = raw.astype(F32) * (high * rim_scale)
+        raw = sib_ref[pl.ds(at + odd * 26, 6)].reshape(3, 32, LAST)
+        rows[frame, even, pl.ds(even * 3, 3)] = raw.astype(F32) * (high * sib_scale)
+        far = rows[frame, odd, pl.ds(2 + odd, 1)].reshape(2, 16, LAST)
+        packet_ref[PACK_ROW + frame * 2 : PACK_ROW + frame * 2 + 2] = far.astype(BF)
+        tap_sums(rows[frame, 0], -3, -1, 2, pair, cots.at[frame, 0])
+        tap_sums(rows[frame, 1], 13, 7, 2, pair, cots.at[frame, 1])
+    first_out = first_conv(
+        lambda kw, kt, kh: act[kw, kt : kt + 4, :, kh : kh + 2].reshape(256, 256), w1_ref
+    ).reshape(16, 16, LAST)
+    row = lax.broadcasted_iota(jnp.int32, (16, 1, 1), 0) % 4
+    row_scale = jnp.where(
+        row == 0, scale_of(scales, UP), jnp.where(row == 3, scale_of(scales, DOWN), 1.0)
+    )
+    gate = sigmoid(first_out)
+    second_in = (first_out * gate * low).astype(BF)
+    slope = gate * (1.0 + first_out * (1.0 - gate)) * (low * row_scale)
+    for frame in range(4):
+        at = PACK_SECOND + frame * 8
+        packet_ref[at] = second_in[frame * 4 + 1]
+        packet_ref[at + 1 : at + 7] = second_ref[frame]
+        packet_ref[at + 7] = second_in[frame * 4 + 2]
+
+    def put(frame, first_grad):
+        blocks_now = first_grad.reshape(4, 16, LAST)
+        packet_ref[frame * 10 : frame * 10 + 2] = blocks_now[0:2]
+        packet_ref[frame * 10 + 2 : frame * 10 + 8] = first_ref[frame]
+        packet_ref[frame * 10 + 8 : frame * 10 + 10] = blocks_now[2:4]
+
+    second_conv_back(cots[...].reshape(128, 1152), w2_ref, slope.reshape(4, 64, LAST), put)
+
+
+def sibling_kernel(scales, tile_ref, sib_ref, act_ref, sums_ref, rows, pair):
+    keep = twice(scale_of(scales, SIB_KEEP))
+    low = twice(low_mask(scales, SIB_COLS))
+    for frame in range(6):
+        values = eff_frame(lambda f: tile_rows(sib_ref, f), frame, keep)
+        act_ref[frame] = (values * sigmoid(values) * low).astype(BF)
+    odd = lax.axis_index("core")
+    link = scale_of(scales, SIB_SCALE)
+    rows[...] = jnp.zeros((18, 32, LAST), F32)
+    for slot, tile, other, which in (
+        (0, tile_ref, sib_ref, COLS),
+        (1, sib_ref, tile_ref, SIB_COLS),
+    ):
+        lower = odd if slot == 0 else 1 - odd
+        high = high_mask(scales, which)
+        for frame in range(2):
+            at = TILE_COT + frame * 32
+            rows[1:17] = tile[at : at + 32].reshape(16, 32, LAST).astype(F32) * high
+            near = other[pl.ds(at + lower * 30, 2)].reshape(1, 32, LAST)
+            rows[pl.ds(17 - lower * 17, 1)] = near.astype(F32) * (high * link)
+
+            def put(kw, values):
+                for n in range(17):
+                    place = n // 2 if n % 2 == 0 else 9 + n // 2
+                    sums_ref[kw, slot, frame, place] = values[n]
+
+            pair_sums(rows[...], pair, put)
+
+
+def input_kernel(scales, tile_ref, packet_ref, w1_ref, grad_ref, firsts):
     for frame in range(4):
         first_grad = packet_ref[frame * 10 : frame * 10 + 10]
         before, after = column_shifts(first_grad.astype(F32))
@@ -259,7 +352,6 @@
             for kh in range(3):
                 tap = kh * 3 + kw
                 firsts[frame, :, :, tap * LAST : (tap + 1) * LAST] = value[2 - kh : 10 - kh]
-    load_w1.wait()
     shifted = firsts[...].reshape(512, 1152)
     by_depth = [
         dot(shifted, jnp.concatenate([w1_ref[kt * 9 + tap] for tap in range(9)], 1), NT)
@@ -276,7 +368,6 @@
                 total = term if total is None else total + term
         values = eff_frame(lambda f: tile_rows(tile_ref, f), frame, keep)
         gate = sigmoid(values)
-        act_ref[0, frame] = (values * gate * low).astype(BF)
         pre = total.reshape(8, 16, 256) * (gate * (1.0 + values * (1.0 - gate)) * low)
         if frame < 4:
             carried = pre if carried is None else carried + pre
@@ -285,40 +376,30 @@
             grad_ref[frame] = (pre + carried * (1.0 - keep)).astype(BF)
         else:
             grad_ref[frame] = pre.astype(BF)
-    keep = twice(scale_of(scales, SIB_KEEP))
-    low = twice(low_mask(scales, SIB_COLS))
-    for frame in range(6):
-        values = eff_frame(lambda f: tile_rows(sib_ref, f), frame, keep)
-        act_ref[1, frame] = (values * sigmoid(values) * low).astype(BF)
 
 
 def weight_kernel(
-    scales, tile_ref, sib_ref, packet_ref, sib_packet_ref, act_ref, part_ref, rows, pair, sums, cols
+    scales, tile_ref, sib_ref, packet_ref, sib_packet_ref, act_ref, sib_act_ref, sums_ref,
+    part_ref, pair, sums, cols,
 ):
     odd = lax.axis_index("core")
     reps = part_ref.shape[0]
-    link = scale_of(scales, SIB_SCALE)
-    for own, tile, other, packet, which in (
-        (True, tile_ref, sib_ref, packet_ref, COLS),
-        (False, sib_ref, tile_ref, sib_packet_ref, SIB_COLS),
+    sums[...] = sums_ref[...]
+    for slot, tile, packet, which in (
+        (0, tile_ref, packet_ref, COLS),
+        (1, sib_ref, sib_packet_ref, SIB_COLS),
     ):
-        slot = 0 if own else 1
-        lower = odd if own else 1 - odd
+        lower = odd if slot == 0 else 1 - odd
         high = high_mask(scales, which)
         for frame in range(2):
-            at = TILE_COT + frame * 32
-            rows[1:17] = tile[at : at + 32].reshape(16, 32, LAST).astype(F32) * high
             far = packet[PACK_ROW + frame * 2 : PACK_ROW + frame * 2 + 2].reshape(1, 32, LAST)
-            rows[pl.ds(lower * 17, 1)] = far.astype(F32)
-            near = other[pl.ds(at + lower * 30, 2)].reshape(1, 32, LAST)
-            rows[pl.ds(17 - lower * 17, 1)] = near.astype(F32) * (high * link)
+            last = tile[pl.ds(TILE_COT + frame * 32 + lower * 30, 2)].reshape(1, 32, LAST)
+            rows = jnp.concatenate([far.astype(F32), last.astype(F32) * high], 0)
 
             def put(kw, values):
-                for n in range(17):
-                    place = n // 2 if n % 2 == 0 else 9 + n // 2
-                    sums[kw, slot, frame, place] = values[n]
-
-            pair_sums(rows[...], -1, pair, put)
+                sums[kw, slot, frame, pl.ds(lower * 8, 1)] = values
+
+            pair_sums(rows, pair, put)
         for frame in range(4):
             first_grad = packet[frame * 10 : frame * 10 + 10]
             before, after = column_shifts(first_grad.astype(F32))
@@ -326,17 +407,16 @@
             cols[1, slot, frame] = first_grad
             cols[2, slot, frame] = before.astype(BF)
 
-    act_all = jnp.concatenate([act_ref[:, kt : kt + 4].reshape(1024, 256) for kt in range(3)], 1)
+    def both(refs, kt, frames):
+        return jnp.concatenate(
+            [ref[kt : kt + frames].reshape(frames * 128, ref.shape[3]) for ref in refs], 0
+        )
+
+    act_all = jnp.concatenate([both((act_ref, sib_act_ref), kt, 4) for kt in range(3)], 1)
     seconds = [
         ref[PACK_SECOND:PACK_ROW].reshape(4, 8, 16, LAST) for ref in (packet_ref, sib_packet_ref)
     ]
-    second_all = jnp.concatenate(
-        [
-            jnp.concatenate([part[kt : kt + 2].reshape(256, LAST) for part in seconds], 0)
-            for kt in range(3)
-        ],
-        1,
-    )
+    second_all = jnp.concatenate([both(seconds, kt, 2) for kt in range(3)], 1)
 
     def put_block(block, at):
         part_ref[:, at] = block.astype(BF).reshape(reps, LAST // reps, LAST)
@@ -391,6 +471,7 @@
 
 VMEM = pl.BlockSpec(memory_space=pltpu.VMEM)
 HBM = pl.BlockSpec(memory_space=pltpu.HBM)
+ANY = pl.BlockSpec(memory_space=pl.ANY)
 
 
 def params(mebibytes):
@@ -424,11 +505,29 @@
             second_weight.reshape(27, LAST, LAST),
         )
     )
-    tile, rim, scales = pl.pallas_call(
+    swap = [(0, 1), (1, 0)]
+    across = [(i, (i + 1) % tiles) for i in range(1, tiles, 2)]
+    across += [(b, a) for a, b in across]
+    own_rim = pl.pallas_call(
+        rim_kernel,
+        out_shape=blocks(RIM_BLOCKS),
+        in_specs=[HBM] * 2,
+        out_specs=VMEM,
+        scratch_shapes=[
+            pltpu.VMEM((6, 2, 16, 256), BF),
+            pltpu.VMEM((2, 3, 32, LAST), BF),
+            pltpu.SemaphoreType.DMA((2,)),
+        ],
+        compiler_params=params(4),
+        cost_estimate=cost(10**5, 3 * 10**5),
+    )(local_in, local_cot)
+    rim = lax.ppermute(own_rim, TILE_AXES, across)
+
+    tile, scales = pl.pallas_call(
         pack_kernel,
-        out_shape=(blocks(TILE_BLOCKS), blocks(RIM_BLOCKS), jax.ShapeDtypeStruct((8, LAST), F32)),
-        in_specs=[HBM] * 5,
-        out_specs=(VMEM, VMEM, VMEM),
+        out_shape=(blocks(TILE_BLOCKS), jax.ShapeDtypeStruct((8, LAST), F32)),
+        in_specs=[HBM] * 5 + [ANY],
+        out_specs=(VMEM, VMEM),
         scratch_shapes=[
             pltpu.SMEM(tile_clip.shape, jnp.int32),
             pltpu.SMEM(clip_cols.shape, jnp.int32),
@@ -438,66 +537,87 @@
             pltpu.SemaphoreType.DMA((5,)),
         ],
         compiler_params=params(8),
-    )(tile_clip, clip_cols, clip_start, local_in, local_cot)
-
-    swap = [(0, 1), (1, 0)]
-    across = [(i, (i + 1) % tiles) for i in range(1, tiles, 2)]
-    across += [(b, a) for a, b in across]
-    rim = lax.ppermute(rim, TILE_AXES, across)
+        cost_estimate=cost(10**6, 2 * 10**6),
+    )(tile_clip, clip_cols, clip_start, local_in, local_cot, own_rim)
     sibling = lax.ppermute(tile, "core", swap)
 
+    inner_first, inner_second, act, w1, w2 = pl.pallas_call(
+        inner_kernel,
+        out_shape=(
+            jax.ShapeDtypeStruct((4, 6, 16, LAST), BF),
+            jax.ShapeDtypeStruct((4, 6, 16, LAST), BF),
+            jax.ShapeDtypeStruct((6, 8, 16, 256), BF),
+            jax.ShapeDtypeStruct(w1.shape, BF),
+            jax.ShapeDtypeStruct(w2.shape, BF),
+        ),
+        in_specs=[VMEM] * 2 + [HBM] * 2,
+        out_specs=(VMEM,) * 5,
+        scratch_shapes=[
+            pltpu.VMEM((3, 6, 8, 16, 256), BF),
+            pltpu.VMEM((13, 48, LAST), F32),
+            pltpu.VMEM((2, 6, 16, 9 * LAST), BF),
+            pltpu.SemaphoreType.DMA((2,)),
+        ],
+        compiler_params=params(24),
+        cost_estimate=cost(2 * 10**9, 4 * 10**6),
+    )(scales, tile, w1, w2)
+
+    sib_act, sums = pl.pallas_call(
+        sibling_kernel,
+        out_shape=(
+            jax.ShapeDtypeStruct((6, 8, 16, 256), BF),
+            jax.ShapeDtypeStruct((3, 2, 2, 17, 16, LAST), BF),
+        ),
+        in_specs=[VMEM] * 3,
+        out_specs=(VMEM, VMEM),
+        scratch_shapes=[
+            pltpu.VMEM((18, 32, LAST), F32),
+            pltpu.VMEM((17, 48, LAST), F32),
+        ],
+        compiler_params=params(16),
+        cost_estimate=cost(10**9, 2 * 10**6),
+    )(scales, tile, sibling)
+
     packet = pl.pallas_call(
-        first_kernel,
+        edge_kernel,
         out_shape=blocks(PACK_BLOCKS),
-        in_specs=[VMEM] * 4 + [HBM] * 2,
+        in_specs=[VMEM] * 8,
         out_specs=VMEM,
         scratch_shapes=[
-            pltpu.VMEM((27, 256, LAST), BF),
-            pltpu.VMEM((27, LAST, LAST), BF),
-            pltpu.VMEM((3, 6, 12, 16, 256), BF),
-            pltpu.VMEM((2, 22, 32, LAST), F32),
-            pltpu.VMEM((21, 48, LAST), F32),
-            pltpu.VMEM((2, 10, 16, 9 * LAST), BF),
-            pltpu.SemaphoreType.DMA((2,)),
+            pltpu.VMEM((3, 6, 2, 4, 16, 256), BF),
+            pltpu.VMEM((2, 2, 6, 32, LAST), F32),
+            pltpu.VMEM((5, 48, LAST), F32),
+            pltpu.VMEM((2, 2, 2, 16, 9 * LAST), BF),
         ],
-        compiler_params=params(32),
+        compiler_params=params(16),
+        cost_estimate=cost(10**9, 4 * 10**6),
+    )(scales, tile, sibling, rim, inner_first, inner_second, w1, w2)
+    sib_packet = lax.ppermute(packet, "core", swap)
+
+    input_grad = pl.pallas_call(
+        input_kernel,
+        out_shape=jax.ShapeDtypeStruct(local_in.shape, BF),
+        in_specs=[VMEM] * 4,
+        out_specs=VMEM,
+        scratch_shapes=[pltpu.VMEM((4, 8, 16, 9 * LAST), BF)],
+        compiler_params=params(24),
         cost_estimate=cost(2 * 10**9, 4 * 10**6),
-    )(scales, tile, sibling, rim, w1, w2)
-
-    sib_packet = lax.ppermute(packet, "core", swap)
-
-    input_grad, act = pl.pallas_call(
-        input_kernel,
-        out_shape=(
-            jax.ShapeDtypeStruct(local_in.shape, BF),
-            jax.ShapeDtypeStruct((2, 6, 8, 16, 256), BF),
-        ),
-        in_specs=[VMEM] * 4 + [HBM],
-        out_specs=(VMEM, VMEM),
-        scratch_shapes=[
-            pltpu.VMEM((27, 256, LAST), BF),
-            pltpu.VMEM((4, 8, 16, 9 * LAST), BF),
-            pltpu.SemaphoreType.DMA((1,)),
-        ],
-        compiler_params=params(32),
-        cost_estimate=cost(2 * 10**9, 4 * 10**6),
-    )(scales, tile, sibling, packet, w1)
+    )(scales, tile, packet, w1)
 
     depth = LAST // reps
     parts = pl.pallas_call(
         weight_kernel,
         out_shape=jax.ShapeDtypeStruct((reps, GRAD_BLOCKS, depth, LAST), BF),
-        in_specs=[VMEM] * 6,
+        in_specs=[VMEM] * 8,
         out_specs=VMEM,
         scratch_shapes=[
-            pltpu.VMEM((18, 32, LAST), F32),
-            pltpu.VMEM((17, 48, LAST), F32),
+            pltpu.VMEM((1, 48, LAST), F32),
             pltpu.VMEM((3, 2, 2, 17, 16, LAST), BF),
             pltpu.VMEM((3, 2, 4, 10, 16, LAST), BF),
         ],
-        compiler_params=params(32),
+        compiler_params=params(24),
         cost_estimate=cost(2 * 10**9, 4 * 10**6),
-    )(scales, tile, sibling, packet, sib_packet, act)
+    )(scales, tile, sibling, packet, sib_packet, act, sib_act, sums)
 
     count = GRAD_BLOCKS * depth
     parts = parts.reshape(reps, count, LAST)

time: 107 us -> 105 us (0.981)
  blocking collectives: 69.6 us -> 48.8 us
  starting transfers between devices: 17.6 us -> 26.3 us
  waiting for transfers between devices: 4.54 us -> 12.6 us
  other arithmetic: 0.47 us -> 1.78 us
    all_to_all x1 -> x0, blocking collectives: 20.2 us -> none  [body(): half = lax.all_to_all(own, PLANE_AXES, 0, 0, tiled=True)]
    all_to_all x0 -> x1, waiting for transfers between devices: none -> 11.7 us  [body(): half = lax.all_to_all(own, PLANE_AXES, 0, 0, tiled=True)]
    all_to_all x0 -> x1, starting transfers between devices: none -> 7.38 us  [body(): half = lax.all_to_all(own, PLANE_AXES, 0, 0, tiled=True)]
    ppermute x1, waiting for transfers between devices: 4.53 us -> 0.35 us  [body(): rim = lax.ppermute(own_rim, TILE_AXES, across)]
    ppermute x1, starting transfers between devices: 6.86 us -> 8.24 us  [body(): sib_packet = lax.ppermute(packet, 'core', swap)]
    reduce_sum x2, other arithmetic: 0.47 us -> 1.78 us  [wide_sum(): return jnp.sum(parts.astype(F32), axis=0).astype(BF)]
    pallas_call x3 -> x6, Pallas kernels: 10.3 us -> 10.7 us  [the longest x1 4.17 us: body(): pl.pallas_call(inner_kernel, out_shape=(jax.ShapeDtypeStruct((4, 6, 16, L...]
  transfers between devices with their start and end apart: 3 -> 4, of which waited for: 1 -> 3; matrix products, arithmetic and copies ran while one was open for 0% -> 0% of each run, Pallas kernels for 3% -> 7%
where the time goes in v3:
time: 105 us
  blocking collectives  48.8 us (46%)
  starting transfers between devices  26.3 us (25%)
  Pallas kernels  13.7 us (13%)
  waiting for transfers between devices  12.6 us (12%)
  other arithmetic  1.78 us (2%)
    all_to_all x1, blocking collectives, body(): of_rep = wide_sum(lax.all_to_all(parts, 'x', 0, 0, tiled=True))  21.8 us
    all_to_all x1, blocking collectives, body(): own = wide_sum(lax.all_to_all(of_rep, PLANE_AXES, 0, 0, tiled=True))  20.8 us
    all_to_all x1, waiting for transfers between devices, body(): half = lax.all_to_all(own, PLANE_AXES, 0, 0, tiled=True)  11.7 us
    ppermute x1, starting transfers between devices, body(): sibling = lax.ppermute(tile, 'core', swap)  8.79 us
    ppermute x1, starting transfers between devices, body(): sib_packet = lax.ppermute(packet, 'core', swap)  8.24 us
    all_to_all x1, starting transfers between devices, body(): half = lax.all_to_all(own, PLANE_AXES, 0, 0, tiled=True)  7.38 us
    all_gather x1, blocking collectives, body(): lax.all_gather(half, 'core', axis=0).reshape(2, GRAD_BLOCKS, depth, LAST)  6.21 us
    pallas_call x1, Pallas kernels, body(): pl.pallas_call(inner_kernel, out_shape=(jax.ShapeDtypeStruct((4, 6, 16, L...  4.17 us
  transfers between devices with their start and end apart: 4, of which 3 were waited for; matrix products, arithmetic and copies ran while one was open for 0% of the time, Pallas kernels for 7%

profile of v3, /device:TPU:1, one launch (start us, length us, event | category | flops | bytes accessed | tf_op | source)
XLA Modules:
  0.0 104.8 jit_solution(3227504232033880706)
XLA Ops:
  0.6 0.9 shard_map.94.rim_any
  1.6 1.1 %shard_map.95 = (bf16[160,16,128]{2,1,0:T(8,128)(2,1)S(1)}, f32[8,128]{1,0:T(8,128)S(1)}) custom-call(s32[1,128]{1,0:T(1,128)} %clip_any.1, s32[1,8]{1,0:T(1,128)} %cols_any.1, s32[1,8]{1,0:T(1,128)} %start_any.1, bf16[6,8,16,256]{3,2,1,0:T(8,128)(2,1)} %bitcast.19, bf16[2,16,32,128]{3,2,1,0:T(8,128)(2,1)} %bitcast.22, ...), custom_call_target="tpu_custom_call" | custom-call | flops 1000000 | bytes 2000000 | tf_op jit(solution)/shard_map/pallas_call | solution.py:526
  2.7 8.8 %collective-permute-start = (bf16[160,16,128]{2,1,0:T(8,128)(2,1)S(1)}, bf16[160,16,128]{2,1,0:T(8,128)(2,1)S(1)}, u32[]{:S(2)}, u32[]{:S(2)}) collective-permute-start(bf16[160,16,128]{2,1,0:T(8,128)(2,1)S(1)} %get-tuple-element.15.tile_ref), channel_id=1, source_target_pairs={{0,4},{4,0},{1,5},{5,1},{2,6},{6,2},{3,7},{7,3},{8,12},{12,8},{9,1... | collective-permute-start | bytes 1966088 | tf_op jit(solution)/shard_map/ppermute | solution.py:542
  11.5 1.9 %collective-permute-start.1 = (bf16[36,16,128]{2,1,0:T(8,128)(2,1)S(1)}, bf16[36,16,128]{2,1,0:T(8,128)(2,1)S(1)}, u32[]{:S(2)}, u32[]{:S(2)}) collective-permute-start(bf16[36,16,128]{2,1,0:T(8,128)(2,1)S(1)} %shard_map.94.rim_any), channel_id=1, source_target_pairs={{4,8},{12,16},{20,24},{28,32},{36,40},{44,48},{52,56},{60,64},{68,... | collective-permute-start | bytes 442376 | tf_op jit(solution)/shard_map/ppermute | solution.py:524
  13.4 4.2 %shard_map.96 = (bf16[4,6,16,128]{3,2,1,0:T(8,128)(2,1)S(1)}, bf16[4,6,16,128]{3,2,1,0:T(8,128)(2,1)S(1)}, bf16[6,8,16,256]{3,2,1,0:T(8,128)(2,1)S(1)}, bf16[27,...) custom-call(f32[8,128]{1,0:T(8,128)S(1)} %get-tuple-element.14.scales, ...), custom_call_target="tpu_custom_call" | custom-call | flops 2000000000 | bytes 4000000 | tf_op jit(solution)/shard_map/pallas_call | solution.py:544
  17.6 0.4 collective-permute-done.1.rim_ref
  18.0 0.0 collective-permute-done.sib_ref
  18.0 1.8 %shard_map.97.packet_ref = bf16[76,16,128]{2,1,0:T(8,128)(2,1)S(1)} custom-call(f32[8,128]{1,0:T(8,128)S(1)} %get-tuple-element.14.scales, bf16[160,16,128]{2,1,0:T(8,128)(2,1)S(1)} %get-tuple-element.15.tile_ref, bf16[160,16,128]{2,1,0:T(8,128)(2,1)S(1)} %collective-permute-done.sib_ref, bf16[36,16,128]{2,1,0:T(8,128)(2,1)S(1)} %collective-permute-done.1.rim_ref, ...), custom_call_target="tpu_custom_call" | custom-call | flops 1000000000 | bytes 4000000 | tf_op jit(solution)/shard_map/pallas_call | solution.py:581
  19.7 8.2 %collective-permute-start.2 = (bf16[76,16,128]{2,1,0:T(8,128)(2,1)S(1)}, bf16[76,16,128]{2,1,0:T(8,128)(2,1)S(1)}, u32[]{:S(2)}, u32[]{:S(2)}) collective-permute-start(bf16[76,16,128]{2,1,0:T(8,128)(2,1)S(1)} %shard_map.97.packet_ref), channel_id=1, source_target_pairs={{0,4},{4,0},{1,5},{5,1},{2,6},{6,2},{3,7},{7,3},{8,12},{12,8},{9,1... | collective-permute-start | bytes 933896 | tf_op jit(solution)/shard_map/ppermute | solution.py:595
  28.0 0.6 shard_map.99
  28.6 0.6 collective-permute-done.2.sib_packet_ref
  29.2 1.8 %shard_map.100 = bf16[4,42,32,128]{3,2,1,0:T(8,128)(2,1)S(1)} custom-call(f32[8,128]{1,0:T(8,128)S(1)} %get-tuple-element.14.scales, bf16[160,16,128]{2,1,0:T(8,128)(2,1)S(1)} %get-tuple-element.15.tile_ref, bf16[160,16,128]{2,1,0:T(8,128)(2,1)S(1)} %collective-permute-done.sib_ref, bf16[76,16,128]{2,1,0:T(8,128)(2,1)S(1)} %shard_map.97.packet_ref, ...), custom_call_target="tpu_custom_call" | custom-call | flops 2000000000 | bytes 4000000 | tf_op jit(solution)/shard_map/pallas_call | solution.py:608
  31.0 21.8 %all_to_all.15 = bf16[4,1344,128]{2,1,0:T(8,128)(2,1)} all-to-all(bf16[4,1344,128]{2,1,0:T(8,128)(2,1)S(1)} %bitcast.16), channel_id=1, replica_groups=mesh['y'=8,'z'=8,'core'=2,'x'=4] {'x'}, dimensions={0} | all-to-all | bytes 2752512 | tf_op jit(solution)/shard_map/all_to_all | solution.py:624
  52.8 1.7 %reduce_sum.24 = bf16[1344,128]{1,0:T(8,128)(2,1)S(1)} reduce(bf16[4,1344,128]{2,1,0:T(8,128)(2,1)} %all_to_all.15, bf16[]{:T(256)} %constant.5.clone.1), dimensions={0}, to_apply=%region_0.0 | reduce | flops 516096 | bytes 1720322 | tf_op jit(solution)/shard_map/reduce_sum | solution.py:486
  54.6 20.8 %all_to_all.16 = bf16[64,24,128]{2,1,0:T(8,128)(2,1)S(1)} all-to-all(bf16[64,24,128]{2,1,0:T(8,128)(2,1)S(1)} %bitcast.17), channel_id=1, replica_groups=mesh['y'=8,'z'=8,'core'=2,'x'=4] {'y','z'}, dimensions={0} | all-to-all | bytes 786432 | tf_op jit(solution)/shard_map/all_to_all | solution.py:627
  75.4 0.1 reduce_sum.25
  75.5 0.8 broadcast_in_dim.10
  76.3 7.4 %all-to-all-start.2 = ((bf16[64,24,128]{2,1,0:T(8,128)(2,1)}), bf16[64,24,128]{2,1,0:T(8,128)(2,1)S(1)}, u32[]{:S(2)}, u32[]{:S(2)}) async-start(bf16[64,24,128]{2,1,0:T(8,128)(2,1)} %broadcast_in_dim.10), calls=%async_computation.2 | async-start | bytes 786432 | tf_op jit(solution)/shard_map/all_to_all | solution.py:629
  83.7 2.1 %shard_map.98 = bf16[6,8,16,256]{3,2,1,0:T(8,128)(2,1)} custom-call(f32[8,128]{1,0:T(8,128)S(1)} %get-tuple-element.14.scales, bf16[160,16,128]{2,1,0:T(8,128)(2,1)S(1)} %get-tuple-element.15.tile_ref, bf16[76,16,128]{2,1,0:T(8,128)(2,1)S(1)} %shard_map.97.packet_ref, bf16[27,256,128]{2,1,0:T(8,128)(2,1)S(1)} %get-tuple-element.18.w1_ref), custom_call_target="tpu_custom_call" | custom-call | flops 2000000000 | bytes 4000000 | tf_op jit(solution)/shard_map/pallas_call | solution.py:597
  85.8 11.7 %all-to-all-done.2 = bf16[64,24,128]{2,1,0:T(8,128)(2,1)S(1)} async-done(((bf16[64,24,128]{2,1,0:T(8,128)(2,1)}), bf16[64,24,128]{2,1,0:T(8,128)(2,1)S(1)}, u32[]{:S(2)}, u32[]{:S(2)}) %all-to-all-start.2) | async-done | bytes 393248 | tf_op jit(solution)/shard_map/all_to_all | solution.py:629
  97.5 6.2 %all_gather.7 = bf16[2,1344,128]{2,1,0:T(8,128)(2,1)S(1)} all-gather(bf16[1,1344,128]{2,1,0:T(8,128)(2,1)S(1)} %bitcast.20), channel_id=1, replica_groups=mesh['y'=8,'z'=8,'core'=2,'x'=4] {'core'}, dimensions={0}, use_global_device_ids=true | all-gather | bytes 1032192 | tf_op jit(solution)/shard_map/all_gather | solution.py:631
  103.7 1.1 %shard_map.101 = (f32[27,32,256]{2,1,0:T(8,128)}, f32[27,32,128]{2,1,0:T(8,128)}) custom-call(bf16[2,42,32,128]{3,2,1,0:T(8,128)(2,1)S(1)} %bitcast.15), custom_call_target="tpu_custom_call" | custom-call | tf_op jit(solution)/shard_map/pallas_call | solution.py:635
  (2 shorter events, 0.1 us)
Async XLA Ops:
  2.7 15.3 %collective-permute-start = (bf16[160,16,128]{2,1,0:T(8,128)(2,1)S(1)}, bf16[160,16,128]{2,1,0:T(8,128)(2,1)S(1)}, u32[]{:S(2)}, u32[]{:S(2)}) collective-permute-start(bf16[160,16,128]{2,1,0:T(8,128)(2,1)S(1)} %get-tuple-element.15.tile_ref), channel_id=1, source_target_pairs={{0,4},{4,0},{1,5},{5,1},{2,6},{6,2},{3,7},{7,3},{8,12},{12,8},{9,1... | collective-permute-start | bytes 1966088 | tf_op jit(solution)/shard_map/ppermute | solution.py:542
  11.5 6.5 %collective-permute-start.1 = (bf16[36,16,128]{2,1,0:T(8,128)(2,1)S(1)}, bf16[36,16,128]{2,1,0:T(8,128)(2,1)S(1)}, u32[]{:S(2)}, u32[]{:S(2)}) collective-permute-start(bf16[36,16,128]{2,1,0:T(8,128)(2,1)S(1)} %shard_map.94.rim_any), channel_id=1, source_target_pairs={{4,8},{12,16},{20,24},{28,32},{36,40},{44,48},{52,56},{60,64},{68,... | collective-permute-start | bytes 442376 | tf_op jit(solution)/shard_map/ppermute | solution.py:524
  19.7 9.5 %collective-permute-start.2 = (bf16[76,16,128]{2,1,0:T(8,128)(2,1)S(1)}, bf16[76,16,128]{2,1,0:T(8,128)(2,1)S(1)}, u32[]{:S(2)}, u32[]{:S(2)}) collective-permute-start(bf16[76,16,128]{2,1,0:T(8,128)(2,1)S(1)} %shard_map.97.packet_ref), channel_id=1, source_target_pairs={{0,4},{4,0},{1,5},{5,1},{2,6},{6,2},{3,7},{7,3},{8,12},{12,8},{9,1... | collective-permute-start | bytes 933896 | tf_op jit(solution)/shard_map/ppermute | solution.py:595
  76.3 21.2 %all-to-all-start.2 = ((bf16[64,24,128]{2,1,0:T(8,128)(2,1)}), bf16[64,24,128]{2,1,0:T(8,128)(2,1)S(1)}, u32[]{:S(2)}, u32[]{:S(2)}) async-start(bf16[64,24,128]{2,1,0:T(8,128)(2,1)} %broadcast_in_dim.10), calls=%async_computation.2 | async-start | bytes 786432 | tf_op jit(solution)/shard_map/all_to_all | solution.py:629

commit v4 on v3

--- a/solution.py
+++ b/solution.py
@@ -8,8 +8,10 @@
 from jax.sharding import Mesh
 from jax.sharding import PartitionSpec as P
 
-TILE_AXES = ("y", "z", "core")
-PLANE_AXES = ("y", "z")
+TILE_AXES = ("yh", "yl", "zh", "zl", "core")
+NEAR_AXES = ("yl", "x", "zl")
+FAR_AXES = ("zh", "yh")
+PLANE_AXES = ("yl", "zl", "zh", "yh")
 BF = jnp.bfloat16
 F32 = jnp.float32
 NT = (((1,), (1,)), ((), ()))
@@ -258,7 +260,7 @@
 
 
 def edge_kernel(
-    scales, tile_ref, sib_ref, rim_ref, first_ref, second_ref, w1_ref, w2_ref, packet_ref,
+    rim_ref, scales, tile_ref, sib_ref, first_ref, second_ref, w1_ref, w2_ref, packet_ref,
     act, rows, pair, cots,
 ):
     odd = lax.axis_index("core")
@@ -344,7 +346,11 @@
             pair_sums(rows[...], pair, put)
 
 
-def input_kernel(scales, tile_ref, packet_ref, w1_ref, grad_ref, firsts):
+def input_kernel(scales, in_any, packet_ref, w1_any, grad_ref, in_ref, w1_ref, firsts, sems):
+    load_in = pltpu.make_async_copy(in_any, in_ref, sems.at[0])
+    load_w1 = pltpu.make_async_copy(w1_any, w1_ref, sems.at[1])
+    load_w1.start()
+    load_in.start()
     for frame in range(4):
         first_grad = packet_ref[frame * 10 : frame * 10 + 10]
         before, after = column_shifts(first_grad.astype(F32))
@@ -352,6 +358,8 @@
             for kh in range(3):
                 tap = kh * 3 + kw
                 firsts[frame, :, :, tap * LAST : (tap + 1) * LAST] = value[2 - kh : 10 - kh]
+    load_w1.wait()
+    load_in.wait()
     shifted = firsts[...].reshape(512, 1152)
     by_depth = [
         dot(shifted, jnp.concatenate([w1_ref[kt * 9 + tap] for tap in range(9)], 1), NT)
@@ -366,7 +374,7 @@
             if 0 <= frame - kt < 4:
                 term = by_depth[kt][(frame - kt) * 128 : (frame - kt + 1) * 128]
                 total = term if total is None else total + term
-        values = eff_frame(lambda f: tile_rows(tile_ref, f), frame, keep)
+        values = eff_frame(lambda f: in_ref[f].astype(F32), frame, keep)
         gate = sigmoid(values)
         pre = total.reshape(8, 16, 256) * (gate * (1.0 + values * (1.0 - gate)) * low)
         if frame < 4:
@@ -383,7 +391,7 @@
     part_ref, pair, sums, cols,
 ):
     odd = lax.axis_index("core")
-    reps = part_ref.shape[0]
+    near_y, reps, near_z, per_quarter, depth = part_ref.shape[:5]
     sums[...] = sums_ref[...]
     for slot, tile, packet, which in (
         (0, tile_ref, packet_ref, COLS),
@@ -419,7 +427,10 @@
     second_all = jnp.concatenate([both(seconds, kt, 2) for kt in range(3)], 1)
 
     def put_block(block, at):
-        part_ref[:, at] = block.astype(BF).reshape(reps, LAST // reps, LAST)
+        halves = block.astype(BF).reshape(reps, 2, depth, LAST)
+        for half in range(2):
+            quarter, place = divmod(at * 2 + half, per_quarter)
+            part_ref[quarter // near_z, :, quarter % near_z, place] = halves[:, half]
 
     def first_taps(step, at):
         tap = 5 * odd + step
@@ -448,25 +459,48 @@
     @pl.when(odd == 1)
     def _():
         second_taps(4, EXTRA_AT)
-        part_ref[:, EXTRA_AT + 3 : EXTRA_AT + 6] = jnp.zeros((reps, 3, LAST // reps, LAST), BF)
-
-
-def finish_kernel(scale, whole_ref, first_ref, second_ref):
+        for at in range(EXTRA_AT + 3, EXTRA_AT + 6):
+            put_block(jnp.zeros((LAST, LAST), F32), at)
+
+
+def near_sum_kernel(parts_ref, scales, sum_ref, token_ref):
+    token_ref[...] = scales[...]
+    rows = parts_ref.shape[1]
+    total = parts_ref[0].astype(F32)
+    for n in range(1, parts_ref.shape[0]):
+        total = total + parts_ref[n].astype(F32)
+    sum_ref[0:rows] = total.astype(BF)
+    if sum_ref.shape[0] > rows:
+        sum_ref[rows:] = jnp.zeros((sum_ref.shape[0] - rows, LAST), BF)
+
+
+def far_sum_kernel(parts_ref, _, copies_ref):
+    total = parts_ref[0].astype(F32)
+    for n in range(1, parts_ref.shape[0]):
+        total = total + parts_ref[n].astype(F32)
+    copies_ref[...] = jnp.broadcast_to(total.astype(BF)[None], copies_ref.shape)
+
+
+def finish_kernel(scale, per_quarter, whole_ref, first_ref, second_ref):
+    depth = first_ref.shape[1] // 2
     for core in range(2):
 
-        def block(at):
-            return whole_ref[core, at].astype(F32) * scale
+        def put(target, tap, columns, at):
+            for half in range(2):
+                quarter, place = divmod(at * 2 + half, per_quarter)
+                rows = whole_ref[core, quarter, place * depth : (place + 1) * depth]
+                target[tap, half * depth : (half + 1) * depth, columns] = rows.astype(F32) * scale
 
         for step in range(5 - core):
             for kt in range(3):
                 for half in range(2):
                     at = (step * 6 if step < 4 else EXTRA_AT) + kt * 2 + half
-                    tap = kt * 9 + 5 * core + step
-                    first_ref[tap, :, half * LAST : (half + 1) * LAST] = block(at)
+                    columns = slice(half * LAST, (half + 1) * LAST)
+                    put(first_ref, kt * 9 + 5 * core + step, columns, at)
         for step in range(4 + core):
             for kt in range(3):
                 at = (SECOND_AT + step * 3 if step < 4 else EXTRA_AT) + kt
-                second_ref[kt * 9 + 4 * core + step] = block(at)
+                put(second_ref, kt * 9 + 4 * core + step, slice(0, LAST), at)
 
 
 VMEM = pl.BlockSpec(memory_space=pltpu.VMEM)
@@ -492,7 +526,8 @@
 
 def body(inputs, cotangent, first_weight, second_weight, tile_clip, clip_cols, clip_start):
     tiles = lax.axis_size(TILE_AXES)
-    reps, plane = lax.axis_size("x"), lax.axis_size(PLANE_AXES)
+    reps, near_y, near_z = (lax.axis_size(name) for name in ("x", "yl", "zl"))
+    far, plane = lax.axis_size(FAR_AXES), lax.axis_size(PLANE_AXES)
     local_in, local_cot, tile_clip, clip_cols, clip_start, w1, w2 = (
         pltpu.with_memory_space_constraint(array, pltpu.HBM)
         for array in (
@@ -541,7 +576,7 @@
     )(tile_clip, clip_cols, clip_start, local_in, local_cot, own_rim)
     sibling = lax.ppermute(tile, "core", swap)
 
-    inner_first, inner_second, act, w1, w2 = pl.pallas_call(
+    inner_first, inner_second, act, inner_w1, inner_w2 = pl.pallas_call(
         inner_kernel,
         out_shape=(
             jax.ShapeDtypeStruct((4, 6, 16, LAST), BF),
@@ -591,23 +626,17 @@
         ],
         compiler_params=params(16),
         cost_estimate=cost(10**9, 4 * 10**6),
-    )(scales, tile, sibling, rim, inner_first, inner_second, w1, w2)
+    )(rim, scales, tile, sibling, inner_first, inner_second, inner_w1, inner_w2)
     sib_packet = lax.ppermute(packet, "core", swap)
 
-    input_grad = pl.pallas_call(
-        input_kernel,
-        out_shape=jax.ShapeDtypeStruct(local_in.shape, BF),
-        in_specs=[VMEM] * 4,
-        out_specs=VMEM,
-        scratch_shapes=[pltpu.VMEM((4, 8, 16, 9 * LAST), BF)],
-        compiler_params=params(24),
-        cost_estimate=cost(2 * 10**9, 4 * 10**6),
-    )(scales, tile, packet, w1)
-
     depth = LAST // reps
+    quarters = near_y * near_z
+    per_quarter = 2 * GRAD_BLOCKS // quarters
     parts = pl.pallas_call(
         weight_kernel,
-        out_shape=jax.ShapeDtypeStruct((reps, GRAD_BLOCKS, depth, LAST), BF),
+        out_shape=jax.ShapeDtypeStruct(
+            (near_y, reps, near_z, per_quarter, depth // 2, LAST), BF
+        ),
         in_specs=[VMEM] * 8,
         out_specs=VMEM,
         scratch_shapes=[
@@ -619,21 +648,54 @@
         cost_estimate=cost(2 * 10**9, 4 * 10**6),
     )(scales, tile, sibling, packet, sib_packet, act, sib_act, sums)
 
-    count = GRAD_BLOCKS * depth
-    parts = parts.reshape(reps, count, LAST)
-    of_rep = wide_sum(lax.all_to_all(parts, "x", 0, 0, tiled=True))
-    share = -(-count // plane // 8) * 8
-    of_rep = jnp.pad(of_rep, ((0, share * plane - count), (0, 0))).reshape(plane, share, LAST)
-    own = wide_sum(lax.all_to_all(of_rep, PLANE_AXES, 0, 0, tiled=True))
-    own = jnp.broadcast_to(own[None], (plane, share, LAST))
-    half = lax.all_to_all(own, PLANE_AXES, 0, 0, tiled=True)
-    half = half.reshape(plane * share, LAST)[:count]
-    whole = lax.all_gather(half, "core", axis=0).reshape(2, GRAD_BLOCKS, depth, LAST)
+    count = per_quarter * depth // 2
+    share = -(-count // far // 8) * 8
+    parts = parts.reshape(near_y * reps * near_z, count, LAST)
+    near, token = pl.pallas_call(
+        near_sum_kernel,
+        out_shape=(
+            jax.ShapeDtypeStruct((far * share, LAST), BF),
+            jax.ShapeDtypeStruct(scales.shape, F32),
+        ),
+        in_specs=[VMEM, VMEM],
+        out_specs=(VMEM, VMEM),
+        compiler_params=params(8),
+        cost_estimate=cost(10**6, 2 * 10**6),
+    )(lax.all_to_all(parts, NEAR_AXES, 0, 0, tiled=True), scales)
+    input_grad = pl.pallas_call(
+        input_kernel,
+        out_shape=jax.ShapeDtypeStruct(local_in.shape, BF),
+        in_specs=[VMEM, HBM, VMEM, HBM],
+        out_specs=VMEM,
+        scratch_shapes=[
+            pltpu.VMEM(local_in.shape, BF),
+            pltpu.VMEM(w1.shape, BF),
+            pltpu.VMEM((4, 8, 16, 9 * LAST), BF),
+            pltpu.SemaphoreType.DMA((2,)),
+        ],
+        compiler_params=params(24),
+        cost_estimate=cost(2 * 10**9, 4 * 10**6),
+    )(token, local_in, packet, w1)
+
+    near = near.reshape(far, share, LAST)
+    copies = pl.pallas_call(
+        far_sum_kernel,
+        out_shape=jax.ShapeDtypeStruct((plane, share, LAST), BF),
+        in_specs=[VMEM, ANY],
+        out_specs=VMEM,
+        compiler_params=params(8),
+        cost_estimate=cost(10**5, 5 * 10**5),
+    )(
+        lax.all_to_all(near, FAR_AXES, 0, 0, tiled=True),
+        pltpu.with_memory_space_constraint(input_grad, pltpu.HBM),
+    )
+    half = lax.all_to_all(copies, PLANE_AXES, 0, 0, tiled=True)
+    whole = lax.all_gather(half.reshape(quarters, far * share, LAST), "core", axis=0)
 
     cell_total = tiles * reps * cotangent.shape[1] * cotangent.shape[2] * cotangent.shape[3]
     scale = 1.0 / math.sqrt(cell_total)
     first, second = pl.pallas_call(
-        lambda *refs: finish_kernel(scale, *refs),
+        lambda *refs: finish_kernel(scale, per_quarter, *refs),
         out_shape=(
             jax.ShapeDtypeStruct((27, depth, 256), F32),
             jax.ShapeDtypeStruct((27, depth, LAST), F32),
@@ -650,8 +712,13 @@
 def solution(mesh):
     devices = mesh.devices
     tiles, reps = devices.shape
-    side = math.isqrt(tiles // 2)
-    wide_mesh = Mesh(devices.reshape(side, tiles // 2 // side, 2, reps), ("y", "z", "core", "x"))
+    height = math.isqrt(tiles // 2)
+    width = tiles // 2 // height
+    near_y, near_z = math.gcd(height, 2), math.gcd(width, 2)
+    wide_mesh = Mesh(
+        devices.reshape(height // near_y, near_y, width // near_z, near_z, 2, reps),
+        (*TILE_AXES, "x"),
+    )
     in_specs = (
         P("x", None, TILE_AXES, None, None),
         P("x", None, TILE_AXES, None, None),

time: 105 us -> 99.3 us (0.946)
  waiting for transfers between devices: 12.6 us -> 8.72 us
  Pallas kernels: 13.7 us -> 16 us
  blocking collectives: 48.8 us -> 47 us
  other arithmetic: 1.78 us -> 0 us
    all_to_all x1, waiting for transfers between devices: 11.7 us -> 7.78 us  [body(): lax.all_to_all(near, FAR_AXES, 0, 0, tiled=True)]
    all_to_all x2, blocking collectives: 42.6 us -> 40.3 us  [the longest x1 22.3 us: body(): lax.all_to_all(parts, NEAR_AXES, 0, 0, tiled=True)]
    reduce_sum x2 -> x0, other arithmetic: 1.78 us -> none  [wide_sum(): return jnp.sum(parts.astype(F32), axis=0).astype(BF)]
    pallas_call x1, Pallas kernels: 2.08 us -> 3.58 us  [body(): pl.pallas_call(input_kernel, out_shape=jax.ShapeDtypeStruct(local_in.shap...]
    pallas_call x2 -> x4, Pallas kernels: 2.97 us -> 3.85 us  [the longest x1 1.84 us: body(): pl.pallas_call(weight_kernel, out_shape=jax.ShapeDtypeStruct((near_y, rep...]
  transfers between devices with their start and end apart: 4 -> 4, of which waited for: 3 -> 3; matrix products, arithmetic and copies ran while one was open for 0% -> 0% of each run, Pallas kernels for 7% -> 8%
where the time goes in v4:
time: 99.3 us; the launch traced here: 98.9 us
  blocking collectives  47 us (47%)
  starting transfers between devices  26.4 us (27%)
  Pallas kernels  16 us (16%)
  waiting for transfers between devices  8.72 us (9%)
    all_to_all x1, blocking collectives, body(): lax.all_to_all(parts, NEAR_AXES, 0, 0, tiled=True)  22.3 us
    all_to_all x1, blocking collectives, body(): half = lax.all_to_all(copies, PLANE_AXES, 0, 0, tiled=True)  18 us
    ppermute x1, starting transfers between devices, body(): sibling = lax.ppermute(tile, 'core', swap)  8.79 us
    ppermute x1, starting transfers between devices, body(): sib_packet = lax.ppermute(packet, 'core', swap)  8.24 us
    all_to_all x1, waiting for transfers between devices, body(): lax.all_to_all(near, FAR_AXES, 0, 0, tiled=True)  7.78 us
    all_to_all x1, starting transfers between devices, body(): lax.all_to_all(near, FAR_AXES, 0, 0, tiled=True)  7.46 us
    all_gather x1, blocking collectives, body(): lax.all_gather(half.reshape(quarters, far * share, LAST), 'core', axis=0)  6.73 us
    pallas_call x1, Pallas kernels, body(): pl.pallas_call(inner_kernel, out_shape=(jax.ShapeDtypeStruct((4, 6, 16, L...  4.17 us
  transfers between devices with their start and end apart: 4, of which 3 were waited for; matrix products, arithmetic and copies ran while one was open for 0% of the time, Pallas kernels for 8%

profile of v4, /device:TPU:1, one launch (start us, length us, event | category | flops | bytes accessed | tf_op | source)
XLA Modules:
  0.0 98.9 jit_solution(13901478291900695637)
XLA Ops:
  0.6 0.9 shard_map.94.rim_any
  1.6 1.1 %shard_map.95 = (bf16[160,16,128]{2,1,0:T(8,128)(2,1)S(1)}, f32[8,128]{1,0:T(8,128)S(1)}) custom-call(s32[1,128]{1,0:T(1,128)} %clip_any.1, s32[1,8]{1,0:T(1,128)} %cols_any.1, s32[1,8]{1,0:T(1,128)} %start_any.1, bf16[6,8,16,256]{3,2,1,0:T(8,128)(2,1)} %bitcast.16, bf16[2,16,32,128]{3,2,1,0:T(8,128)(2,1)} %bitcast.20, ...), custom_call_target="tpu_custom_call" | custom-call | flops 1000000 | bytes 2000000 | tf_op jit(solution)/shard_map/pallas_call | solution.py:561
  2.7 8.8 %collective-permute-start = (bf16[160,16,128]{2,1,0:T(8,128)(2,1)S(1)}, bf16[160,16,128]{2,1,0:T(8,128)(2,1)S(1)}, u32[]{:S(2)}, u32[]{:S(2)}) collective-permute-start(bf16[160,16,128]{2,1,0:T(8,128)(2,1)S(1)} %get-tuple-element.17.tile_ref), channel_id=1, source_target_pairs={{0,4},{4,0},{1,5},{5,1},{2,6},{6,2},{3,7},{7,3},{8,12},{12,8},{9,1... | collective-permute-start | bytes 1966088 | tf_op jit(solution)/shard_map/ppermute | solution.py:577
  11.5 1.9 %collective-permute-start.1 = (bf16[36,16,128]{2,1,0:T(8,128)(2,1)S(1)}, bf16[36,16,128]{2,1,0:T(8,128)(2,1)S(1)}, u32[]{:S(2)}, u32[]{:S(2)}) collective-permute-start(bf16[36,16,128]{2,1,0:T(8,128)(2,1)S(1)} %shard_map.94.rim_any), channel_id=1, source_target_pairs={{4,8},{12,16},{20,24},{28,32},{36,40},{44,48},{52,56},{60,64},{68,... | collective-permute-start | bytes 442376 | tf_op jit(solution)/shard_map/ppermute | solution.py:559
  13.4 4.2 %shard_map.96 = (bf16[4,6,16,128]{3,2,1,0:T(8,128)(2,1)S(1)}, bf16[4,6,16,128]{3,2,1,0:T(8,128)(2,1)S(1)}, bf16[6,8,16,256]{3,2,1,0:T(8,128)(2,1)S(1)}, bf16[27,...) custom-call(f32[8,128]{1,0:T(8,128)S(1)} %get-tuple-element.16.scales, ...), custom_call_target="tpu_custom_call" | custom-call | flops 2000000000 | bytes 4000000 | tf_op jit(solution)/shard_map/pallas_call | solution.py:579
  17.6 0.4 collective-permute-done.1.rim_ref
  18.0 0.0 collective-permute-done.sib_ref
  18.0 1.7 %shard_map.97.packet_ref = bf16[76,16,128]{2,1,0:T(8,128)(2,1)S(1)} custom-call(bf16[36,16,128]{2,1,0:T(8,128)(2,1)S(1)} %collective-permute-done.1.rim_ref, f32[8,128]{1,0:T(8,128)S(1)} %get-tuple-element.16.scales, bf16[160,16,128]{2,1,0:T(8,128)(2,1)S(1)} %get-tuple-element.17.tile_ref, bf16[160,16,128]{2,1,0:T(8,128)(2,1)S(1)} %collective-permute-done.sib_ref, ...), custom_call_target="tpu_custom_call" | custom-call | flops 1000000000 | bytes 4000000 | tf_op jit(solution)/shard_map/pallas_call | solution.py:616
  19.7 8.2 %collective-permute-start.2 = (bf16[76,16,128]{2,1,0:T(8,128)(2,1)S(1)}, bf16[76,16,128]{2,1,0:T(8,128)(2,1)S(1)}, u32[]{:S(2)}, u32[]{:S(2)}) collective-permute-start(bf16[76,16,128]{2,1,0:T(8,128)(2,1)S(1)} %shard_map.97.packet_ref), channel_id=1, source_target_pairs={{0,4},{4,0},{1,5},{5,1},{2,6},{6,2},{3,7},{7,3},{8,12},{12,8},{9,1... | collective-permute-start | bytes 933896 | tf_op jit(solution)/shard_map/ppermute | solution.py:630
  28.0 0.6 shard_map.98
  28.6 0.6 collective-permute-done.2.sib_packet_ref
  29.2 1.8 %shard_map.99 = bf16[2,4,2,21,16,128]{5,4,3,2,1,0:T(8,128)(2,1)S(1)} custom-call(f32[8,128]{1,0:T(8,128)S(1)} %get-tuple-element.16.scales, bf16[160,16,128]{2,1,0:T(8,128)(2,1)S(1)} %get-tuple-element.17.tile_ref, bf16[160,16,128]{2,1,0:T(8,128)(2,1)S(1)} %collective-permute-done.sib_ref, bf16[76,16,128]{2,1,0:T(8,128)(2,1)S(1)} %shard_map.97.packet_ref, ...), custom_call_target="tpu_custom_call" | custom-call | flops 2000000000 | bytes 4000000 | tf_op jit(solution)/shard_map/pallas_call | solution.py:635
  31.0 22.3 %all_to_all.15.parts_ref = bf16[16,336,128]{2,1,0:T(8,128)(2,1)S(1)} all-to-all(bf16[16,336,128]{2,1,0:T(8,128)(2,1)S(1)} %bitcast.14), channel_id=1, replica_groups=mesh['yh'=4,'yl'=2,'zh'=4,'zl'=2,'core'=2,'x'=4] {'yl','x','zl'}, dimensions={0} | all-to-all | bytes 2752512 | tf_op jit(solution)/shard_map/all_to_all | solution.py:664
  53.3 0.8 shard_map.100
  54.1 7.5 %all-to-all-start.1 = ((bf16[16,24,128]{2,1,0:T(8,128)(2,1)}), bf16[16,24,128]{2,1,0:T(8,128)(2,1)S(1)}, u32[]{:S(2)}, u32[]{:S(2)}) async-start(bf16[16,24,128]{2,1,0:T(8,128)(2,1)} %bitcast.6), calls=%async_computation.1 | async-start | bytes 196608 | tf_op jit(solution)/shard_map/all_to_all | solution.py:689
  61.6 3.6 %shard_map.101._ = bf16[6,8,16,256]{3,2,1,0:T(8,128)(2,1)} custom-call(f32[8,128]{1,0:T(8,128)S(1)} %get-tuple-element.25.scales, bf16[6,8,16,256]{3,2,1,0:T(8,128)(2,1)} %bitcast.17, bf16[76,16,128]{2,1,0:T(8,128)(2,1)S(1)} %shard_map.97.packet_ref, bf16[27,256,128]{2,1,0:T(8,128)(2,1)} %bitcast.23), custom_call_target="tpu_custom_call" | custom-call | flops 2000000000 | bytes 4000000 | tf_op jit(solution)/shard_map/pallas_call | solution.py:665
  65.2 7.8 %all-to-all-done.1.parts_ref = bf16[16,24,128]{2,1,0:T(8,128)(2,1)S(1)} async-done(((bf16[16,24,128]{2,1,0:T(8,128)(2,1)}), bf16[16,24,128]{2,1,0:T(8,128)(2,1)S(1)}, u32[]{:S(2)}, u32[]{:S(2)}) %all-to-all-start.1) | async-done | bytes 98336 | tf_op jit(solution)/shard_map/all_to_all | solution.py:689
  73.0 18.0 %all_to_all.16 = bf16[64,24,128]{2,1,0:T(8,128)(2,1)S(1)} all-to-all(bf16[64,24,128]{2,1,0:T(8,128)(2,1)S(1)} %shard_map.102), channel_id=1, replica_groups=mesh['yh'=4,'yl'=2,'zh'=4,'zl'=2,'core'=2,'x'=4] {'yl','zl','zh','yh'}, dimensions={0} | all-to-all | bytes 786432 | tf_op jit(solution)/shard_map/all_to_all | solution.py:692
  91.0 6.7 %all_gather.3.refs_0_ = bf16[2,4,384,128]{3,2,1,0:T(8,128)(2,1)S(1)} all-gather(bf16[1,4,384,128]{3,2,1,0:T(8,128)(2,1)S(1)} %bitcast.18), channel_id=1, replica_groups=mesh['yh'=4,'yl'=2,'zh'=4,'zl'=2,'core'=2,'x'=4] {'core'}, dimensions={0}, use_global_device_ids=true | all-gather | bytes 1179648 | tf_op jit(solution)/shard_map/all_gather | solution.py:693
  97.7 1.1 %shard_map.103 = (f32[27,32,256]{2,1,0:T(8,128)}, f32[27,32,128]{2,1,0:T(8,128)}) custom-call(bf16[2,4,384,128]{3,2,1,0:T(8,128)(2,1)S(1)} %all_gather.3.refs_0_), custom_call_target="tpu_custom_call" | custom-call | tf_op jit(solution)/shard_map/pallas_call | solution.py:697
  (1 shorter events, 0.0 us)
Async XLA Ops:
  2.7 15.3 %collective-permute-start = (bf16[160,16,128]{2,1,0:T(8,128)(2,1)S(1)}, bf16[160,16,128]{2,1,0:T(8,128)(2,1)S(1)}, u32[]{:S(2)}, u32[]{:S(2)}) collective-permute-start(bf16[160,16,128]{2,1,0:T(8,128)(2,1)S(1)} %get-tuple-element.17.tile_ref), channel_id=1, source_target_pairs={{0,4},{4,0},{1,5},{5,1},{2,6},{6,2},{3,7},{7,3},{8,12},{12,8},{9,1... | collective-permute-start | bytes 1966088 | tf_op jit(solution)/shard_map/ppermute | solution.py:577
  11.5 6.5 %collective-permute-start.1 = (bf16[36,16,128]{2,1,0:T(8,128)(2,1)S(1)}, bf16[36,16,128]{2,1,0:T(8,128)(2,1)S(1)}, u32[]{:S(2)}, u32[]{:S(2)}) collective-permute-start(bf16[36,16,128]{2,1,0:T(8,128)(2,1)S(1)} %shard_map.94.rim_any), channel_id=1, source_target_pairs={{4,8},{12,16},{20,24},{28,32},{36,40},{44,48},{52,56},{60,64},{68,... | collective-permute-start | bytes 442376 | tf_op jit(solution)/shard_map/ppermute | solution.py:559
  19.7 9.5 %collective-permute-start.2 = (bf16[76,16,128]{2,1,0:T(8,128)(2,1)S(1)}, bf16[76,16,128]{2,1,0:T(8,128)(2,1)S(1)}, u32[]{:S(2)}, u32[]{:S(2)}) collective-permute-start(bf16[76,16,128]{2,1,0:T(8,128)(2,1)S(1)} %shard_map.97.packet_ref), channel_id=1, source_target_pairs={{0,4},{4,0},{1,5},{5,1},{2,6},{6,2},{3,7},{7,3},{8,12},{12,8},{9,1... | collective-permute-start | bytes 933896 | tf_op jit(solution)/shard_map/ppermute | solution.py:630
  54.1 18.8 %all-to-all-start.1 = ((bf16[16,24,128]{2,1,0:T(8,128)(2,1)}), bf16[16,24,128]{2,1,0:T(8,128)(2,1)S(1)}, u32[]{:S(2)}, u32[]{:S(2)}) async-start(bf16[16,24,128]{2,1,0:T(8,128)(2,1)} %bitcast.6), calls=%async_computation.1 | async-start | bytes 196608 | tf_op jit(solution)/shard_map/all_to_all | solution.py:689

commit v5 on v4

--- a/solution.py
+++ b/solution.py
@@ -99,32 +99,8 @@
     )
 
 
-def rim_kernel(in_any, cot_any, rim_ref, in_ref, cot_ref, sems):
-    odd = lax.axis_index("core")
-    copies = (
-        pltpu.make_async_copy(in_any.at[:, pl.ds(odd * 6, 2)], in_ref, sems.at[0]),
-        pltpu.make_async_copy(cot_any.at[:, pl.ds(odd * 13, 3)], cot_ref, sems.at[1]),
-    )
-    for copy in copies:
-        copy.start()
-    copies[0].wait()
-    for frame in range(6):
-        for row in range(2):
-            for half in range(2):
-                rim_ref[frame * 4 + row * 2 + half] = in_ref[
-                    frame, row, :, half * LAST : (half + 1) * LAST
-                ]
-    copies[1].wait()
-    for frame in range(2):
-        for row in range(3):
-            for half in range(2):
-                rim_ref[RIM_COT + frame * 6 + row * 2 + half] = cot_ref[
-                    frame, row, half * 16 : (half + 1) * 16, :
-                ]
-
-
 def pack_kernel(
-    clip_any, cols_any, start_any, in_any, cot_any, rim_any, tile_ref, scales_ref,
+    clip_any, cols_any, start_any, in_any, cot_any, rim_ref, tile_ref, scales_ref,
     clip_ref, cols_ref, start_ref, in_ref, cot_ref, sems,
 ):
     copies = [
@@ -141,10 +117,6 @@
     ]
     for copy in copies:
         copy.start()
-    for copy in copies[:3]:
-        copy.wait()
-    for row, value in enumerate(load_scales(clip_ref, cols_ref, start_ref)):
-        scales_ref[row : row + 1] = jnp.full((1, LAST), value, F32)
     copies[3].wait()
     for frame in range(6):
         for row in range(8):
@@ -159,6 +131,16 @@
                 tile_ref[TILE_COT + frame * 32 + row * 2 + half] = cot_ref[
                     frame, row, half * 16 : (half + 1) * 16, :
                 ]
+    odd = lax.axis_index("core")
+    for frame in range(6):
+        rim_ref[frame * 4 : frame * 4 + 4] = tile_ref[pl.ds(frame * 16 + odd * 12, 4)]
+    for frame in range(2):
+        at = RIM_COT + frame * 6
+        rim_ref[at : at + 6] = tile_ref[pl.ds(TILE_COT + frame * 32 + odd * 26, 6)]
+    for copy in copies[:3]:
+        copy.wait()
+    for row, value in enumerate(load_scales(clip_ref, cols_ref, start_ref)):
+        scales_ref[row : row + 1] = jnp.full((1, LAST), value, F32)
 
 
 def pair_sums(rows, pair, put):
@@ -317,7 +299,8 @@
     second_conv_back(cots[...].reshape(128, 1152), w2_ref, slope.reshape(4, 64, LAST), put)
 
 
-def sibling_kernel(scales, tile_ref, sib_ref, act_ref, sums_ref, rows, pair):
+def sibling_kernel(scales, tile_ref, sib_ref, act_ref, sums_ref, token_ref, rows, pair):
+    token_ref[...] = scales[...]
     keep = twice(scale_of(scales, SIB_KEEP))
     low = twice(low_mask(scales, SIB_COLS))
     for frame in range(6):
@@ -387,10 +370,11 @@
 
 
 def weight_kernel(
-    scales, tile_ref, sib_ref, packet_ref, sib_packet_ref, act_ref, sib_act_ref, sums_ref,
+    packets_ref, scales, tile_ref, sib_ref, act_ref, sib_act_ref, sums_ref,
     part_ref, pair, sums, cols,
 ):
     odd = lax.axis_index("core")
+    packet_ref, sib_packet_ref = packets_ref.at[odd], packets_ref.at[1 - odd]
     near_y, reps, near_z, per_quarter, depth = part_ref.shape[:5]
     sums[...] = sums_ref[...]
     for slot, tile, packet, which in (
@@ -463,8 +447,7 @@
             put_block(jnp.zeros((LAST, LAST), F32), at)
 
 
-def near_sum_kernel(parts_ref, scales, sum_ref, token_ref):
-    token_ref[...] = scales[...]
+def near_sum_kernel(parts_ref, sum_ref):
     rows = parts_ref.shape[1]
     total = parts_ref[0].astype(F32)
     for n in range(1, parts_ref.shape[0]):
@@ -474,14 +457,15 @@
         sum_ref[rows:] = jnp.zeros((sum_ref.shape[0] - rows, LAST), BF)
 
 
-def far_sum_kernel(parts_ref, _, copies_ref):
+def far_sum_kernel(parts_ref, scales, copies_ref, token_ref):
+    token_ref[...] = scales[...]
     total = parts_ref[0].astype(F32)
     for n in range(1, parts_ref.shape[0]):
         total = total + parts_ref[n].astype(F32)
     copies_ref[...] = jnp.broadcast_to(total.astype(BF)[None], copies_ref.shape)
 
 
-def finish_kernel(scale, per_quarter, whole_ref, first_ref, second_ref):
+def finish_kernel(scale, per_quarter, whole_ref, _, first_ref, second_ref):
     depth = first_ref.shape[1] // 2
     for core in range(2):
 
@@ -543,26 +527,11 @@
     swap = [(0, 1), (1, 0)]
     across = [(i, (i + 1) % tiles) for i in range(1, tiles, 2)]
     across += [(b, a) for a, b in across]
-    own_rim = pl.pallas_call(
-        rim_kernel,
-        out_shape=blocks(RIM_BLOCKS),
-        in_specs=[HBM] * 2,
-        out_specs=VMEM,
-        scratch_shapes=[
-            pltpu.VMEM((6, 2, 16, 256), BF),
-            pltpu.VMEM((2, 3, 32, LAST), BF),
-            pltpu.SemaphoreType.DMA((2,)),
-        ],
-        compiler_params=params(4),
-        cost_estimate=cost(10**5, 3 * 10**5),
-    )(local_in, local_cot)
-    rim = lax.ppermute(own_rim, TILE_AXES, across)
-
-    tile, scales = pl.pallas_call(
+    own_rim, tile, scales = pl.pallas_call(
         pack_kernel,
-        out_shape=(blocks(TILE_BLOCKS), jax.ShapeDtypeStruct((8, LAST), F32)),
-        in_specs=[HBM] * 5 + [ANY],
-        out_specs=(VMEM, VMEM),
+        out_shape=(blocks(RIM_BLOCKS), blocks(TILE_BLOCKS), jax.ShapeDtypeStruct((8, LAST), F32)),
+        in_specs=[HBM] * 5,
+        out_specs=(VMEM, VMEM, VMEM),
         scratch_shapes=[
             pltpu.SMEM(tile_clip.shape, jnp.int32),
             pltpu.SMEM(clip_cols.shape, jnp.int32),
@@ -573,7 +542,8 @@
         ],
         compiler_params=params(8),
         cost_estimate=cost(10**6, 2 * 10**6),
-    )(tile_clip, clip_cols, clip_start, local_in, local_cot, own_rim)
+    )(tile_clip, clip_cols, clip_start, local_in, local_cot)
+    rim = lax.ppermute(own_rim, TILE_AXES, across)
     sibling = lax.ppermute(tile, "core", swap)
 
     inner_first, inner_second, act, inner_w1, inner_w2 = pl.pallas_call(
@@ -597,14 +567,15 @@
         cost_estimate=cost(2 * 10**9, 4 * 10**6),
     )(scales, tile, w1, w2)
 
-    sib_act, sums = pl.pallas_call(
+    sib_act, sums, scales = pl.pallas_call(
         sibling_kernel,
         out_shape=(
             jax.ShapeDtypeStruct((6, 8, 16, 256), BF),
             jax.ShapeDtypeStruct((3, 2, 2, 17, 16, LAST), BF),
+            jax.ShapeDtypeStruct(scales.shape, F32),
         ),
         in_specs=[VMEM] * 3,
-        out_specs=(VMEM, VMEM),
+        out_specs=(VMEM, VMEM, VMEM),
         scratch_shapes=[
             pltpu.VMEM((18, 32, LAST), F32),
             pltpu.VMEM((17, 48, LAST), F32),
@@ -627,7 +598,7 @@
         compiler_params=params(16),
         cost_estimate=cost(10**9, 4 * 10**6),
     )(rim, scales, tile, sibling, inner_first, inner_second, inner_w1, inner_w2)
-    sib_packet = lax.ppermute(packet, "core", swap)
+    packets = lax.all_gather(packet, "core", axis=0)
 
     depth = LAST // reps
     quarters = near_y * near_z
@@ -637,7 +608,7 @@
         out_shape=jax.ShapeDtypeStruct(
             (near_y, reps, near_z, per_quarter, depth // 2, LAST), BF
         ),
-        in_specs=[VMEM] * 8,
+        in_specs=[VMEM] * 7,
         out_specs=VMEM,
         scratch_shapes=[
             pltpu.VMEM((1, 48, LAST), F32),
@@ -646,22 +617,31 @@
         ],
         compiler_params=params(24),
         cost_estimate=cost(2 * 10**9, 4 * 10**6),
-    )(scales, tile, sibling, packet, sib_packet, act, sib_act, sums)
+    )(packets, scales, tile, sibling, act, sib_act, sums)
 
     count = per_quarter * depth // 2
     share = -(-count // far // 8) * 8
     parts = parts.reshape(near_y * reps * near_z, count, LAST)
-    near, token = pl.pallas_call(
+    near = pl.pallas_call(
         near_sum_kernel,
+        out_shape=jax.ShapeDtypeStruct((far * share, LAST), BF),
+        in_specs=[VMEM],
+        out_specs=VMEM,
+        compiler_params=params(8),
+        cost_estimate=cost(10**6, 2 * 10**6),
+    )(lax.all_to_all(parts, NEAR_AXES, 0, 0, tiled=True))
+    near = near.reshape(far, share, LAST)
+    copies, token = pl.pallas_call(
+        far_sum_kernel,
         out_shape=(
-            jax.ShapeDtypeStruct((far * share, LAST), BF),
+            jax.ShapeDtypeStruct((plane, share, LAST), BF),
             jax.ShapeDtypeStruct(scales.shape, F32),
         ),
         in_specs=[VMEM, VMEM],
         out_specs=(VMEM, VMEM),
         compiler_params=params(8),
-        cost_estimate=cost(10**6, 2 * 10**6),
-    )(lax.all_to_all(parts, NEAR_AXES, 0, 0, tiled=True), scales)
+        cost_estimate=cost(10**5, 5 * 10**5),
+    )(lax.all_to_all(near, FAR_AXES, 0, 0, tiled=True), scales)
     input_grad = pl.pallas_call(
         input_kernel,
         out_shape=jax.ShapeDtypeStruct(local_in.shape, BF),
@@ -677,18 +657,6 @@
         cost_estimate=cost(2 * 10**9, 4 * 10**6),
     )(token, local_in, packet, w1)
 
-    near = near.reshape(far, share, LAST)
-    copies = pl.pallas_call(
-        far_sum_kernel,
-        out_shape=jax.ShapeDtypeStruct((plane, share, LAST), BF),
-        in_specs=[VMEM, ANY],
-        out_specs=VMEM,
-        compiler_params=params(8),
-        cost_estimate=cost(10**5, 5 * 10**5),
-    )(
-        lax.all_to_all(near, FAR_AXES, 0, 0, tiled=True),
-        pltpu.with_memory_space_constraint(input_grad, pltpu.HBM),
-    )
     half = lax.all_to_all(copies, PLANE_AXES, 0, 0, tiled=True)
     whole = lax.all_gather(half.reshape(quarters, far * share, LAST), "core", axis=0)
 
@@ -700,10 +668,10 @@
             jax.ShapeDtypeStruct((27, depth, 256), F32),
             jax.ShapeDtypeStruct((27, depth, LAST), F32),
         ),
-        in_specs=[VMEM],
+        in_specs=[VMEM, ANY],
         out_specs=(VMEM, VMEM),
         compiler_params=params(16),
-    )(whole)
+    )(whole, pltpu.with_memory_space_constraint(input_grad, pltpu.HBM))
     first = jnp.swapaxes(first, 1, 2).reshape(3, 3, 3, 256, depth)
     second = jnp.swapaxes(second, 1, 2).reshape(3, 3, 3, LAST, depth)
     return input_grad[None], first, second

time: 99.3 us -> 97.4 us (0.981)
  starting transfers between devices: 26.4 us -> 15.3 us
  blocking collectives: 47 us -> 56 us
    all_gather x0 -> x1, blocking collectives: none -> 8.55 us  [body(): packets = lax.all_gather(packet, 'core', axis=0)]
    ppermute x1 -> x0, starting transfers between devices: 8.24 us -> none  [body(): sib_packet = lax.ppermute(packet, 'core', swap)]
    all_to_all x1, starting transfers between devices: 7.46 us -> 4.63 us  [body(): half = lax.all_to_all(copies, PLANE_AXES, 0, 0, tiled=True)]
    all_to_all x1, waiting for transfers between devices: 7.78 us -> 9.69 us  [body(): half = lax.all_to_all(copies, PLANE_AXES, 0, 0, tiled=True)]
    pallas_call x4 -> x3, Pallas kernels: 2.94 us -> 2.17 us  [the longest x1 1.2 us: body(): pl.pallas_call(pack_kernel, out_shape=(blocks(RIM_BLOCKS), blocks(TILE_BL...]
  transfers between devices with their start and end apart: 4 -> 3, of which waited for: 3 -> 1; matrix products, arithmetic and copies ran while one was open for 0% -> 0% of each run, Pallas kernels for 8% -> 9%
where the time goes in v5:
time: 97.4 us; the launch traced here: 97 us
  blocking collectives  56 us (57%)
  starting transfers between devices  15.3 us (16%)
  Pallas kernels  15.2 us (16%)
  waiting for transfers between devices  9.69 us (10%)
    all_to_all x1, blocking collectives, body(): lax.all_to_all(parts, NEAR_AXES, 0, 0, tiled=True)  22.3 us
    all_to_all x1, blocking collectives, body(): lax.all_to_all(near, FAR_AXES, 0, 0, tiled=True)  18 us
    all_to_all x1, waiting for transfers between devices, body(): half = lax.all_to_all(copies, PLANE_AXES, 0, 0, tiled=True)  9.69 us
    ppermute x1, starting transfers between devices, body(): sibling = lax.ppermute(tile, 'core', swap)  8.79 us
    all_gather x1, blocking collectives, body(): packets = lax.all_gather(packet, 'core', axis=0)  8.55 us
    all_gather x1, blocking collectives, body(): lax.all_gather(half.reshape(quarters, far * share, LAST), 'core', axis=0)  7.15 us
    all_to_all x1, starting transfers between devices, body(): half = lax.all_to_all(copies, PLANE_AXES, 0, 0, tiled=True)  4.63 us
    pallas_call x1, Pallas kernels, body(): pl.pallas_call(inner_kernel, out_shape=(jax.ShapeDtypeStruct((4, 6, 16, L...  4.16 us
  transfers between devices with their start and end apart: 3, of which 1 were waited for; matrix products, arithmetic and copies ran while one was open for 0% of the time, Pallas kernels for 9%

profile of v5, /device:TPU:1, one launch (start us, length us, event | category | flops | bytes accessed | tf_op | source)
XLA Modules:
  0.0 97.0 jit_solution(17510416783608927308)
XLA Ops:
  0.6 1.2 %shard_map.94 = (bf16[36,16,128]{2,1,0:T(8,128)(2,1)S(1)}, bf16[160,16,128]{2,1,0:T(8,128)(2,1)S(1)}, f32[8,128]{1,0:T(8,128)S(1)}) custom-call(s32[1,128]{1,0:T(1,128)} %clip_any.1, s32[1,8]{1,0:T(1,128)} %cols_any.1, s32[1,8]{1,0:T(1,128)} %start_any.1, bf16[6,8,16,256]{3,2,1,0:T(8,128)(2,1)} %bitcast.19, bf16[2,16,32,128]{3,2,1,0:T(8,128)(2,1)} %bitcast.22), custom_call_target="tpu_custom_call" | custom-call | flops 1000000 | bytes 2000000 | tf_op jit(solution)/shard_map/pallas_call | solution.py:530
  1.8 8.8 %collective-permute-start.1 = (bf16[160,16,128]{2,1,0:T(8,128)(2,1)S(1)}, bf16[160,16,128]{2,1,0:T(8,128)(2,1)S(1)}, u32[]{:S(2)}, u32[]{:S(2)}) collective-permute-start(bf16[160,16,128]{2,1,0:T(8,128)(2,1)S(1)} %get-tuple-element.20.tile_ref), channel_id=1, source_target_pairs={{0,4},{4,0},{1,5},{5,1},{2,6},{6,2},{3,7},{7,3},{8,12},{12,8},{9,1... | collective-permute-start | bytes 1966088 | tf_op jit(solution)/shard_map/ppermute | solution.py:547
  10.6 1.9 %collective-permute-start = (bf16[36,16,128]{2,1,0:T(8,128)(2,1)S(1)}, bf16[36,16,128]{2,1,0:T(8,128)(2,1)S(1)}, u32[]{:S(2)}, u32[]{:S(2)}) collective-permute-start(bf16[36,16,128]{2,1,0:T(8,128)(2,1)S(1)} %get-tuple-element.18), channel_id=1, source_target_pairs={{4,8},{12,16},{20,24},{28,32},{36,40},{44,48},{52,56},{60,64},{68,... | collective-permute-start | bytes 442376 | tf_op jit(solution)/shard_map/ppermute | solution.py:546
  12.6 4.2 %shard_map.96 = (bf16[4,6,16,128]{3,2,1,0:T(8,128)(2,1)S(1)}, bf16[4,6,16,128]{3,2,1,0:T(8,128)(2,1)S(1)}, bf16[6,8,16,256]{3,2,1,0:T(8,128)(2,1)S(1)}, bf16[27,...) custom-call(f32[8,128]{1,0:T(8,128)S(1)} %get-tuple-element.19.scales, ...), custom_call_target="tpu_custom_call" | custom-call | flops 2000000000 | bytes 4000000 | tf_op jit(solution)/shard_map/pallas_call | solution.py:549
  16.7 0.0 collective-permute-done.1.sib_ref
  16.7 0.6 shard_map.95
  17.4 0.0 collective-permute-done.rim_ref
  17.4 1.8 %shard_map.97.packet_ref = bf16[76,16,128]{2,1,0:T(8,128)(2,1)S(1)} custom-call(bf16[36,16,128]{2,1,0:T(8,128)(2,1)S(1)} %collective-permute-done.rim_ref, f32[8,128]{1,0:T(8,128)S(1)} %get-tuple-element.21.scales, bf16[160,16,128]{2,1,0:T(8,128)(2,1)S(1)} %get-tuple-element.20.tile_ref, bf16[160,16,128]{2,1,0:T(8,128)(2,1)S(1)} %collective-permute-done.1.sib_ref, ...), custom_call_target="tpu_custom_call" | custom-call | flops 1000000000 | bytes 4000000 | tf_op jit(solution)/shard_map/pallas_call | solution.py:587
  19.1 8.5 %all-gather = bf16[152,16,128]{2,1,0:T(8,128)(2,1)S(1)} all-gather(bf16[76,16,128]{2,1,0:T(8,128)(2,1)S(1)} %shard_map.97.packet_ref), channel_id=2, replica_groups=mesh['yh'=4,'yl'=2,'zh'=4,'zl'=2,'core'=2,'x'=4] {'core'}, dimensions={0}, use_global_device_ids=true | all-gather | bytes 933888 | tf_op jit(solution)/shard_map/all_gather | solution.py:601
  27.7 1.8 %shard_map.98 = bf16[2,4,2,21,16,128]{5,4,3,2,1,0:T(8,128)(2,1)S(1)} custom-call(bf16[2,76,16,128]{3,2,1,0:T(8,128)(2,1)S(1)} %bitcast.16, f32[8,128]{1,0:T(8,128)S(1)} %get-tuple-element.21.scales, bf16[160,16,128]{2,1,0:T(8,128)(2,1)S(1)} %get-tuple-element.20.tile_ref, bf16[160,16,128]{2,1,0:T(8,128)(2,1)S(1)} %collective-permute-done.1.sib_ref, ...), custom_call_target="tpu_custom_call" | custom-call | flops 2000000000 | bytes 4000000 | tf_op jit(solution)/shard_map/pallas_call | solution.py:606
  29.5 22.3 %all_to_all.15.parts_ref = bf16[16,336,128]{2,1,0:T(8,128)(2,1)S(1)} all-to-all(bf16[16,336,128]{2,1,0:T(8,128)(2,1)S(1)} %bitcast.15), channel_id=1, replica_groups=mesh['yh'=4,'yl'=2,'zh'=4,'zl'=2,'core'=2,'x'=4] {'yl','x','zl'}, dimensions={0} | all-to-all | bytes 2752512 | tf_op jit(solution)/shard_map/all_to_all | solution.py:632
  51.8 0.2 shard_map.99
  52.0 18.0 %all_to_all.16.parts_ref = bf16[16,24,128]{2,1,0:T(8,128)(2,1)S(1)} all-to-all(bf16[16,24,128]{2,1,0:T(8,128)(2,1)S(1)} %bitcast.17), channel_id=1, replica_groups=mesh['yh'=4,'yl'=2,'zh'=4,'zl'=2,'core'=2,'x'=4] {'zh','yh'}, dimensions={0} | all-to-all | bytes 196608 | tf_op jit(solution)/shard_map/all_to_all | solution.py:644
  70.0 0.8 shard_map.100
  70.8 4.6 %all-to-all-start.2 = ((bf16[64,24,128]{2,1,0:T(8,128)(2,1)}), bf16[64,24,128]{2,1,0:T(8,128)(2,1)S(1)}, u32[]{:S(2)}, u32[]{:S(2)}) async-start(bf16[64,24,128]{2,1,0:T(8,128)(2,1)} %get-tuple-element.30), calls=%async_computation.2 | async-start | bytes 786432 | tf_op jit(solution)/shard_map/all_to_all | solution.py:660
  75.4 3.6 %shard_map.101.refs_1_ = bf16[6,8,16,256]{3,2,1,0:T(8,128)(2,1)} custom-call(f32[8,128]{1,0:T(8,128)S(1)} %get-tuple-element.29.scales, bf16[6,8,16,256]{3,2,1,0:T(8,128)(2,1)} %bitcast.20, bf16[76,16,128]{2,1,0:T(8,128)(2,1)S(1)} %shard_map.97.packet_ref, bf16[27,256,128]{2,1,0:T(8,128)(2,1)} %bitcast.24), custom_call_target="tpu_custom_call" | custom-call | flops 2000000000 | bytes 4000000 | tf_op jit(solution)/shard_map/pallas_call | solution.py:645
  79.0 9.7 %all-to-all-done.2 = bf16[64,24,128]{2,1,0:T(8,128)(2,1)S(1)} async-done(((bf16[64,24,128]{2,1,0:T(8,128)(2,1)}), bf16[64,24,128]{2,1,0:T(8,128)(2,1)S(1)}, u32[]{:S(2)}, u32[]{:S(2)}) %all-to-all-start.2) | async-done | bytes 393248 | tf_op jit(solution)/shard_map/all_to_all | solution.py:660
  88.7 7.1 %all_gather.11.refs_0_ = bf16[2,4,384,128]{3,2,1,0:T(8,128)(2,1)S(1)} all-gather(bf16[1,4,384,128]{3,2,1,0:T(8,128)(2,1)S(1)} %bitcast.18), channel_id=1, replica_groups=mesh['yh'=4,'yl'=2,'zh'=4,'zl'=2,'core'=2,'x'=4] {'core'}, dimensions={0}, use_global_device_ids=true | all-gather | bytes 1179648 | tf_op jit(solution)/shard_map/all_gather | solution.py:661
  95.8 1.1 %shard_map.102 = (f32[27,32,256]{2,1,0:T(8,128)}, f32[27,32,128]{2,1,0:T(8,128)}) custom-call(bf16[2,4,384,128]{3,2,1,0:T(8,128)(2,1)S(1)} %all_gather.11.refs_0_, bf16[6,8,16,256]{3,2,1,0:T(8,128)(2,1)} %shard_map.101.refs_1_), custom_call_target="tpu_custom_call" | custom-call | tf_op jit(solution)/shard_map/pallas_call | solution.py:665
Async XLA Ops:
  1.8 14.9 %collective-permute-start.1 = (bf16[160,16,128]{2,1,0:T(8,128)(2,1)S(1)}, bf16[160,16,128]{2,1,0:T(8,128)(2,1)S(1)}, u32[]{:S(2)}, u32[]{:S(2)}) collective-permute-start(bf16[160,16,128]{2,1,0:T(8,128)(2,1)S(1)} %get-tuple-element.20.tile_ref), channel_id=1, source_target_pairs={{0,4},{4,0},{1,5},{5,1},{2,6},{6,2},{3,7},{7,3},{8,12},{12,8},{9,1... | collective-permute-start | bytes 1966088 | tf_op jit(solution)/shard_map/ppermute | solution.py:547
  10.6 6.7 %collective-permute-start = (bf16[36,16,128]{2,1,0:T(8,128)(2,1)S(1)}, bf16[36,16,128]{2,1,0:T(8,128)(2,1)S(1)}, u32[]{:S(2)}, u32[]{:S(2)}) collective-permute-start(bf16[36,16,128]{2,1,0:T(8,128)(2,1)S(1)} %get-tuple-element.18), channel_id=1, source_target_pairs={{4,8},{12,16},{20,24},{28,32},{36,40},{44,48},{52,56},{60,64},{68,... | collective-permute-start | bytes 442376 | tf_op jit(solution)/shard_map/ppermute | solution.py:546
  70.8 17.9 %all-to-all-start.2 = ((bf16[64,24,128]{2,1,0:T(8,128)(2,1)}), bf16[64,24,128]{2,1,0:T(8,128)(2,1)S(1)}, u32[]{:S(2)}, u32[]{:S(2)}) async-start(bf16[64,24,128]{2,1,0:T(8,128)(2,1)} %get-tuple-element.30), calls=%async_computation.2 | async-start | bytes 786432 | tf_op jit(solution)/shard_map/all_to_all | solution.py:660

commit v6 on v5

--- a/solution.py
+++ b/solution.py
@@ -2,6 +2,7 @@
 
 import jax
 import jax.numpy as jnp
+import numpy as np
 from jax import lax
 from jax.experimental import pallas as pl
 from jax.experimental.pallas import tpu as pltpu
@@ -9,8 +10,7 @@
 from jax.sharding import PartitionSpec as P
 
 TILE_AXES = ("yh", "yl", "zh", "zl", "core")
-NEAR_AXES = ("yl", "x", "zl")
-FAR_AXES = ("zh", "yh")
+ALL_AXES = (*TILE_AXES, "x")
 PLANE_AXES = ("yl", "zl", "zh", "yh")
 BF = jnp.bfloat16
 F32 = jnp.float32
@@ -375,7 +375,7 @@
 ):
     odd = lax.axis_index("core")
     packet_ref, sib_packet_ref = packets_ref.at[odd], packets_ref.at[1 - odd]
-    near_y, reps, near_z, per_quarter, depth = part_ref.shape[:5]
+    reps, quarters, per_quarter, depth = part_ref.shape[:4]
     sums[...] = sums_ref[...]
     for slot, tile, packet, which in (
         (0, tile_ref, packet_ref, COLS),
@@ -414,7 +414,9 @@
         halves = block.astype(BF).reshape(reps, 2, depth, LAST)
         for half in range(2):
             quarter, place = divmod(at * 2 + half, per_quarter)
-            part_ref[quarter // near_z, :, quarter % near_z, place] = halves[:, half]
+            for rep in range(reps):
+                first = rep + (quarter - rep) * odd
+                part_ref[first, rep + quarter - first, place] = halves[rep, half]
 
     def first_taps(step, at):
         tap = 5 * odd + step
@@ -448,13 +450,16 @@
 
 
 def near_sum_kernel(parts_ref, sum_ref):
-    rows = parts_ref.shape[1]
-    total = parts_ref[0].astype(F32)
-    for n in range(1, parts_ref.shape[0]):
-        total = total + parts_ref[n].astype(F32)
-    sum_ref[0:rows] = total.astype(BF)
-    if sum_ref.shape[0] > rows:
-        sum_ref[rows:] = jnp.zeros((sum_ref.shape[0] - rows, LAST), BF)
+    shares, others, share, _ = sum_ref.shape
+    rows = parts_ref.shape[2]
+    for other in range(others):
+        total = parts_ref[0, other].astype(F32)
+        for n in range(1, parts_ref.shape[0]):
+            total = total + parts_ref[n, other].astype(F32)
+        if shares * share > rows:
+            padding = jnp.zeros((shares * share - rows, LAST), F32)
+            total = jnp.concatenate([total, padding], 0)
+        sum_ref[:, other] = total.reshape(shares, share, LAST).astype(BF)
 
 
 def far_sum_kernel(parts_ref, scales, copies_ref, token_ref):
@@ -463,6 +468,21 @@
     for n in range(1, parts_ref.shape[0]):
         total = total + parts_ref[n].astype(F32)
     copies_ref[...] = jnp.broadcast_to(total.astype(BF)[None], copies_ref.shape)
+
+
+def sum_groups(sizes):
+    numbers = np.arange(math.prod(sizes)).reshape(sizes)
+    even, odd = numbers[..., 0, :], numbers[..., 1, :]
+    reps, quarters = sizes[5], sizes[1] * sizes[3]
+    near = (
+        even.reshape(-1, reps),
+        odd.transpose(0, 2, 4, 1, 3).reshape(-1, quarters),
+    )
+    far = (
+        even.transpose(4, 2, 0, 1, 3).reshape(reps, -1),
+        odd.transpose(1, 3, 2, 0, 4).reshape(quarters, -1),
+    )
+    return [[row.tolist() for part in parts for row in part] for parts in (near, far)]
 
 
 def finish_kernel(scale, per_quarter, whole_ref, _, first_ref, second_ref):
@@ -511,7 +531,8 @@
 def body(inputs, cotangent, first_weight, second_weight, tile_clip, clip_cols, clip_start):
     tiles = lax.axis_size(TILE_AXES)
     reps, near_y, near_z = (lax.axis_size(name) for name in ("x", "yl", "zl"))
-    far, plane = lax.axis_size(FAR_AXES), lax.axis_size(PLANE_AXES)
+    plane = lax.axis_size(PLANE_AXES)
+    near_groups, far_groups = sum_groups(tuple(map(lax.axis_size, ALL_AXES)))
     local_in, local_cot, tile_clip, clip_cols, clip_start, w1, w2 = (
         pltpu.with_memory_space_constraint(array, pltpu.HBM)
         for array in (
@@ -606,7 +627,7 @@
     parts = pl.pallas_call(
         weight_kernel,
         out_shape=jax.ShapeDtypeStruct(
-            (near_y, reps, near_z, per_quarter, depth // 2, LAST), BF
+            (reps, quarters, per_quarter, depth // 2, LAST), BF
         ),
         in_specs=[VMEM] * 7,
         out_specs=VMEM,
@@ -620,17 +641,21 @@
     )(packets, scales, tile, sibling, act, sib_act, sums)
 
     count = per_quarter * depth // 2
-    share = -(-count // far // 8) * 8
-    parts = parts.reshape(near_y * reps * near_z, count, LAST)
+    share = -(-count * quarters // plane // 8) * 8
+    parts = parts.reshape(reps, quarters, count, LAST)
+
+    def exchange(values, groups):
+        return lax.all_to_all(values, ALL_AXES, 0, 0, axis_index_groups=groups, tiled=True)
+
     near = pl.pallas_call(
         near_sum_kernel,
-        out_shape=jax.ShapeDtypeStruct((far * share, LAST), BF),
+        out_shape=jax.ShapeDtypeStruct((plane // quarters, quarters, share, LAST), BF),
         in_specs=[VMEM],
         out_specs=VMEM,
         compiler_params=params(8),
         cost_estimate=cost(10**6, 2 * 10**6),
-    )(lax.all_to_all(parts, NEAR_AXES, 0, 0, tiled=True))
-    near = near.reshape(far, share, LAST)
+    )(exchange(parts, near_groups))
+    near = near.reshape(plane, share, LAST)
     copies, token = pl.pallas_call(
         far_sum_kernel,
         out_shape=(
@@ -641,7 +666,7 @@
         out_specs=(VMEM, VMEM),
         compiler_params=params(8),
         cost_estimate=cost(10**5, 5 * 10**5),
-    )(lax.all_to_all(near, FAR_AXES, 0, 0, tiled=True), scales)
+    )(exchange(near, far_groups), scales)
     input_grad = pl.pallas_call(
         input_kernel,
         out_shape=jax.ShapeDtypeStruct(local_in.shape, BF),
@@ -658,7 +683,7 @@
     )(token, local_in, packet, w1)
 
     half = lax.all_to_all(copies, PLANE_AXES, 0, 0, tiled=True)
-    whole = lax.all_gather(half.reshape(quarters, far * share, LAST), "core", axis=0)
+    whole = lax.all_gather(half.reshape(quarters, plane // quarters * share, LAST), "core", axis=0)
 
     cell_total = tiles * reps * cotangent.shape[1] * cotangent.shape[2] * cotangent.shape[3]
     scale = 1.0 / math.sqrt(cell_total)

time: 97.4 us -> 96.6 us (level)
  blocking collectives: 56 us -> 51.2 us
  waiting for transfers between devices: 9.69 us -> 12.9 us
    all_gather x1, blocking collectives: 7.15 us -> 2.36 us  [body(): lax.all_gather(half.reshape(quarters, plane // quarters * share, LAST), '...]
    all_to_all x1, waiting for transfers between devices: 9.69 us -> 12.9 us  [body(): half = lax.all_to_all(copies, PLANE_AXES, 0, 0, tiled=True)]
where the time goes in v6:
time: 96.6 us; the launch traced here: 96.3 us
  blocking collectives  51.2 us (53%)
  starting transfers between devices  16.1 us (17%)
  Pallas kernels  15.4 us (16%)
  waiting for transfers between devices  12.9 us (13%)
    all_to_all x2, blocking collectives, exchange(): lax.all_to_all(values, ALL_AXES, 0, 0, axis_index_groups=groups, tiled=True)  40.3 us
    all_to_all x1, waiting for transfers between devices, body(): half = lax.all_to_all(copies, PLANE_AXES, 0, 0, tiled=True)  12.9 us
    ppermute x1, starting transfers between devices, body(): sibling = lax.ppermute(tile, 'core', swap)  8.79 us
    all_gather x1, blocking collectives, body(): packets = lax.all_gather(packet, 'core', axis=0)  8.55 us
    all_to_all x1, starting transfers between devices, body(): half = lax.all_to_all(copies, PLANE_AXES, 0, 0, tiled=True)  5.34 us
    pallas_call x1, Pallas kernels, body(): pl.pallas_call(inner_kernel, out_shape=(jax.ShapeDtypeStruct((4, 6, 16, L...  4.16 us
    pallas_call x1, Pallas kernels, body(): pl.pallas_call(input_kernel, out_shape=jax.ShapeDtypeStruct(local_in.shap...  3.58 us
    all_gather x1, blocking collectives, body(): lax.all_gather(half.reshape(quarters, plane // quarters * share, LAST), '...  2.36 us
  transfers between devices with their start and end apart: 3, of which 1 were waited for; matrix products, arithmetic and copies ran while one was open for 0% of the time, Pallas kernels for 9%

profile of v6, /device:TPU:1, one launch (start us, length us, event | category | flops | bytes accessed | tf_op | source)
XLA Modules:
  0.0 96.3 jit_solution(11068067080163086418)
XLA Ops:
  0.6 1.2 %shard_map.94 = (bf16[36,16,128]{2,1,0:T(8,128)(2,1)S(1)}, bf16[160,16,128]{2,1,0:T(8,128)(2,1)S(1)}, f32[8,128]{1,0:T(8,128)S(1)}) custom-call(s32[1,128]{1,0:T(1,128)} %clip_any.1, s32[1,8]{1,0:T(1,128)} %cols_any.1, s32[1,8]{1,0:T(1,128)} %start_any.1, bf16[6,8,16,256]{3,2,1,0:T(8,128)(2,1)} %bitcast.19, bf16[2,16,32,128]{3,2,1,0:T(8,128)(2,1)} %bitcast.22), custom_call_target="tpu_custom_call" | custom-call | flops 1000000 | bytes 2000000 | tf_op jit(solution)/shard_map/pallas_call | solution.py:551
  1.8 8.8 %collective-permute-start.1 = (bf16[160,16,128]{2,1,0:T(8,128)(2,1)S(1)}, bf16[160,16,128]{2,1,0:T(8,128)(2,1)S(1)}, u32[]{:S(2)}, u32[]{:S(2)}) collective-permute-start(bf16[160,16,128]{2,1,0:T(8,128)(2,1)S(1)} %get-tuple-element.20.tile_ref), channel_id=1, source_target_pairs={{0,4},{4,0},{1,5},{5,1},{2,6},{6,2},{3,7},{7,3},{8,12},{12,8},{9,1... | collective-permute-start | bytes 1966088 | tf_op jit(solution)/shard_map/ppermute | solution.py:568
  10.6 1.9 %collective-permute-start = (bf16[36,16,128]{2,1,0:T(8,128)(2,1)S(1)}, bf16[36,16,128]{2,1,0:T(8,128)(2,1)S(1)}, u32[]{:S(2)}, u32[]{:S(2)}) collective-permute-start(bf16[36,16,128]{2,1,0:T(8,128)(2,1)S(1)} %get-tuple-element.18), channel_id=1, source_target_pairs={{4,8},{12,16},{20,24},{28,32},{36,40},{44,48},{52,56},{60,64},{68,... | collective-permute-start | bytes 442376 | tf_op jit(solution)/shard_map/ppermute | solution.py:567
  12.6 4.2 %shard_map.96 = (bf16[4,6,16,128]{3,2,1,0:T(8,128)(2,1)S(1)}, bf16[4,6,16,128]{3,2,1,0:T(8,128)(2,1)S(1)}, bf16[6,8,16,256]{3,2,1,0:T(8,128)(2,1)S(1)}, bf16[27,...) custom-call(f32[8,128]{1,0:T(8,128)S(1)} %get-tuple-element.19.scales, ...), custom_call_target="tpu_custom_call" | custom-call | flops 2000000000 | bytes 4000000 | tf_op jit(solution)/shard_map/pallas_call | solution.py:570
  16.7 0.0 collective-permute-done.1.sib_ref
  16.7 0.6 shard_map.95
  17.4 0.0 collective-permute-done.rim_ref
  17.4 1.8 %shard_map.97.packet_ref = bf16[76,16,128]{2,1,0:T(8,128)(2,1)S(1)} custom-call(bf16[36,16,128]{2,1,0:T(8,128)(2,1)S(1)} %collective-permute-done.rim_ref, f32[8,128]{1,0:T(8,128)S(1)} %get-tuple-element.21.scales, bf16[160,16,128]{2,1,0:T(8,128)(2,1)S(1)} %get-tuple-element.20.tile_ref, bf16[160,16,128]{2,1,0:T(8,128)(2,1)S(1)} %collective-permute-done.1.sib_ref, ...), custom_call_target="tpu_custom_call" | custom-call | flops 1000000000 | bytes 4000000 | tf_op jit(solution)/shard_map/pallas_call | solution.py:608
  19.1 8.5 %all-gather = bf16[152,16,128]{2,1,0:T(8,128)(2,1)S(1)} all-gather(bf16[76,16,128]{2,1,0:T(8,128)(2,1)S(1)} %shard_map.97.packet_ref), channel_id=2, replica_groups=mesh['yh'=4,'yl'=2,'zh'=4,'zl'=2,'core'=2,'x'=4] {'core'}, dimensions={0}, use_global_device_ids=true | all-gather | bytes 933888 | tf_op jit(solution)/shard_map/all_gather | solution.py:622
  27.7 1.9 %shard_map.98 = bf16[4,4,21,16,128]{4,3,2,1,0:T(8,128)(2,1)S(1)} custom-call(bf16[2,76,16,128]{3,2,1,0:T(8,128)(2,1)S(1)} %bitcast.17, f32[8,128]{1,0:T(8,128)S(1)} %get-tuple-element.21.scales, bf16[160,16,128]{2,1,0:T(8,128)(2,1)S(1)} %get-tuple-element.20.tile_ref, bf16[160,16,128]{2,1,0:T(8,128)(2,1)S(1)} %collective-permute-done.1.sib_ref, ...), custom_call_target="tpu_custom_call" | custom-call | flops 2000000000 | bytes 4000000 | tf_op jit(solution)/shard_map/pallas_call | solution.py:627
  29.6 13.4 %all_to_all.15.parts_ref = bf16[4,4,336,128]{3,2,1,0:T(8,128)(2,1)S(1)} all-to-all(bf16[4,4,336,128]{3,2,1,0:T(8,128)(2,1)S(1)} %bitcast.16), channel_id=1, replica_groups={{0,1,2,3},{8,9,10,11},{16,17,18,19},{24,25,26,27},{32,33,34,35},{40,41,..., dimensions={0} | all-to-all | bytes 2752512 | tf_op jit(solution)/shard_map/all_to_all | solution.py:648
  43.0 0.2 shard_map.99
  43.2 26.8 %all_to_all.16.parts_ref = bf16[64,24,128]{2,1,0:T(8,128)(2,1)S(1)} all-to-all(bf16[64,24,128]{2,1,0:T(8,128)(2,1)S(1)} %bitcast.15), channel_id=1, replica_groups={{0,8,64,72,128,136,192,200,256,264,320,328,384,392,448,456,16,24,80,88,..., dimensions={0} | all-to-all | bytes 786432 | tf_op jit(solution)/shard_map/all_to_all | solution.py:648
  70.0 0.8 shard_map.100
  70.9 5.3 %all-to-all-start.2 = ((bf16[64,24,128]{2,1,0:T(8,128)(2,1)}), bf16[64,24,128]{2,1,0:T(8,128)(2,1)S(1)}, u32[]{:S(2)}, u32[]{:S(2)}) async-start(bf16[64,24,128]{2,1,0:T(8,128)(2,1)} %get-tuple-element.30), calls=%async_computation.2 | async-start | bytes 786432 | tf_op jit(solution)/shard_map/all_to_all | solution.py:685
  76.2 3.6 %shard_map.101.refs_1_ = bf16[6,8,16,256]{3,2,1,0:T(8,128)(2,1)} custom-call(f32[8,128]{1,0:T(8,128)S(1)} %get-tuple-element.29.scales, bf16[6,8,16,256]{3,2,1,0:T(8,128)(2,1)} %bitcast.20, bf16[76,16,128]{2,1,0:T(8,128)(2,1)S(1)} %shard_map.97.packet_ref, bf16[27,256,128]{2,1,0:T(8,128)(2,1)} %bitcast.24), custom_call_target="tpu_custom_call" | custom-call | flops 2000000000 | bytes 4000000 | tf_op jit(solution)/shard_map/pallas_call | solution.py:670
  79.8 12.9 %all-to-all-done.2 = bf16[64,24,128]{2,1,0:T(8,128)(2,1)S(1)} async-done(((bf16[64,24,128]{2,1,0:T(8,128)(2,1)}), bf16[64,24,128]{2,1,0:T(8,128)(2,1)S(1)}, u32[]{:S(2)}, u32[]{:S(2)}) %all-to-all-start.2) | async-done | bytes 393248 | tf_op jit(solution)/shard_map/all_to_all | solution.py:685
  92.8 2.4 %all_gather.11.refs_0_ = bf16[2,4,384,128]{3,2,1,0:T(8,128)(2,1)S(1)} all-gather(bf16[1,4,384,128]{3,2,1,0:T(8,128)(2,1)S(1)} %bitcast.18), channel_id=1, replica_groups=mesh['yh'=4,'yl'=2,'zh'=4,'zl'=2,'core'=2,'x'=4] {'core'}, dimensions={0}, use_global_device_ids=true | all-gather | bytes 1179648 | tf_op jit(solution)/shard_map/all_gather | solution.py:686
  95.1 1.1 %shard_map.102 = (f32[27,32,256]{2,1,0:T(8,128)}, f32[27,32,128]{2,1,0:T(8,128)}) custom-call(bf16[2,4,384,128]{3,2,1,0:T(8,128)(2,1)S(1)} %all_gather.11.refs_0_, bf16[6,8,16,256]{3,2,1,0:T(8,128)(2,1)} %shard_map.101.refs_1_), custom_call_target="tpu_custom_call" | custom-call | tf_op jit(solution)/shard_map/pallas_call | solution.py:690
Async XLA Ops:
  1.8 14.9 %collective-permute-start.1 = (bf16[160,16,128]{2,1,0:T(8,128)(2,1)S(1)}, bf16[160,16,128]{2,1,0:T(8,128)(2,1)S(1)}, u32[]{:S(2)}, u32[]{:S(2)}) collective-permute-start(bf16[160,16,128]{2,1,0:T(8,128)(2,1)S(1)} %get-tuple-element.20.tile_ref), channel_id=1, source_target_pairs={{0,4},{4,0},{1,5},{5,1},{2,6},{6,2},{3,7},{7,3},{8,12},{12,8},{9,1... | collective-permute-start | bytes 1966088 | tf_op jit(solution)/shard_map/ppermute | solution.py:568
  10.6 6.7 %collective-permute-start = (bf16[36,16,128]{2,1,0:T(8,128)(2,1)S(1)}, bf16[36,16,128]{2,1,0:T(8,128)(2,1)S(1)}, u32[]{:S(2)}, u32[]{:S(2)}) collective-permute-start(bf16[36,16,128]{2,1,0:T(8,128)(2,1)S(1)} %get-tuple-element.18), channel_id=1, source_target_pairs={{4,8},{12,16},{20,24},{28,32},{36,40},{44,48},{52,56},{60,64},{68,... | collective-permute-start | bytes 442376 | tf_op jit(solution)/shard_map/ppermute | solution.py:567
  70.9 21.9 %all-to-all-start.2 = ((bf16[64,24,128]{2,1,0:T(8,128)(2,1)}), bf16[64,24,128]{2,1,0:T(8,128)(2,1)S(1)}, u32[]{:S(2)}, u32[]{:S(2)}) async-start(bf16[64,24,128]{2,1,0:T(8,128)(2,1)} %get-tuple-element.30), calls=%async_computation.2 | async-start | bytes 786432 | tf_op jit(solution)/shard_map/all_to_all | solution.py:685

commit v7 on v6

--- a/solution.py
+++ b/solution.py
@@ -207,8 +207,8 @@
 
 
 def inner_kernel(
-    scales, tile_ref, w1_any, w2_any, first_ref, second_ref, act_ref, w1_ref, w2_ref,
-    act, pair, cots, sems,
+    scales, tile_ref, w1_any, w2_any, first_ref, second_ref, act, w1_ref, w2_ref,
+    pair, cots, sems,
 ):
     load_w1 = pltpu.make_async_copy(w1_any, w1_ref, sems.at[0])
     load_w2 = pltpu.make_async_copy(w2_any, w2_ref, sems.at[1])
@@ -220,7 +220,6 @@
         values = eff_frame(lambda f: tile_rows(tile_ref, f), frame, keep)
         values = values * sigmoid(values) * twice(low)
         shifted_act(act, (frame,), values)
-        act_ref[frame] = values.astype(BF)
     load_w1.wait()
     first_out = first_conv(
         lambda kw, kt, kh: act[kw, kt : kt + 4, kh : kh + 6].reshape(384, 256), w1_ref
@@ -242,7 +241,7 @@
 
 
 def edge_kernel(
-    rim_ref, scales, tile_ref, sib_ref, first_ref, second_ref, w1_ref, w2_ref, packet_ref,
+    rim_ref, scales, tile_ref, sib_ref, first_ref, second_ref, own_act, w1_ref, w2_ref, packet_ref,
     act, rows, pair, cots,
 ):
     odd = lax.axis_index("core")
@@ -254,12 +253,12 @@
     for frame in range(6):
         for part, at, read, mask in (
             (odd, odd * 2, lambda f: joined(rim_ref[f * 4 : f * 4 + 4]), wide_low * twice(rim_scale)),
-            (0, 2, lambda f: joined(tile_ref[f * 16 : f * 16 + 4]), wide_low),
-            (1, 0, lambda f: joined(tile_ref[f * 16 + 12 : f * 16 + 16]), wide_low),
             (even, even * 2, lambda f: joined(sib_ref[pl.ds(f * 16 + odd * 12, 4)]), wide_low * twice(sib_scale)),
         ):
             values = eff_frame(lambda f, read=read: read(f).astype(F32), frame, keep)
             shifted_act(act, (frame, part, pl.ds(at, 2)), values * sigmoid(values) * mask)
+    act[:, :, 0, 2:4] = own_act[:, :, 0:2]
+    act[:, :, 1, 0:2] = own_act[:, :, 6:8]
     high = high_mask(scales, COLS)
     for frame in range(2):
         at = TILE_COT + frame * 32
@@ -404,7 +403,7 @@
             [ref[kt : kt + frames].reshape(frames * 128, ref.shape[3]) for ref in refs], 0
         )
 
-    act_all = jnp.concatenate([both((act_ref, sib_act_ref), kt, 4) for kt in range(3)], 1)
+    act_all = jnp.concatenate([both((act_ref.at[1], sib_act_ref), kt, 4) for kt in range(3)], 1)
     seconds = [
         ref[PACK_SECOND:PACK_ROW].reshape(4, 8, 16, LAST) for ref in (packet_ref, sib_packet_ref)
     ]
@@ -572,14 +571,13 @@
         out_shape=(
             jax.ShapeDtypeStruct((4, 6, 16, LAST), BF),
             jax.ShapeDtypeStruct((4, 6, 16, LAST), BF),
-            jax.ShapeDtypeStruct((6, 8, 16, 256), BF),
+            jax.ShapeDtypeStruct((3, 6, 8, 16, 256), BF),
             jax.ShapeDtypeStruct(w1.shape, BF),
             jax.ShapeDtypeStruct(w2.shape, BF),
         ),
         in_specs=[VMEM] * 2 + [HBM] * 2,
         out_specs=(VMEM,) * 5,
         scratch_shapes=[
-            pltpu.VMEM((3, 6, 8, 16, 256), BF),
             pltpu.VMEM((13, 48, LAST), F32),
             pltpu.VMEM((2, 6, 16, 9 * LAST), BF),
             pltpu.SemaphoreType.DMA((2,)),
@@ -608,7 +606,7 @@
     packet = pl.pallas_call(
         edge_kernel,
         out_shape=blocks(PACK_BLOCKS),
-        in_specs=[VMEM] * 8,
+        in_specs=[VMEM] * 9,
         out_specs=VMEM,
         scratch_shapes=[
             pltpu.VMEM((3, 6, 2, 4, 16, 256), BF),
@@ -618,7 +616,7 @@
         ],
         compiler_params=params(16),
         cost_estimate=cost(10**9, 4 * 10**6),
-    )(rim, scales, tile, sibling, inner_first, inner_second, inner_w1, inner_w2)
+    )(rim, scales, tile, sibling, inner_first, inner_second, act, inner_w1, inner_w2)
     packets = lax.all_gather(packet, "core", axis=0)
 
     depth = LAST // reps

time: 96.6 us -> 96.4 us (level)
  no operation moved by 1% of the time
where the time goes in v7:
time: 96.4 us; the launch traced here: 96 us
  blocking collectives  51.1 us (53%)
  starting transfers between devices  16.1 us (17%)
  Pallas kernels  15.2 us (16%)
  waiting for transfers between devices  12.9 us (13%)
    all_to_all x2, blocking collectives, exchange(): lax.all_to_all(values, ALL_AXES, 0, 0, axis_index_groups=groups, tiled=True)  40.2 us
    all_to_all x1, waiting for transfers between devices, body(): half = lax.all_to_all(copies, PLANE_AXES, 0, 0, tiled=True)  12.9 us
    ppermute x1, starting transfers between devices, body(): sibling = lax.ppermute(tile, 'core', swap)  8.79 us
    all_gather x1, blocking collectives, body(): packets = lax.all_gather(packet, 'core', axis=0)  8.54 us
    all_to_all x1, starting transfers between devices, body(): half = lax.all_to_all(copies, PLANE_AXES, 0, 0, tiled=True)  5.39 us
    pallas_call x1, Pallas kernels, body(): pl.pallas_call(inner_kernel, out_shape=(jax.ShapeDtypeStruct((4, 6, 16, L...  4.12 us
    pallas_call x1, Pallas kernels, body(): pl.pallas_call(input_kernel, out_shape=jax.ShapeDtypeStruct(local_in.shap...  3.58 us
    all_gather x1, blocking collectives, body(): lax.all_gather(half.reshape(quarters, plane // quarters * share, LAST), '...  2.36 us
  transfers between devices with their start and end apart: 3, of which 1 were waited for; matrix products, arithmetic and copies ran while one was open for 0% of the time, Pallas kernels for 9%

profile of v7, /device:TPU:1, one launch (start us, length us, event | category | flops | bytes accessed | tf_op | source)
XLA Modules:
  0.0 96.0 jit_solution(18030325847179257798)
XLA Ops:
  0.6 1.2 %shard_map.94 = (bf16[36,16,128]{2,1,0:T(8,128)(2,1)S(1)}, bf16[160,16,128]{2,1,0:T(8,128)(2,1)S(1)}, f32[8,128]{1,0:T(8,128)S(1)}) custom-call(s32[1,128]{1,0:T(1,128)} %clip_any.1, s32[1,8]{1,0:T(1,128)} %cols_any.1, s32[1,8]{1,0:T(1,128)} %start_any.1, bf16[6,8,16,256]{3,2,1,0:T(8,128)(2,1)} %bitcast.19, bf16[2,16,32,128]{3,2,1,0:T(8,128)(2,1)} %bitcast.22), custom_call_target="tpu_custom_call" | custom-call | flops 1000000 | bytes 2000000 | tf_op jit(solution)/shard_map/pallas_call | solution.py:550
  1.8 8.8 %collective-permute-start.1 = (bf16[160,16,128]{2,1,0:T(8,128)(2,1)S(1)}, bf16[160,16,128]{2,1,0:T(8,128)(2,1)S(1)}, u32[]{:S(2)}, u32[]{:S(2)}) collective-permute-start(bf16[160,16,128]{2,1,0:T(8,128)(2,1)S(1)} %get-tuple-element.20.tile_ref), channel_id=1, source_target_pairs={{0,4},{4,0},{1,5},{5,1},{2,6},{6,2},{3,7},{7,3},{8,12},{12,8},{9,1... | collective-permute-start | bytes 1966088 | tf_op jit(solution)/shard_map/ppermute | solution.py:567
  10.6 1.9 %collective-permute-start = (bf16[36,16,128]{2,1,0:T(8,128)(2,1)S(1)}, bf16[36,16,128]{2,1,0:T(8,128)(2,1)S(1)}, u32[]{:S(2)}, u32[]{:S(2)}) collective-permute-start(bf16[36,16,128]{2,1,0:T(8,128)(2,1)S(1)} %get-tuple-element.18), channel_id=1, source_target_pairs={{4,8},{12,16},{20,24},{28,32},{36,40},{44,48},{52,56},{60,64},{68,... | collective-permute-start | bytes 442376 | tf_op jit(solution)/shard_map/ppermute | solution.py:566
  12.6 4.1 %shard_map.96 = (bf16[4,6,16,128]{3,2,1,0:T(8,128)(2,1)S(1)}, bf16[4,6,16,128]{3,2,1,0:T(8,128)(2,1)S(1)}, bf16[3,6,8,16,256]{4,3,2,1,0:T(8,128)(2,1)S(1)}, bf16...) custom-call(f32[8,128]{1,0:T(8,128)S(1)} %get-tuple-element.19.scales, ...), custom_call_target="tpu_custom_call" | custom-call | flops 2000000000 | bytes 4000000 | tf_op jit(solution)/shard_map/pallas_call | solution.py:569
  16.7 0.0 collective-permute-done.1.sib_ref
  16.7 0.6 shard_map.95
  17.3 0.0 collective-permute-done.rim_ref
  17.3 1.6 %shard_map.97.packet_ref = bf16[76,16,128]{2,1,0:T(8,128)(2,1)S(1)} custom-call(bf16[36,16,128]{2,1,0:T(8,128)(2,1)S(1)} %collective-permute-done.rim_ref, f32[8,128]{1,0:T(8,128)S(1)} %get-tuple-element.21.scales, bf16[160,16,128]{2,1,0:T(8,128)(2,1)S(1)} %get-tuple-element.20.tile_ref, bf16[160,16,128]{2,1,0:T(8,128)(2,1)S(1)} %collective-permute-done.1.sib_ref, ...), custom_call_target="tpu_custom_call" | custom-call | flops 1000000000 | bytes 4000000 | tf_op jit(solution)/shard_map/pallas_call | solution.py:606
  18.9 8.5 %all-gather = bf16[152,16,128]{2,1,0:T(8,128)(2,1)S(1)} all-gather(bf16[76,16,128]{2,1,0:T(8,128)(2,1)S(1)} %shard_map.97.packet_ref), channel_id=2, replica_groups=mesh['yh'=4,'yl'=2,'zh'=4,'zl'=2,'core'=2,'x'=4] {'core'}, dimensions={0}, use_global_device_ids=true | all-gather | bytes 933888 | tf_op jit(solution)/shard_map/all_gather | solution.py:620
  27.5 1.9 %shard_map.98 = bf16[4,4,21,16,128]{4,3,2,1,0:T(8,128)(2,1)S(1)} custom-call(bf16[2,76,16,128]{3,2,1,0:T(8,128)(2,1)S(1)} %bitcast.17, f32[8,128]{1,0:T(8,128)S(1)} %get-tuple-element.21.scales, bf16[160,16,128]{2,1,0:T(8,128)(2,1)S(1)} %get-tuple-element.20.tile_ref, bf16[160,16,128]{2,1,0:T(8,128)(2,1)S(1)} %collective-permute-done.1.sib_ref, ...), custom_call_target="tpu_custom_call" | custom-call | flops 2000000000 | bytes 4000000 | tf_op jit(solution)/shard_map/pallas_call | solution.py:625
  29.4 13.4 %all_to_all.15.parts_ref = bf16[4,4,336,128]{3,2,1,0:T(8,128)(2,1)S(1)} all-to-all(bf16[4,4,336,128]{3,2,1,0:T(8,128)(2,1)S(1)} %bitcast.16), channel_id=1, replica_groups={{0,1,2,3},{8,9,10,11},{16,17,18,19},{24,25,26,27},{32,33,34,35},{40,41,..., dimensions={0} | all-to-all | bytes 2752512 | tf_op jit(solution)/shard_map/all_to_all | solution.py:646
  42.8 0.2 shard_map.99
  43.0 26.8 %all_to_all.16.parts_ref = bf16[64,24,128]{2,1,0:T(8,128)(2,1)S(1)} all-to-all(bf16[64,24,128]{2,1,0:T(8,128)(2,1)S(1)} %bitcast.15), channel_id=1, replica_groups={{0,8,64,72,128,136,192,200,256,264,320,328,384,392,448,456,16,24,80,88,..., dimensions={0} | all-to-all | bytes 786432 | tf_op jit(solution)/shard_map/all_to_all | solution.py:646
  69.8 0.8 shard_map.100
  70.6 5.4 %all-to-all-start.2 = ((bf16[64,24,128]{2,1,0:T(8,128)(2,1)}), bf16[64,24,128]{2,1,0:T(8,128)(2,1)S(1)}, u32[]{:S(2)}, u32[]{:S(2)}) async-start(bf16[64,24,128]{2,1,0:T(8,128)(2,1)} %get-tuple-element.30), calls=%async_computation.2 | async-start | bytes 786432 | tf_op jit(solution)/shard_map/all_to_all | solution.py:683
  76.0 3.6 %shard_map.101.refs_1_ = bf16[6,8,16,256]{3,2,1,0:T(8,128)(2,1)} custom-call(f32[8,128]{1,0:T(8,128)S(1)} %get-tuple-element.29.scales, bf16[6,8,16,256]{3,2,1,0:T(8,128)(2,1)} %bitcast.20, bf16[76,16,128]{2,1,0:T(8,128)(2,1)S(1)} %shard_map.97.packet_ref, bf16[27,256,128]{2,1,0:T(8,128)(2,1)} %bitcast.24), custom_call_target="tpu_custom_call" | custom-call | flops 2000000000 | bytes 4000000 | tf_op jit(solution)/shard_map/pallas_call | solution.py:668
  79.6 12.9 %all-to-all-done.2 = bf16[64,24,128]{2,1,0:T(8,128)(2,1)S(1)} async-done(((bf16[64,24,128]{2,1,0:T(8,128)(2,1)}), bf16[64,24,128]{2,1,0:T(8,128)(2,1)S(1)}, u32[]{:S(2)}, u32[]{:S(2)}) %all-to-all-start.2) | async-done | bytes 393248 | tf_op jit(solution)/shard_map/all_to_all | solution.py:683
  92.5 2.4 %all_gather.11.refs_0_ = bf16[2,4,384,128]{3,2,1,0:T(8,128)(2,1)S(1)} all-gather(bf16[1,4,384,128]{3,2,1,0:T(8,128)(2,1)S(1)} %bitcast.18), channel_id=1, replica_groups=mesh['yh'=4,'yl'=2,'zh'=4,'zl'=2,'core'=2,'x'=4] {'core'}, dimensions={0}, use_global_device_ids=true | all-gather | bytes 1179648 | tf_op jit(solution)/shard_map/all_gather | solution.py:684
  94.9 1.1 %shard_map.102 = (f32[27,32,256]{2,1,0:T(8,128)}, f32[27,32,128]{2,1,0:T(8,128)}) custom-call(bf16[2,4,384,128]{3,2,1,0:T(8,128)(2,1)S(1)} %all_gather.11.refs_0_, bf16[6,8,16,256]{3,2,1,0:T(8,128)(2,1)} %shard_map.101.refs_1_), custom_call_target="tpu_custom_call" | custom-call | tf_op jit(solution)/shard_map/pallas_call | solution.py:688
Async XLA Ops:
  1.8 14.9 %collective-permute-start.1 = (bf16[160,16,128]{2,1,0:T(8,128)(2,1)S(1)}, bf16[160,16,128]{2,1,0:T(8,128)(2,1)S(1)}, u32[]{:S(2)}, u32[]{:S(2)}) collective-permute-start(bf16[160,16,128]{2,1,0:T(8,128)(2,1)S(1)} %get-tuple-element.20.tile_ref), channel_id=1, source_target_pairs={{0,4},{4,0},{1,5},{5,1},{2,6},{6,2},{3,7},{7,3},{8,12},{12,8},{9,1... | collective-permute-start | bytes 1966088 | tf_op jit(solution)/shard_map/ppermute | solution.py:567
  10.6 6.7 %collective-permute-start = (bf16[36,16,128]{2,1,0:T(8,128)(2,1)S(1)}, bf16[36,16,128]{2,1,0:T(8,128)(2,1)S(1)}, u32[]{:S(2)}, u32[]{:S(2)}) collective-permute-start(bf16[36,16,128]{2,1,0:T(8,128)(2,1)S(1)} %get-tuple-element.18), channel_id=1, source_target_pairs={{4,8},{12,16},{20,24},{28,32},{36,40},{44,48},{52,56},{60,64},{68,... | collective-permute-start | bytes 442376 | tf_op jit(solution)/shard_map/ppermute | solution.py:566
  70.6 21.9 %all-to-all-start.2 = ((bf16[64,24,128]{2,1,0:T(8,128)(2,1)}), bf16[64,24,128]{2,1,0:T(8,128)(2,1)S(1)}, u32[]{:S(2)}, u32[]{:S(2)}) async-start(bf16[64,24,128]{2,1,0:T(8,128)(2,1)} %get-tuple-element.30), calls=%async_computation.2 | async-start | bytes 786432 | tf_op jit(solution)/shard_map/all_to_all | solution.py:683

commit v8 on v7

--- a/solution.py
+++ b/solution.py
@@ -369,13 +369,12 @@
 
 
 def weight_kernel(
-    packets_ref, scales, tile_ref, sib_ref, act_ref, sib_act_ref, sums_ref,
-    part_ref, pair, sums, cols,
+    packets_ref, scales, tile_ref, sib_ref, act_ref, sib_act_ref, _,
+    part_ref, sums, pair, cols,
 ):
     odd = lax.axis_index("core")
     packet_ref, sib_packet_ref = packets_ref.at[odd], packets_ref.at[1 - odd]
     reps, quarters, per_quarter, depth = part_ref.shape[:4]
-    sums[...] = sums_ref[...]
     for slot, tile, packet, which in (
         (0, tile_ref, packet_ref, COLS),
         (1, sib_ref, sib_packet_ref, SIB_COLS),
@@ -622,16 +621,17 @@
     depth = LAST // reps
     quarters = near_y * near_z
     per_quarter = 2 * GRAD_BLOCKS // quarters
-    parts = pl.pallas_call(
+    parts, _ = pl.pallas_call(
         weight_kernel,
-        out_shape=jax.ShapeDtypeStruct(
-            (reps, quarters, per_quarter, depth // 2, LAST), BF
+        out_shape=(
+            jax.ShapeDtypeStruct((reps, quarters, per_quarter, depth // 2, LAST), BF),
+            jax.ShapeDtypeStruct(sums.shape, BF),
         ),
         in_specs=[VMEM] * 7,
-        out_specs=VMEM,
+        out_specs=(VMEM, VMEM),
+        input_output_aliases={6: 1},
         scratch_shapes=[
             pltpu.VMEM((1, 48, LAST), F32),
-            pltpu.VMEM((3, 2, 2, 17, 16, LAST), BF),
             pltpu.VMEM((3, 2, 4, 10, 16, LAST), BF),
         ],
         compiler_params=params(24),

time: 96.4 us -> 96.4 us (level)
  no operation moved by 1% of the time
where the time goes in v8:
time: 96.4 us; the launch traced here: 96 us
  blocking collectives  51.1 us (53%)
  starting transfers between devices  16.1 us (17%)
  Pallas kernels  15.2 us (16%)
  waiting for transfers between devices  12.9 us (13%)
    all_to_all x2, blocking collectives, exchange(): lax.all_to_all(values, ALL_AXES, 0, 0, axis_index_groups=groups, tiled=True)  40.2 us
    all_to_all x1, waiting for transfers between devices, body(): half = lax.all_to_all(copies, PLANE_AXES, 0, 0, tiled=True)  12.9 us
    ppermute x1, starting transfers between devices, body(): sibling = lax.ppermute(tile, 'core', swap)  8.79 us
    all_gather x1, blocking collectives, body(): packets = lax.all_gather(packet, 'core', axis=0)  8.54 us
    all_to_all x1, starting transfers between devices, body(): half = lax.all_to_all(copies, PLANE_AXES, 0, 0, tiled=True)  5.4 us
    pallas_call x1, Pallas kernels, body(): pl.pallas_call(inner_kernel, out_shape=(jax.ShapeDtypeStruct((4, 6, 16, L...  4.12 us
    pallas_call x1, Pallas kernels, body(): pl.pallas_call(input_kernel, out_shape=jax.ShapeDtypeStruct(local_in.shap...  3.58 us
    all_gather x1, blocking collectives, body(): lax.all_gather(half.reshape(quarters, plane // quarters * share, LAST), '...  2.36 us
  transfers between devices with their start and end apart: 3, of which 1 were waited for; matrix products, arithmetic and copies ran while one was open for 0% of the time, Pallas kernels for 9%

profile of v8, /device:TPU:1, one launch (start us, length us, event | category | flops | bytes accessed | tf_op | source)
XLA Modules:
  0.0 96.0 jit_solution(15974884364963943401)
XLA Ops:
  0.6 1.2 %shard_map.94 = (bf16[36,16,128]{2,1,0:T(8,128)(2,1)S(1)}, bf16[160,16,128]{2,1,0:T(8,128)(2,1)S(1)}, f32[8,128]{1,0:T(8,128)S(1)}) custom-call(s32[1,128]{1,0:T(1,128)} %clip_any.1, s32[1,8]{1,0:T(1,128)} %cols_any.1, s32[1,8]{1,0:T(1,128)} %start_any.1, bf16[6,8,16,256]{3,2,1,0:T(8,128)(2,1)} %bitcast.19, bf16[2,16,32,128]{3,2,1,0:T(8,128)(2,1)} %bitcast.22), custom_call_target="tpu_custom_call" | custom-call | flops 1000000 | bytes 2000000 | tf_op jit(solution)/shard_map/pallas_call | solution.py:549
  1.8 8.8 %collective-permute-start.1 = (bf16[160,16,128]{2,1,0:T(8,128)(2,1)S(1)}, bf16[160,16,128]{2,1,0:T(8,128)(2,1)S(1)}, u32[]{:S(2)}, u32[]{:S(2)}) collective-permute-start(bf16[160,16,128]{2,1,0:T(8,128)(2,1)S(1)} %get-tuple-element.21.tile_ref), channel_id=1, source_target_pairs={{0,4},{4,0},{1,5},{5,1},{2,6},{6,2},{3,7},{7,3},{8,12},{12,8},{9,1... | collective-permute-start | bytes 1966088 | tf_op jit(solution)/shard_map/ppermute | solution.py:566
  10.6 1.9 %collective-permute-start = (bf16[36,16,128]{2,1,0:T(8,128)(2,1)S(1)}, bf16[36,16,128]{2,1,0:T(8,128)(2,1)S(1)}, u32[]{:S(2)}, u32[]{:S(2)}) collective-permute-start(bf16[36,16,128]{2,1,0:T(8,128)(2,1)S(1)} %get-tuple-element.19), channel_id=1, source_target_pairs={{4,8},{12,16},{20,24},{28,32},{36,40},{44,48},{52,56},{60,64},{68,... | collective-permute-start | bytes 442376 | tf_op jit(solution)/shard_map/ppermute | solution.py:565
  12.6 4.1 %shard_map.96 = (bf16[4,6,16,128]{3,2,1,0:T(8,128)(2,1)S(1)}, bf16[4,6,16,128]{3,2,1,0:T(8,128)(2,1)S(1)}, bf16[3,6,8,16,256]{4,3,2,1,0:T(8,128)(2,1)S(1)}, bf16...) custom-call(f32[8,128]{1,0:T(8,128)S(1)} %get-tuple-element.20.scales, ...), custom_call_target="tpu_custom_call" | custom-call | flops 2000000000 | bytes 4000000 | tf_op jit(solution)/shard_map/pallas_call | solution.py:568
  16.7 0.0 collective-permute-done.1.sib_ref
  16.7 0.6 shard_map.95
  17.3 0.0 collective-permute-done.rim_ref
  17.3 1.6 %shard_map.97.packet_ref = bf16[76,16,128]{2,1,0:T(8,128)(2,1)S(1)} custom-call(bf16[36,16,128]{2,1,0:T(8,128)(2,1)S(1)} %collective-permute-done.rim_ref, f32[8,128]{1,0:T(8,128)S(1)} %get-tuple-element.22.scales, bf16[160,16,128]{2,1,0:T(8,128)(2,1)S(1)} %get-tuple-element.21.tile_ref, bf16[160,16,128]{2,1,0:T(8,128)(2,1)S(1)} %collective-permute-done.1.sib_ref, ...), custom_call_target="tpu_custom_call" | custom-call | flops 1000000000 | bytes 4000000 | tf_op jit(solution)/shard_map/pallas_call | solution.py:605
  18.9 8.5 %all-gather = bf16[152,16,128]{2,1,0:T(8,128)(2,1)S(1)} all-gather(bf16[76,16,128]{2,1,0:T(8,128)(2,1)S(1)} %shard_map.97.packet_ref), channel_id=2, replica_groups=mesh['yh'=4,'yl'=2,'zh'=4,'zl'=2,'core'=2,'x'=4] {'core'}, dimensions={0}, use_global_device_ids=true | all-gather | bytes 933888 | tf_op jit(solution)/shard_map/all_gather | solution.py:619
  27.5 1.9 %shard_map.98 = (bf16[4,4,21,16,128]{4,3,2,1,0:T(8,128)(2,1)S(1)}, bf16[3,2,2,17,16,128]{5,4,3,2,1,0:T(8,128)(2,1)S(1)}) custom-call(bf16[2,76,16,128]{3,2,1,0:T(8,128)(2,1)S(1)} %bitcast.17, f32[8,128]{1,0:T(8,128)S(1)} %get-tuple-element.22.scales, bf16[160,16,128]{2,1,0:T(8,128)(2,1)S(1)} %get-tuple-element.21.tile_ref, ...), custom_call_target="tpu_custom_call", output_to_operand_aliasing={{1}: (6, {})} | custom-call | flops 2000000000 | bytes 4000000 | tf_op jit(solution)/shard_map/pallas_call | solution.py:624
  29.4 13.4 %all_to_all.15.parts_ref = bf16[4,4,336,128]{3,2,1,0:T(8,128)(2,1)S(1)} all-to-all(bf16[4,4,336,128]{3,2,1,0:T(8,128)(2,1)S(1)} %bitcast.16), channel_id=1, replica_groups={{0,1,2,3},{8,9,10,11},{16,17,18,19},{24,25,26,27},{32,33,34,35},{40,41,..., dimensions={0} | all-to-all | bytes 2752512 | tf_op jit(solution)/shard_map/all_to_all | solution.py:646
  42.8 0.2 shard_map.99
  43.0 26.8 %all_to_all.16.parts_ref = bf16[64,24,128]{2,1,0:T(8,128)(2,1)S(1)} all-to-all(bf16[64,24,128]{2,1,0:T(8,128)(2,1)S(1)} %bitcast.15), channel_id=1, replica_groups={{0,8,64,72,128,136,192,200,256,264,320,328,384,392,448,456,16,24,80,88,..., dimensions={0} | all-to-all | bytes 786432 | tf_op jit(solution)/shard_map/all_to_all | solution.py:646
  69.7 0.8 shard_map.100
  70.6 5.4 %all-to-all-start.2 = ((bf16[64,24,128]{2,1,0:T(8,128)(2,1)}), bf16[64,24,128]{2,1,0:T(8,128)(2,1)S(1)}, u32[]{:S(2)}, u32[]{:S(2)}) async-start(bf16[64,24,128]{2,1,0:T(8,128)(2,1)} %get-tuple-element.32), calls=%async_computation.2 | async-start | bytes 786432 | tf_op jit(solution)/shard_map/all_to_all | solution.py:683
  76.0 3.6 %shard_map.101.refs_1_ = bf16[6,8,16,256]{3,2,1,0:T(8,128)(2,1)} custom-call(f32[8,128]{1,0:T(8,128)S(1)} %get-tuple-element.31.scales, bf16[6,8,16,256]{3,2,1,0:T(8,128)(2,1)} %bitcast.20, bf16[76,16,128]{2,1,0:T(8,128)(2,1)S(1)} %shard_map.97.packet_ref, bf16[27,256,128]{2,1,0:T(8,128)(2,1)} %bitcast.24), custom_call_target="tpu_custom_call" | custom-call | flops 2000000000 | bytes 4000000 | tf_op jit(solution)/shard_map/pallas_call | solution.py:668
  79.6 12.9 %all-to-all-done.2 = bf16[64,24,128]{2,1,0:T(8,128)(2,1)S(1)} async-done(((bf16[64,24,128]{2,1,0:T(8,128)(2,1)}), bf16[64,24,128]{2,1,0:T(8,128)(2,1)S(1)}, u32[]{:S(2)}, u32[]{:S(2)}) %all-to-all-start.2) | async-done | bytes 393248 | tf_op jit(solution)/shard_map/all_to_all | solution.py:683
  92.5 2.4 %all_gather.11.refs_0_ = bf16[2,4,384,128]{3,2,1,0:T(8,128)(2,1)S(1)} all-gather(bf16[1,4,384,128]{3,2,1,0:T(8,128)(2,1)S(1)} %bitcast.18), channel_id=1, replica_groups=mesh['yh'=4,'yl'=2,'zh'=4,'zl'=2,'core'=2,'x'=4] {'core'}, dimensions={0}, use_global_device_ids=true | all-gather | bytes 1179648 | tf_op jit(solution)/shard_map/all_gather | solution.py:684
  94.8 1.1 %shard_map.102 = (f32[27,32,256]{2,1,0:T(8,128)}, f32[27,32,128]{2,1,0:T(8,128)}) custom-call(bf16[2,4,384,128]{3,2,1,0:T(8,128)(2,1)S(1)} %all_gather.11.refs_0_, bf16[6,8,16,256]{3,2,1,0:T(8,128)(2,1)} %shard_map.101.refs_1_), custom_call_target="tpu_custom_call" | custom-call | tf_op jit(solution)/shard_map/pallas_call | solution.py:688
Async XLA Ops:
  1.8 14.9 %collective-permute-start.1 = (bf16[160,16,128]{2,1,0:T(8,128)(2,1)S(1)}, bf16[160,16,128]{2,1,0:T(8,128)(2,1)S(1)}, u32[]{:S(2)}, u32[]{:S(2)}) collective-permute-start(bf16[160,16,128]{2,1,0:T(8,128)(2,1)S(1)} %get-tuple-element.21.tile_ref), channel_id=1, source_target_pairs={{0,4},{4,0},{1,5},{5,1},{2,6},{6,2},{3,7},{7,3},{8,12},{12,8},{9,1... | collective-permute-start | bytes 1966088 | tf_op jit(solution)/shard_map/ppermute | solution.py:566
  10.6 6.7 %collective-permute-start = (bf16[36,16,128]{2,1,0:T(8,128)(2,1)S(1)}, bf16[36,16,128]{2,1,0:T(8,128)(2,1)S(1)}, u32[]{:S(2)}, u32[]{:S(2)}) collective-permute-start(bf16[36,16,128]{2,1,0:T(8,128)(2,1)S(1)} %get-tuple-element.19), channel_id=1, source_target_pairs={{4,8},{12,16},{20,24},{28,32},{36,40},{44,48},{52,56},{60,64},{68,... | collective-permute-start | bytes 442376 | tf_op jit(solution)/shard_map/ppermute | solution.py:565
  70.6 21.9 %all-to-all-start.2 = ((bf16[64,24,128]{2,1,0:T(8,128)(2,1)}), bf16[64,24,128]{2,1,0:T(8,128)(2,1)S(1)}, u32[]{:S(2)}, u32[]{:S(2)}) async-start(bf16[64,24,128]{2,1,0:T(8,128)(2,1)} %get-tuple-element.32), calls=%async_computation.2 | async-start | bytes 786432 | tf_op jit(solution)/shard_map/all_to_all | solution.py:683

commit v9 on v8

--- a/solution.py
+++ b/solution.py
@@ -115,7 +115,7 @@
             )
         )
     ]
-    for copy in copies:
+    for copy in copies[3:] + copies[:3]:
         copy.start()
     copies[3].wait()
     for frame in range(6):

time: 96.4 us -> 96.3 us (level)
  no operation moved by 1% of the time
where the time goes in v9:
time: 96.3 us; the launch traced here: 95.9 us
  blocking collectives  51.1 us (53%)
  starting transfers between devices  16.1 us (17%)
  Pallas kernels  15.1 us (16%)
  waiting for transfers between devices  12.9 us (13%)
    all_to_all x2, blocking collectives, exchange(): lax.all_to_all(values, ALL_AXES, 0, 0, axis_index_groups=groups, tiled=True)  40.2 us
    all_to_all x1, waiting for transfers between devices, body(): half = lax.all_to_all(copies, PLANE_AXES, 0, 0, tiled=True)  12.9 us
    ppermute x1, starting transfers between devices, body(): sibling = lax.ppermute(tile, 'core', swap)  8.79 us
    all_gather x1, blocking collectives, body(): packets = lax.all_gather(packet, 'core', axis=0)  8.55 us
    all_to_all x1, starting transfers between devices, body(): half = lax.all_to_all(copies, PLANE_AXES, 0, 0, tiled=True)  5.39 us
    pallas_call x1, Pallas kernels, body(): pl.pallas_call(inner_kernel, out_shape=(jax.ShapeDtypeStruct((4, 6, 16, L...  4.12 us
    pallas_call x1, Pallas kernels, body(): pl.pallas_call(input_kernel, out_shape=jax.ShapeDtypeStruct(local_in.shap...  3.58 us
    all_gather x1, blocking collectives, body(): lax.all_gather(half.reshape(quarters, plane // quarters * share, LAST), '...  2.36 us
  transfers between devices with their start and end apart: 3, of which 1 were waited for; matrix products, arithmetic and copies ran while one was open for 0% of the time, Pallas kernels for 9%

profile of v9, /device:TPU:1, one launch (start us, length us, event | category | flops | bytes accessed | tf_op | source)
XLA Modules:
  0.0 95.9 jit_solution(11509312309655976619)
XLA Ops:
  0.6 1.2 %shard_map.94 = (bf16[36,16,128]{2,1,0:T(8,128)(2,1)S(1)}, bf16[160,16,128]{2,1,0:T(8,128)(2,1)S(1)}, f32[8,128]{1,0:T(8,128)S(1)}) custom-call(s32[1,128]{1,0:T(1,128)} %clip_any.1, s32[1,8]{1,0:T(1,128)} %cols_any.1, s32[1,8]{1,0:T(1,128)} %start_any.1, bf16[6,8,16,256]{3,2,1,0:T(8,128)(2,1)} %bitcast.19, bf16[2,16,32,128]{3,2,1,0:T(8,128)(2,1)} %bitcast.22), custom_call_target="tpu_custom_call" | custom-call | flops 1000000 | bytes 2000000 | tf_op jit(solution)/shard_map/pallas_call | solution.py:549
  1.8 8.8 %collective-permute-start.1 = (bf16[160,16,128]{2,1,0:T(8,128)(2,1)S(1)}, bf16[160,16,128]{2,1,0:T(8,128)(2,1)S(1)}, u32[]{:S(2)}, u32[]{:S(2)}) collective-permute-start(bf16[160,16,128]{2,1,0:T(8,128)(2,1)S(1)} %get-tuple-element.21.tile_ref), channel_id=1, source_target_pairs={{0,4},{4,0},{1,5},{5,1},{2,6},{6,2},{3,7},{7,3},{8,12},{12,8},{9,1... | collective-permute-start | bytes 1966088 | tf_op jit(solution)/shard_map/ppermute | solution.py:566
  10.6 1.9 %collective-permute-start = (bf16[36,16,128]{2,1,0:T(8,128)(2,1)S(1)}, bf16[36,16,128]{2,1,0:T(8,128)(2,1)S(1)}, u32[]{:S(2)}, u32[]{:S(2)}) collective-permute-start(bf16[36,16,128]{2,1,0:T(8,128)(2,1)S(1)} %get-tuple-element.19), channel_id=1, source_target_pairs={{4,8},{12,16},{20,24},{28,32},{36,40},{44,48},{52,56},{60,64},{68,... | collective-permute-start | bytes 442376 | tf_op jit(solution)/shard_map/ppermute | solution.py:565
  12.6 4.1 %shard_map.96 = (bf16[4,6,16,128]{3,2,1,0:T(8,128)(2,1)S(1)}, bf16[4,6,16,128]{3,2,1,0:T(8,128)(2,1)S(1)}, bf16[3,6,8,16,256]{4,3,2,1,0:T(8,128)(2,1)S(1)}, bf16...) custom-call(f32[8,128]{1,0:T(8,128)S(1)} %get-tuple-element.20.scales, ...), custom_call_target="tpu_custom_call" | custom-call | flops 2000000000 | bytes 4000000 | tf_op jit(solution)/shard_map/pallas_call | solution.py:568
  16.7 0.0 collective-permute-done.1.sib_ref
  16.7 0.6 shard_map.95
  17.3 0.0 collective-permute-done.rim_ref
  17.3 1.6 %shard_map.97.packet_ref = bf16[76,16,128]{2,1,0:T(8,128)(2,1)S(1)} custom-call(bf16[36,16,128]{2,1,0:T(8,128)(2,1)S(1)} %collective-permute-done.rim_ref, f32[8,128]{1,0:T(8,128)S(1)} %get-tuple-element.22.scales, bf16[160,16,128]{2,1,0:T(8,128)(2,1)S(1)} %get-tuple-element.21.tile_ref, bf16[160,16,128]{2,1,0:T(8,128)(2,1)S(1)} %collective-permute-done.1.sib_ref, ...), custom_call_target="tpu_custom_call" | custom-call | flops 1000000000 | bytes 4000000 | tf_op jit(solution)/shard_map/pallas_call | solution.py:605
  18.9 8.5 %all-gather = bf16[152,16,128]{2,1,0:T(8,128)(2,1)S(1)} all-gather(bf16[76,16,128]{2,1,0:T(8,128)(2,1)S(1)} %shard_map.97.packet_ref), channel_id=2, replica_groups=mesh['yh'=4,'yl'=2,'zh'=4,'zl'=2,'core'=2,'x'=4] {'core'}, dimensions={0}, use_global_device_ids=true | all-gather | bytes 933888 | tf_op jit(solution)/shard_map/all_gather | solution.py:619
  27.5 1.9 %shard_map.98 = (bf16[4,4,21,16,128]{4,3,2,1,0:T(8,128)(2,1)S(1)}, bf16[3,2,2,17,16,128]{5,4,3,2,1,0:T(8,128)(2,1)S(1)}) custom-call(bf16[2,76,16,128]{3,2,1,0:T(8,128)(2,1)S(1)} %bitcast.17, f32[8,128]{1,0:T(8,128)S(1)} %get-tuple-element.22.scales, bf16[160,16,128]{2,1,0:T(8,128)(2,1)S(1)} %get-tuple-element.21.tile_ref, ...), custom_call_target="tpu_custom_call", output_to_operand_aliasing={{1}: (6, {})} | custom-call | flops 2000000000 | bytes 4000000 | tf_op jit(solution)/shard_map/pallas_call | solution.py:624
  29.4 13.4 %all_to_all.15.parts_ref = bf16[4,4,336,128]{3,2,1,0:T(8,128)(2,1)S(1)} all-to-all(bf16[4,4,336,128]{3,2,1,0:T(8,128)(2,1)S(1)} %bitcast.16), channel_id=1, replica_groups={{0,1,2,3},{8,9,10,11},{16,17,18,19},{24,25,26,27},{32,33,34,35},{40,41,..., dimensions={0} | all-to-all | bytes 2752512 | tf_op jit(solution)/shard_map/all_to_all | solution.py:646
  42.8 0.2 shard_map.99
  43.0 26.8 %all_to_all.16.parts_ref = bf16[64,24,128]{2,1,0:T(8,128)(2,1)S(1)} all-to-all(bf16[64,24,128]{2,1,0:T(8,128)(2,1)S(1)} %bitcast.15), channel_id=1, replica_groups={{0,8,64,72,128,136,192,200,256,264,320,328,384,392,448,456,16,24,80,88,..., dimensions={0} | all-to-all | bytes 786432 | tf_op jit(solution)/shard_map/all_to_all | solution.py:646
  69.7 0.8 shard_map.100
  70.6 5.4 %all-to-all-start.2 = ((bf16[64,24,128]{2,1,0:T(8,128)(2,1)}), bf16[64,24,128]{2,1,0:T(8,128)(2,1)S(1)}, u32[]{:S(2)}, u32[]{:S(2)}) async-start(bf16[64,24,128]{2,1,0:T(8,128)(2,1)} %get-tuple-element.32), calls=%async_computation.2 | async-start | bytes 786432 | tf_op jit(solution)/shard_map/all_to_all | solution.py:683
  76.0 3.6 %shard_map.101.refs_1_ = bf16[6,8,16,256]{3,2,1,0:T(8,128)(2,1)} custom-call(f32[8,128]{1,0:T(8,128)S(1)} %get-tuple-element.31.scales, bf16[6,8,16,256]{3,2,1,0:T(8,128)(2,1)} %bitcast.20, bf16[76,16,128]{2,1,0:T(8,128)(2,1)S(1)} %shard_map.97.packet_ref, bf16[27,256,128]{2,1,0:T(8,128)(2,1)} %bitcast.24), custom_call_target="tpu_custom_call" | custom-call | flops 2000000000 | bytes 4000000 | tf_op jit(solution)/shard_map/pallas_call | solution.py:668
  79.6 12.9 %all-to-all-done.2 = bf16[64,24,128]{2,1,0:T(8,128)(2,1)S(1)} async-done(((bf16[64,24,128]{2,1,0:T(8,128)(2,1)}), bf16[64,24,128]{2,1,0:T(8,128)(2,1)S(1)}, u32[]{:S(2)}, u32[]{:S(2)}) %all-to-all-start.2) | async-done | bytes 393248 | tf_op jit(solution)/shard_map/all_to_all | solution.py:683
  92.5 2.4 %all_gather.11.refs_0_ = bf16[2,4,384,128]{3,2,1,0:T(8,128)(2,1)S(1)} all-gather(bf16[1,4,384,128]{3,2,1,0:T(8,128)(2,1)S(1)} %bitcast.18), channel_id=1, replica_groups=mesh['yh'=4,'yl'=2,'zh'=4,'zl'=2,'core'=2,'x'=4] {'core'}, dimensions={0}, use_global_device_ids=true | all-gather | bytes 1179648 | tf_op jit(solution)/shard_map/all_gather | solution.py:684
  94.8 1.1 %shard_map.102 = (f32[27,32,256]{2,1,0:T(8,128)}, f32[27,32,128]{2,1,0:T(8,128)}) custom-call(bf16[2,4,384,128]{3,2,1,0:T(8,128)(2,1)S(1)} %all_gather.11.refs_0_, bf16[6,8,16,256]{3,2,1,0:T(8,128)(2,1)} %shard_map.101.refs_1_), custom_call_target="tpu_custom_call" | custom-call | tf_op jit(solution)/shard_map/pallas_call | solution.py:688
Async XLA Ops:
  1.8 14.9 %collective-permute-start.1 = (bf16[160,16,128]{2,1,0:T(8,128)(2,1)S(1)}, bf16[160,16,128]{2,1,0:T(8,128)(2,1)S(1)}, u32[]{:S(2)}, u32[]{:S(2)}) collective-permute-start(bf16[160,16,128]{2,1,0:T(8,128)(2,1)S(1)} %get-tuple-element.21.tile_ref), channel_id=1, source_target_pairs={{0,4},{4,0},{1,5},{5,1},{2,6},{6,2},{3,7},{7,3},{8,12},{12,8},{9,1... | collective-permute-start | bytes 1966088 | tf_op jit(solution)/shard_map/ppermute | solution.py:566
  10.6 6.7 %collective-permute-start = (bf16[36,16,128]{2,1,0:T(8,128)(2,1)S(1)}, bf16[36,16,128]{2,1,0:T(8,128)(2,1)S(1)}, u32[]{:S(2)}, u32[]{:S(2)}) collective-permute-start(bf16[36,16,128]{2,1,0:T(8,128)(2,1)S(1)} %get-tuple-element.19), channel_id=1, source_target_pairs={{4,8},{12,16},{20,24},{28,32},{36,40},{44,48},{52,56},{60,64},{68,... | collective-permute-start | bytes 442376 | tf_op jit(solution)/shard_map/ppermute | solution.py:565
  70.6 21.9 %all-to-all-start.2 = ((bf16[64,24,128]{2,1,0:T(8,128)(2,1)}), bf16[64,24,128]{2,1,0:T(8,128)(2,1)S(1)}, u32[]{:S(2)}, u32[]{:S(2)}) async-start(bf16[64,24,128]{2,1,0:T(8,128)(2,1)} %get-tuple-element.32), calls=%async_computation.2 | async-start | bytes 786432 | tf_op jit(solution)/shard_map/all_to_all | solution.py:683
